TPU v7x, 32 devices: a whole 2x2x4 slice. The times are simulated.
32 devices in a mesh: grp: 8 (over z, y), blk: 4 (over x, core).
Axes of the slice: x: 2, y: 2, z: 4, core: 2. Of those that a mesh axis runs over, the one named last changes fastest.
Arguments:
- source: bfloat16 [32768, 256], P(('grp', 'blk')), may hold values from -6 to 6
- send_ids: int32 [32, 8], P(('grp', 'blk')), may hold values from 0 to 15
- send_counts: int32 [32, 4], P(('grp', 'blk')), may hold values from 1 to 2, as said below
- tile_slot: int32 [32, 128], P(('grp', 'blk')), may hold values from 0 to 7, as said below
- tile_target: int32 [32, 128], P(('grp', 'blk')), may hold values from 0 to 63, as said below
- tile_weights: bfloat16 [4096, 4096], P(('grp', 'blk')), may hold values from 0 to 0.0625
Outputs:
- remapped: float32 [65536, 256], P(('grp', 'blk'))
Inputs may be any that keep to these rules, and one draw needn't show every extreme that they name: `send_counts`: every reader of every partition is sent at least one block, and each partition sends 2 blocks to some reader. `tile_slot`: each of the 4 * 2 receive slots is read by at least one tile of every partition. `tile_target`: each of the 64 partial target blocks is written by at least one tile of every partition.
All inputs are finite; a program needn't handle non-finite values.
Results may differ from a plain program's by a relative error of at most 0.0003.
Values may be sent and summed in bfloat16 or wider, within the bound.
No kernel may reach another device: no remote copies, remote signals or barrier semaphores. Data moves between devices by JAX's collectives and lax.ppermute only.
A program may use at most 64 MiB of HBM per device.

v0:
```python
import jax
import jax.numpy as jnp
from jax import lax
from jax.sharding import PartitionSpec as P

COLS = 256
BLOCK = 64
TB = 32
EB = 16


def passed_along(shard, axis, by):
    count = lax.axis_size(axis)
    return lax.ppermute(shard, axis, [(i, (i + by) % count) for i in range(count)])


def body(source, send_ids, send_counts, tile_slot, tile_target, tile_weights):
    group_size = lax.axis_size("blk")
    own_index = lax.axis_index("blk")
    capacity = send_ids.shape[1] // group_size
    source_blocks = source.reshape(-1, BLOCK, COLS)
    slot_rank = jnp.arange(group_size * capacity, dtype=jnp.int32) % capacity
    all_ids, all_counts = (
        lax.all_gather(send_ids, "blk", axis=0, tiled=True),
        lax.all_gather(send_counts, "blk", axis=0, tiled=True),
    )
    block_ids = lax.dynamic_slice_in_dim(all_ids, own_index * capacity, capacity, 1)
    live_counts = lax.dynamic_slice_in_dim(all_counts, own_index, 1, 1)
    live_mask = (slot_rank.reshape(group_size, capacity) < live_counts).reshape(-1)
    sender_rank = jnp.arange(group_size * capacity, dtype=jnp.int32) // capacity
    global_ids = sender_rank * source_blocks.shape[0] + block_ids.reshape(-1)
    empty_slots = jnp.zeros((group_size * capacity, BLOCK, COLS), jnp.bfloat16)
    shard_blocks = lax.all_gather(source, "blk", axis=0, tiled=True).reshape(-1, BLOCK, COLS)
    count_here = shard_blocks.shape[0]
    wanted = (global_ids >= 0) & (global_ids < count_here) & live_mask
    picked = jnp.take(shard_blocks, jnp.clip(global_ids, 0, count_here - 1), axis=0)
    received = jnp.where(wanted[:, None, None], picked, empty_slots)
    tile_slots = tile_slot[0]
    tile_targets = tile_target[0]
    count_tiles = tile_slots.shape[0]
    weights = tile_weights.reshape(count_tiles, BLOCK, BLOCK)
    operands = jnp.take(received, tile_slots, axis=0)
    products = jnp.einsum("kij,kjc->kic", weights, operands, preferred_element_type=jnp.float32)
    segments = TB + 2 * EB
    onehot_table = (tile_targets[None, :] == jnp.arange(segments, dtype=jnp.int32)[:, None]).astype(
        jnp.float32
    )
    pieces = jnp.dot(
        onehot_table, products.reshape(count_tiles, BLOCK * COLS), precision=lax.Precision.HIGHEST
    )
    pieces = pieces.reshape(segments, BLOCK, COLS)
    lower_edge = pieces[:EB]
    middle = pieces[EB : EB + TB]
    upper_edge = pieces[EB + TB :]
    from_next = passed_along(lower_edge, ("grp", "blk"), -1)
    from_prior = passed_along(upper_edge, ("grp", "blk"), 1)
    assembled = jnp.concatenate(
        [middle[:EB] + from_prior, middle[EB : TB - EB], middle[TB - EB :] + from_next], axis=0
    )
    return assembled.reshape(TB * BLOCK, COLS)


def solution(mesh):
    return jax.shard_map(
        body,
        mesh=mesh,
        in_specs=(
            P(("grp", "blk"), None),
            P(("grp", "blk"), None),
            P(("grp", "blk"), None),
            P(("grp", "blk"), None),
            P(("grp", "blk"), None),
            P(("grp", "blk"), None),
        ),
        out_specs=P(("grp", "blk"), None),
        check_vma=False,
    )
```

profile of v0, /device:TPU:5, one launch (start us, length us, event | category | flops | bytes accessed | tf_op | source)
XLA Modules:
  0.0 87.5 jit_solution(10644610136237245104)
XLA Ops:
  6.5 0.7 all-gather.4.cloned.1.call-update
  7.3 5.6 %all-gather.1 = s32[4,1,4]{2,1,0:T(1,128)S(1)} all-gather(s32[1,1,4]{2,1,0:T(1,128)} %bitcast.42), channel_id=1, replica_groups=mesh['grp'=8,'blk'=4] {'blk'}, dimensions={0}, use_global_device_ids=true | all-gather | bytes 80 | tf_op jit(solution)/shard_map/all_gather | solution.py:25
  12.9 5.2 %all-gather = s32[4,1,8]{2,1,0:T(1,128)S(1)} all-gather(s32[1,1,8]{2,1,0:T(1,128)} %bitcast.43), channel_id=1, replica_groups=mesh['grp'=8,'blk'=4] {'blk'}, dimensions={0}, use_global_device_ids=true | all-gather | bytes 160 | tf_op jit(solution)/shard_map/all_gather | solution.py:24
  18.1 0.5 broadcast.248
  18.6 0.7 fusion.15
  19.3 0.1 reshape.164
  19.4 0.1 reshape.166
  19.5 0.2 dynamic-slice_reduce_fusion
  19.7 0.1 lt.79
  19.8 0.1 lt.80
  19.9 1.6 %copy.9 = bf16[128,4096]{0,1:T(8,128)(2,1)S(1)} copy(bf16[128,4096]{1,0:T(8,128)(2,1)} %param.11) | data formatting | bytes 2097152 | tf_op args[5]
  21.5 3.0 %copy.10 = bf16[128,64,64]{2,1,0:T(8,128)(2,1)S(1)} copy(bf16[128,64,64]{0,2,1:T(8,128)(2,1)S(1)} %bitcast.32) | data formatting | bytes 2097152 | tf_op jit(solution)/shard_map/reshape | solution.py:41
  24.6 8.5 %all-gather.4.cloned.1.call-done = bf16[4096,256]{1,0:T(8,128)(2,1)} async-done(((bf16[1024,256]{1,0:T(8,128)(2,1)}), bf16[4096,256]{1,0:T(8,128)(2,1)}) %all-gather.4.cloned.1.call-update) | async-done | bytes 2097168 | tf_op jit(solution)/shard_map/all_gather | solution.py:33
  33.1 2.2 %gather_fusion = bf16[8,64,256]{2,1,0:T(8,128)(2,1)S(1)} fusion(bf16[64,64,256]{2,1,0:T(8,128)(2,1)} %bitcast.39, s32[1024]{0:T(1024)S(1)} %pad_clamp_fusion.1), kind=kCustom, calls=%fused_computation | custom fusion | bytes 524320 | tf_op jit(solution)/shard_map/jit(_take)/gather | solution.py:36
  35.3 0.1 select_select_fusion
  35.4 2.8 %gather_fusion.1 = bf16[128,64,256]{2,1,0:T(8,128)(2,1)} fusion(bf16[8,64,256]{2,1,0:T(8,128)(2,1)S(1)} %select_select_fusion, s32[1024]{0:T(1024)S(1)} %pad_clamp_fusion), kind=kCustom, calls=%fused_computation.1 | custom fusion | bytes 8389120 | tf_op jit(solution)/shard_map/jit(_take)/gather | solution.py:42
  38.2 3.5 %fusion = f32[128,256,64]{1,2,0:T(8,128)S(1)} fusion(bf16[128,64,64]{2,1,0:T(8,128)(2,1)S(1)} %copy.10, bf16[128,64,256]{2,1,0:T(8,128)(2,1)} %gather_fusion.1, pred[128]{0:T(512)(128)(4,1)S(1)} %compare_and_fusion.2), kind=kOutput, calls=%fused_computation.2 | convolution fusion | flops 270532608 | bytes 13631616 | tf_op jit(solution)/shard_map/kij,kjc->kic/dot_general | solution.py:43
  41.7 0.0 copy-start
  41.7 6.6 %copy.11 = f32[16,8,64,256]{3,1,2,0:T(8,128)S(1)} copy(f32[16,8,64,256]{3,2,1,0:T(8,128)S(1)} %bitcast.30) | data formatting | bytes 16777216
  48.3 3.8 %fusion.4 = f32[64,16384]{1,0:T(8,128)S(1)} fusion(f32[128,16384]{1,0:T(8,128)S(1)} %bitcast.31, s32[128]{0:T(128)S(1)} %bitcast.41), kind=kOutput, calls=%fused_computation.11 | convolution fusion | flops 1610620928 | bytes 12583424 | tf_op jit(solution)/shard_map/dot_general | solution.py:48
  52.1 0.3 fusion.16
  52.4 0.3 copy.13
  52.7 0.5 collective-permute-start
  53.2 0.3 copy.15
  53.5 0.1 collective-permute-start.1
  53.6 0.3 copy.12
  53.9 0.3 copy.14
  54.3 18.8 %collective-permute-done = f32[16,64,256]{2,1,0:T(8,128)S(1)} collective-permute-done((f32[16,64,256]{2,1,0:T(8,128)S(1)}, f32[16,64,256]{2,1,0:T(8,128)S(1)}, u32[]{:S(2)}, u32[]{:S(2)}) %collective-permute-start) | collective-permute-done | bytes 1048608 | tf_op jit(solution)/shard_map/ppermute | solution.py:14
  73.1 0.1 bitcast_add_fusion.1
  73.2 5.8 %collective-permute-done.1 = f32[16,64,256]{2,1,0:T(8,128)S(1)} collective-permute-done((f32[16,64,256]{2,1,0:T(8,128)S(1)}, f32[16,64,256]{2,1,0:T(8,128)S(1)}, u32[]{:S(2)}, u32[]{:S(2)}) %collective-permute-start.1) | collective-permute-done | bytes 1048608 | tf_op jit(solution)/shard_map/ppermute | solution.py:14
  79.0 0.1 bitcast_add_fusion
  79.2 1.5 %pad_maximum_fusion = f32[32,64,256]{2,1,0:T(8,128)} fusion(f32[16,64,256]{2,1,0:T(8,128)S(1)} %bitcast_add_fusion, f32[16,64,256]{2,1,0:T(8,128)S(1)} %bitcast_add_fusion.1), kind=kLoop, calls=%fused_computation.5 | loop fusion | flops 524288 | bytes 4194304 | tf_op jit(solution)/shard_map/concatenate | solution.py:57
  (11 shorter events, 0.1 us)
Async XLA Ops:
  6.5 18.0 %copy-start.1 = (s32[1,128]{1,0:T(1,128)S(1)}, s32[1,128]{1,0:T(1,128)}, u32[]{:S(2)}) copy-start(s32[1,128]{1,0:T(1,128)} %param.9) | copy-start | bytes 1540
  6.5 26.6 %all-gather.4.cloned.1.call-start = ((), (), s32[]{:S(2)}) async-start(), calls=%async_computation | async-start | bytes 2621440 | tf_op jit(solution)/shard_map/all_gather | solution.py:33
  41.7 6.6 %copy-start = (s32[1,128]{1,0:T(1,128)S(1)}, s32[1,128]{1,0:T(1,128)}, u32[]{:S(2)}) copy-start(s32[1,128]{1,0:T(1,128)} %param.10) | copy-start | bytes 1540
  52.7 20.4 %collective-permute-start = (f32[16,64,256]{2,1,0:T(8,128)S(1)}, f32[16,64,256]{2,1,0:T(8,128)S(1)}, u32[]{:S(2)}, u32[]{:S(2)}) collective-permute-start(f32[16,64,256]{2,1,0:T(8,128)S(1)} %bitcast.38), channel_id=1, source_target_pairs={{0,1},{1,2},{2,3},{3,4},{4,5},{5,6},{6,7},{7,8},{8,9},{9,10},{10,1... | collective-permute-start | bytes 3145736 | tf_op jit(solution)/shard_map/ppermute | solution.py:14
  53.5 25.5 %collective-permute-start.1 = (f32[16,64,256]{2,1,0:T(8,128)S(1)}, f32[16,64,256]{2,1,0:T(8,128)S(1)}, u32[]{:S(2)}, u32[]{:S(2)}) collective-permute-start(f32[16,64,256]{2,1,0:T(8,128)S(1)} %bitcast.37), channel_id=1, source_target_pairs={{0,31},{1,0},{2,1},{3,2},{4,3},{5,4},{6,5},{7,6},{8,7},{9,8},{10,9... | collective-permute-start | bytes 3145736 | tf_op jit(solution)/shard_map/ppermute | solution.py:14
Sparse Core Ops, SparseCore 0:
  8.9 24.1 all-gather.3
where the time goes:
time: 88.3 us; the launch traced here: 87.5 us
  waiting for transfers between devices  33.8 us (38%)
  local copies, waits for them, and re-layouts  19.5 us (22%)
  between operations  13.6 us (15%)
  blocking collectives  10.8 us (12%)
  matrix products  7.28 us (8%)
  other arithmetic  1.95 us (2%)
    ppermute x2, waiting for transfers between devices, passed_along(): lax.ppermute(shard, axis, [(i, (i + by) % count) for i in range(count)])  24.6 us
    unnamed x10, local copies, waits for them, and re-layouts  9.49 us
    all_gather x1, waiting for transfers between devices, body(): lax.all_gather(source, 'blk', axis=0, tiled=True).reshape(-1, BLOCK, COLS)  8.53 us
    all_gather x1, blocking collectives, body(): lax.all_gather(send_counts, 'blk', axis=0, tiled=True)  5.65 us
    all_gather x1, blocking collectives, body(): lax.all_gather(send_ids, 'blk', axis=0, tiled=True)  5.16 us
    dot_general x1, matrix products, body(): jnp.dot(onehot_table, products.reshape(count_tiles, BLOCK * COLS), precis...  3.79 us
    dot_general x1, matrix products, body(): jnp.einsum('kij,kjc->kic', weights, operands, preferred_element_type=jnp....  3.5 us
    reshape x1, local copies, waits for them, and re-layouts, body(): weights = tile_weights.reshape(count_tiles, BLOCK, BLOCK)  2.99 us
  transfers between devices with their start and end apart: 3, of which 3 were waited for; matrix products, arithmetic and copies ran while one was open for 9% of the time, Pallas kernels for 0%

commit v1 on v0

v1 whole, which is shorter than its diff:
```python
import functools

import jax
import jax.numpy as jnp
from jax import lax
from jax.experimental import pallas as pl
from jax.experimental.pallas import tpu as pltpu
from jax.sharding import PartitionSpec as P

COLS = 256
BLOCK = 64
EB = 16
CHUNK = 2 * BLOCK
ROWS = EB * BLOCK
GROUP = 64
GROUPS = ROWS // GROUP
FLOOR = 2.0**-110
VMEM = pl.BlockSpec(memory_space=pltpu.VMEM)
SMEM = pl.BlockSpec(memory_space=pltpu.SMEM)
ANY = pl.BlockSpec(memory_space=pl.ANY)


def params():
    return pltpu.CompilerParams(vmem_limit_bytes=40 * 1024 * 1024)


def cost(flops, nbytes):
    return pl.CostEstimate(flops=flops, bytes_accessed=nbytes, transcendentals=0)


def pick_kernel(members, capacity, ids, counts, source, *refs):
    outs, sems = refs[:members], refs[members]
    own = lax.axis_index("blk")
    copies = []
    for k in range(members):
        reader = lax.rem(own + k, members)
        for j in range(capacity):
            start = pl.multiple_of(ids[0, reader * capacity + j] * BLOCK, BLOCK)
            copy = pltpu.make_async_copy(
                source.at[pl.ds(start, BLOCK)],
                outs[k].at[pl.ds(j * BLOCK, BLOCK)],
                sems.at[k * capacity + j],
            )
            copy.start()
            copies.append(copy)
    for copy in copies:
        copy.wait()
    for k in range(members):
        reader = lax.rem(own + k, members)
        for j in range(capacity):

            @pl.when(j >= counts[0, reader])
            def _():
                outs[k][pl.ds(j * BLOCK, BLOCK)] = jnp.zeros((BLOCK, COLS), jnp.bfloat16)


def pick(members, capacity, send_ids, send_counts, source):
    shape = (capacity * BLOCK, COLS)
    return pl.pallas_call(
        functools.partial(pick_kernel, members, capacity),
        out_shape=[pltpu.VMEM(shape, jnp.bfloat16)] * members,
        in_specs=[SMEM, SMEM, ANY],
        out_specs=[VMEM] * members,
        scratch_shapes=[pltpu.SemaphoreType.DMA((members * capacity,))],
        compiler_params=params(),
        name="pick",
    )(send_ids, send_counts, source)


def spread_kernel(members, capacity, quarters, slots, targets, weights, *outs):
    own = lax.axis_index("blk")
    tiles = weights.shape[0]
    width = members * CHUNK
    count = len(quarters)
    slot = slots[...]
    sender = slot // capacity
    shift = lax.rem(own - sender + members, members)
    place = shift * capacity + slot % capacity
    target = targets[...]
    rows = lax.broadcasted_iota(jnp.int32, (count * EB, tiles), 0)
    wanted = rows
    for n, q in enumerate(quarters):
        wanted = jnp.where(rows // EB == n, rows % EB + q * EB, wanted)
    hit = target == wanted
    table = jnp.concatenate(
        [
            jnp.concatenate(
                [(hit & (place == k * capacity + j)).astype(jnp.float32) for j in range(capacity)], axis=1
            )
            for k in range(members)
        ],
        axis=0,
    ).astype(jnp.bfloat16)
    left = (lax.broadcasted_iota(jnp.int32, (1, CHUNK), 1) < BLOCK).astype(jnp.float32)
    low = left.astype(jnp.bfloat16)
    high = (1.0 - left).astype(jnp.bfloat16)

    def step(c, _):
        x = weights[:, pl.ds(pl.multiple_of(c * CHUNK, CHUNK), CHUNK)]
        swapped = jnp.concatenate([x[:, BLOCK:], x[:, :BLOCK]], axis=1)
        right = jnp.concatenate(
            [
                jnp.concatenate([x * low, swapped * low], axis=1),
                jnp.concatenate([swapped * high, x * high], axis=1),
            ],
            axis=0,
        )
        sums = jnp.dot(table, right, preferred_element_type=jnp.float32)
        coarse = sums.astype(jnp.bfloat16)
        fine = (sums - coarse.astype(jnp.float32)).astype(jnp.bfloat16)
        for k in range(members):
            for n in range(count):
                top = (k * count + n) * EB
                for h in range(2):
                    row = pl.ds(pl.multiple_of((2 * c + h) * EB, EB), EB)
                    part = (slice(top, top + EB), slice(h * CHUNK, (h + 1) * CHUNK))
                    outs[n][row, k * CHUNK : (k + 1) * CHUNK] = coarse[part]
                    outs[n][row, width + k * CHUNK : width + (k + 1) * CHUNK] = fine[part]
        return 0

    lax.fori_loop(0, BLOCK // 2, step, 0, unroll=2)


def spread(members, capacity, quarters, slots, targets, weights):
    shape = (ROWS, 2 * members * CHUNK)
    tiles = weights.shape[0]
    return pl.pallas_call(
        functools.partial(spread_kernel, members, capacity, quarters),
        out_shape=[pltpu.VMEM(shape, jnp.bfloat16)] * len(quarters),
        in_specs=[VMEM] * 3,
        out_specs=[VMEM] * len(quarters),
        compiler_params=params(),
        cost_estimate=cost(2 * members * EB * len(quarters) * 2 * tiles * 8192, 6 * 2**20),
        name="spread",
    )(slots, targets, weights)


def stack(blocks, both):
    rows = blocks[0].shape[0]
    for half in range(2):
        for k, block in enumerate(blocks):
            start = (half * len(blocks) + k) * rows
            both[start : start + rows] = block[...]


def edge_kernel(members, left, *refs):
    blocks, message, both, powers = refs[:members], refs[members], refs[members + 1], refs[members + 2]
    stack(blocks, both)
    step = 4 * GROUP
    for start in range(0, ROWS, step):
        piece = jnp.dot(left[start : start + step], both[...], preferred_element_type=jnp.float32)
        for g in range(step // GROUP):
            rows = piece[g * GROUP : (g + 1) * GROUP]
            most = jnp.maximum(jnp.max(jnp.abs(rows), axis=0, keepdims=True), FLOOR)
            power = jnp.floor(jnp.log2(most) + 0.001) + 1.0
            whole = jnp.round(rows * jnp.exp2(15.0 - power)).astype(jnp.int32)
            message[start + g * GROUP : start + (g + 1) * GROUP] = whole.astype(jnp.int16)
            at = start // GROUP + g
            powers[at : at + 1] = power.astype(jnp.int32)
    message[ROWS : ROWS + GROUPS] = powers[...].astype(jnp.int16)


def edge(members, left, blocks):
    return pl.pallas_call(
        functools.partial(edge_kernel, members),
        out_shape=pltpu.VMEM((ROWS + GROUPS, COLS), jnp.int16),
        in_specs=[VMEM] * (1 + members),
        out_specs=VMEM,
        scratch_shapes=[
            pltpu.VMEM((left.shape[1], COLS), jnp.bfloat16),
            pltpu.VMEM((GROUPS, COLS), jnp.int32),
        ],
        compiler_params=params(),
        cost_estimate=cost(2 * ROWS * left.shape[1] * COLS, 2 * 2**20),
        name="edge",
    )(left, *blocks)


def middle_kernel(members, first, second, *refs):
    blocks, outs, both = refs[:members], refs[members : members + 2], refs[members + 2]
    stack(blocks, both)
    step = 256
    for left, out in zip((first, second), outs):
        for start in range(0, ROWS, step):
            out[start : start + step] = jnp.dot(
                left[start : start + step], both[...], preferred_element_type=jnp.float32
            )


def middle(members, first, second, blocks):
    return pl.pallas_call(
        functools.partial(middle_kernel, members),
        out_shape=[pltpu.VMEM((ROWS, COLS), jnp.float32)] * 2,
        in_specs=[VMEM] * (2 + members),
        out_specs=[VMEM] * 2,
        scratch_shapes=[pltpu.VMEM((first.shape[1], COLS), jnp.bfloat16)],
        compiler_params=params(),
        cost_estimate=cost(4 * ROWS * first.shape[1] * COLS, 4 * 2**20),
        name="middle",
    )(first, second, *blocks)


def finish_kernel(half, own, message, *refs):
    out, rows, sems = refs[-3:]
    scale = jnp.exp2(message[ROWS : ROWS + GROUPS].astype(jnp.float32) - 15.0)
    for i in range(BLOCK):
        at = i * EB
        g = at // GROUP
        value = own[at : at + EB] + message[at : at + EB].astype(jnp.float32) * scale[g : g + 1]
        for n in range(COLS // 128):
            rows[n, pl.ds(i, EB, stride=BLOCK)] = value[:, n * 128 : (n + 1) * 128]
    copies = []
    for n in range(COLS // 128):
        there = out.at[pl.ds(half * ROWS, ROWS), pl.ds(n * 128, 128)]
        copies.append(pltpu.make_async_copy(rows.at[n], there, sems.at[n]))
        copies[n].start()
    for copy in copies:
        copy.wait()


def finish(half, own, message, out=None):
    given = [] if out is None else [out]
    return pl.pallas_call(
        functools.partial(finish_kernel, half),
        out_shape=jax.ShapeDtypeStruct((2 * ROWS, COLS), jnp.float32),
        in_specs=[VMEM] * 2 + [ANY] * len(given),
        out_specs=ANY,
        scratch_shapes=[
            pltpu.VMEM((COLS // 128, ROWS, 128), jnp.float32),
            pltpu.SemaphoreType.DMA((COLS // 128,)),
        ],
        input_output_aliases={} if out is None else {2: 0},
        compiler_params=params(),
        cost_estimate=cost(3 * ROWS * COLS, 2 * 2**20),
        name="finish",
    )(own, message, *given)


def passed_along(shard, axis, by):
    count = lax.axis_size(axis)
    return lax.ppermute(shard, axis, [(i, (i + by) % count) for i in range(count)])


def body(source, send_ids, send_counts, tile_slot, tile_target, tile_weights):
    members = lax.axis_size("blk")
    capacity = send_ids.shape[1] // members
    picked = pick(members, capacity, send_ids, send_counts, source)
    blocks = [picked[0]] + [passed_along(picked[k], "blk", k) for k in range(1, members)]
    tiles = (tile_slot, tile_target, tile_weights)
    lower, upper = spread(members, capacity, (0, 3), *tiles)
    first, second = spread(members, capacity, (1, 2), *tiles)
    from_prior = passed_along(edge(members, upper, blocks), ("grp", "blk"), 1)
    from_next = passed_along(edge(members, lower, blocks), ("grp", "blk"), -1)
    own_first, own_second = middle(members, first, second, blocks)
    out = finish(0, own_first, from_prior)
    return finish(1, own_second, from_next, out)


def solution(mesh):
    spec = P(("grp", "blk"), None)
    return jax.shard_map(body, mesh=mesh, in_specs=(spec,) * 6, out_specs=spec, check_vma=False)
```

time: 88.3 us -> 33.5 us (0.38)
  the two profiles are of different devices: /device:TPU:5 before, /device:TPU:4 now
where the time goes in v1:
time: 33.5 us; the launch traced here: 33.2 us
  Pallas kernels  16.9 us (50%)
  starting transfers between devices  5.75 us (17%)
  waiting for transfers between devices  5.53 us (17%)
  local copies, waits for them, and re-layouts  4.9 us (15%)
    pallas_call x2, Pallas kernels, spread(): pl.pallas_call(functools.partial(spread_kernel, members, capacity, quarte...  8.96 us
    ppermute x5, starting transfers between devices, passed_along(): lax.ppermute(shard, axis, [(i, (i + by) % count) for i in range(count)])  5.75 us
    ppermute x5, waiting for transfers between devices, passed_along(): lax.ppermute(shard, axis, [(i, (i + by) % count) for i in range(count)])  5.53 us
    unnamed x16, local copies, waits for them, and re-layouts  4.9 us
    pallas_call x2, Pallas kernels, finish(): pl.pallas_call(functools.partial(finish_kernel, half), out_shape=jax.Shap...  3.99 us
    pallas_call x2, Pallas kernels, edge(): pl.pallas_call(functools.partial(edge_kernel, members), out_shape=pltpu.V...  1.65 us
    pallas_call x1, Pallas kernels, middle(): pl.pallas_call(functools.partial(middle_kernel, members), out_shape=[pltp...  1.26 us
    pallas_call x1, Pallas kernels, pick(): pl.pallas_call(functools.partial(pick_kernel, members, capacity), out_sha...  1.07 us
  transfers between devices with their start and end apart: 5, of which 1 were waited for; matrix products, arithmetic and copies ran while one was open for 0% of the time, Pallas kernels for 39%

profile of v1, /device:TPU:4, one launch (start us, length us, event | category | flops | bytes accessed | tf_op | source)
XLA Modules:
  0.0 33.2 jit_solution(16525090547806035254)
XLA Ops:
  0.0 0.0 copy-start
  0.0 1.0 %copy-done = bf16[1024,256]{1,0:T(8,128)(2,1)S(1)} copy-done((bf16[1024,256]{1,0:T(8,128)(2,1)S(1)}, bf16[1024,256]{1,0:T(8,128)(2,1)}, u32[]{:S(2)}) %copy-start) | copy-done | bytes 524312
  1.0 0.0 copy-start.1
  1.0 0.7 %copy-done.1 = s32[1,8]{1,0:T(1,128)S(1)} copy-done((s32[1,8]{1,0:T(1,128)S(1)}, s32[1,8]{1,0:T(1,128)}, u32[]{:S(2)}) %copy-start.1) | copy-done | bytes 56
  1.7 0.0 copy-start.2
  1.7 0.7 %copy-done.2 = s32[1,4]{1,0:T(1,128)S(1)} copy-done((s32[1,4]{1,0:T(1,128)S(1)}, s32[1,4]{1,0:T(1,128)}, u32[]{:S(2)}) %copy-start.2) | copy-done | bytes 40
  2.4 1.1 %pick.1 = (bf16[128,256]{1,0:T(8,128)(2,1)S(1)}, bf16[128,256]{1,0:T(8,128)(2,1)S(1)}, bf16[128,256]{1,0:T(8,128)(2,1)S(1)}, bf16[128,256]{1,0:T(8,128)(2,1)S(1)}) custom-call(s32[1,8]{1,0:T(1,128)S(1)} %copy-done.1, s32[1,4]{1,0:T(1,128)S(1)} %copy-done.2, bf16[1024,256]{1,0:T(8,128)(2,1)S(1)} %copy-done), custom_call_target="tpu_custom_call" | custom-call | tf_op jit(solution)/shard_map/pick/pallas_call | solution.py:59
  3.4 0.1 collective-permute-start
  3.5 1.6 %collective-permute-start.1 = (bf16[128,256]{1,0:T(8,128)(2,1)S(1)}, bf16[128,256]{1,0:T(8,128)(2,1)S(1)}, u32[]{:S(2)}, u32[]{:S(2)}) collective-permute-start(bf16[128,256]{1,0:T(8,128)(2,1)S(1)} %get-tuple-element.19), channel_id=1, source_target_pairs={{0,2},{1,3},{2,0},{3,1},{4,6},{5,7},{6,4},{7,5},{8,10},{9,11},{10,... | collective-permute-start | bytes 196616 | tf_op jit(solution)/shard_map/ppermute | solution.py:241
  5.1 1.4 %collective-permute-start.2 = (bf16[128,256]{1,0:T(8,128)(2,1)S(1)}, bf16[128,256]{1,0:T(8,128)(2,1)S(1)}, u32[]{:S(2)}, u32[]{:S(2)}) collective-permute-start(bf16[128,256]{1,0:T(8,128)(2,1)S(1)} %get-tuple-element.20), channel_id=1, source_target_pairs={{0,3},{1,0},{2,1},{3,2},{4,7},{5,4},{6,5},{7,6},{8,11},{9,8},{10,9... | collective-permute-start | bytes 196616 | tf_op jit(solution)/shard_map/ppermute | solution.py:241
  6.4 0.0 copy-start.3
  6.4 1.2 %copy-done.3 = bf16[128,4096]{1,0:T(8,128)(2,1)S(1)} copy-done((bf16[128,4096]{1,0:T(8,128)(2,1)S(1)}, bf16[128,4096]{1,0:T(8,128)(2,1)}, u32[]{:S(2)}) %copy-start.3) | copy-done | bytes 1048600
  7.7 0.7 %copy-done.5 = s32[1,128]{1,0:T(1,128)S(1)} copy-done((s32[1,128]{1,0:T(1,128)S(1)}, s32[1,128]{1,0:T(1,128)}, u32[]{:S(2)}) %copy-start.5) | copy-done | bytes 536
  8.3 0.7 %copy-done.6 = s32[1,128]{1,0:T(1,128)S(1)} copy-done((s32[1,128]{1,0:T(1,128)S(1)}, s32[1,128]{1,0:T(1,128)}, u32[]{:S(2)}) %copy-start.6) | copy-done | bytes 536
  9.0 4.5 %spread.3 = (bf16[1024,1024]{1,0:T(8,128)(2,1)S(1)}, bf16[1024,1024]{1,0:T(8,128)(2,1)S(1)}) custom-call(s32[1,128]{1,0:T(1,128)S(1)} %copy-done.5, s32[1,128]{1,0:T(1,128)S(1)} %copy-done.6, bf16[128,4096]{1,0:T(8,128)(2,1)S(1)} %copy-done.3), custom_call_target="tpu_custom_call" | custom-call | flops 536870912 | bytes 6291456 | tf_op jit(solution)/shard_map/spread/pallas_call | solution.py:127
  13.5 0.0 collective-permute-done.refs_1_
  13.5 0.0 collective-permute-done.1.refs_2_
  13.5 0.0 collective-permute-done.2.refs_3_
  13.5 0.8 %edge.3 = s16[1040,256]{1,0:T(8,128)(2,1)S(1)} custom-call(bf16[1024,1024]{1,0:T(8,128)(2,1)S(1)} %get-tuple-element.24.left, bf16[128,256]{1,0:T(8,128)(2,1)S(1)} %get-tuple-element.17.refs_0_, bf16[128,256]{1,0:T(8,128)(2,1)S(1)} %collective-permute-done.refs_1_, bf16[128,256]{1,0:T(8,128)(2,1)S(1)} %collective-permute-done.1.refs_2_, ...), custom_call_target="tpu_custom_call" | custom-call | flops 536870912 | bytes 2097152 | tf_op jit(solution)/shard_map/edge/pallas_call | solution.py:164
  14.3 0.0 copy-start.4
  14.3 0.0 copy-start.7
  14.4 0.1 collective-permute-start.4
  14.4 0.8 %edge.2 = s16[1040,256]{1,0:T(8,128)(2,1)S(1)} custom-call(bf16[1024,1024]{1,0:T(8,128)(2,1)S(1)} %get-tuple-element.22.left, bf16[128,256]{1,0:T(8,128)(2,1)S(1)} %get-tuple-element.17.refs_0_, bf16[128,256]{1,0:T(8,128)(2,1)S(1)} %collective-permute-done.refs_1_, bf16[128,256]{1,0:T(8,128)(2,1)S(1)} %collective-permute-done.1.refs_2_, ...), custom_call_target="tpu_custom_call" | custom-call | flops 536870912 | bytes 2097152 | tf_op jit(solution)/shard_map/edge/pallas_call | solution.py:164
  15.2 2.7 %collective-permute-start.3 = (s16[1040,256]{1,0:T(8,128)(2,1)S(1)}, s16[1040,256]{1,0:T(8,128)(2,1)S(1)}, u32[]{:S(2)}, u32[]{:S(2)}) collective-permute-start(s16[1040,256]{1,0:T(8,128)(2,1)S(1)} %edge.2), channel_id=1, source_target_pairs={{0,31},{1,0},{2,1},{3,2},{4,3},{5,4},{6,5},{7,6},{8,7},{9,8},{10,9... | collective-permute-start | bytes 1597448 | tf_op jit(solution)/shard_map/ppermute | solution.py:241
  17.9 0.0 copy-done.4
  17.9 0.0 copy-done.7
  17.9 4.5 %spread.2 = (bf16[1024,1024]{1,0:T(8,128)(2,1)S(1)}, bf16[1024,1024]{1,0:T(8,128)(2,1)S(1)}) custom-call(s32[1,128]{1,0:T(1,128)S(1)} %copy-done.5, s32[1,128]{1,0:T(1,128)S(1)} %copy-done.7, bf16[128,4096]{1,0:T(8,128)(2,1)S(1)} %copy-done.4), custom_call_target="tpu_custom_call" | custom-call | flops 536870912 | bytes 6291456 | tf_op jit(solution)/shard_map/spread/pallas_call | solution.py:127
  22.4 1.3 %middle.1 = (f32[1024,256]{1,0:T(8,128)S(1)}, f32[1024,256]{1,0:T(8,128)S(1)}) custom-call(bf16[1024,1024]{1,0:T(8,128)(2,1)S(1)} %get-tuple-element.15.first, bf16[1024,1024]{1,0:T(8,128)(2,1)S(1)} %get-tuple-element.16.second, bf16[128,256]{1,0:T(8,128)(2,1)S(1)} %get-tuple-element.17.refs_0_, bf16[128,256]{1,0:T(8,128)(2,1)S(1)} %collective-permute-done.refs_1_, ...), custom_call_target="tpu_custom_call" | custom-call | flops 1073741824 | bytes 4194304 | tf_op jit(solution)/shard_map/middle/pallas_call | solution.py:191
  23.7 5.5 %collective-permute-done.4.message = s16[1040,256]{1,0:T(8,128)(2,1)S(1)} collective-permute-done((s16[1040,256]{1,0:T(8,128)(2,1)S(1)}, s16[1040,256]{1,0:T(8,128)(2,1)S(1)}, u32[]{:S(2)}, u32[]{:S(2)}) %collective-permute-start.4) | collective-permute-done | bytes 532512 | tf_op jit(solution)/shard_map/ppermute | solution.py:241
  29.2 2.0 %finish.2.refs_0_ = f32[2048,256]{1,0:T(8,128)} custom-call(f32[1024,256]{1,0:T(8,128)S(1)} %get-tuple-element.23.own, s16[1040,256]{1,0:T(8,128)(2,1)S(1)} %collective-permute-done.4.message), custom_call_target="tpu_custom_call" | custom-call | flops 786432 | bytes 2097152 | tf_op jit(solution)/shard_map/finish/pallas_call | solution.py:223
  31.2 0.0 collective-permute-done.3.message
  31.2 2.0 %finish.3 = f32[2048,256]{1,0:T(8,128)} custom-call(f32[1024,256]{1,0:T(8,128)S(1)} %get-tuple-element.21.own, s16[1040,256]{1,0:T(8,128)(2,1)S(1)} %collective-permute-done.3.message, f32[2048,256]{1,0:T(8,128)} %finish.2.refs_0_), custom_call_target="tpu_custom_call", output_to_operand_aliasing={{}: (2, {})} | custom-call | flops 786432 | bytes 2097152 | tf_op jit(solution)/shard_map/finish/pallas_call | solution.py:223
  (2 shorter events, 0.0 us)
Async XLA Ops:
  0.0 1.0 %copy-start = (bf16[1024,256]{1,0:T(8,128)(2,1)S(1)}, bf16[1024,256]{1,0:T(8,128)(2,1)}, u32[]{:S(2)}) copy-start(bf16[1024,256]{1,0:T(8,128)(2,1)} %source.1) | copy-start | bytes 1572868
  1.0 0.7 %copy-start.1 = (s32[1,8]{1,0:T(1,128)S(1)}, s32[1,8]{1,0:T(1,128)}, u32[]{:S(2)}) copy-start(s32[1,8]{1,0:T(1,128)} %ids.1) | copy-start | bytes 100
  1.7 0.7 %copy-start.2 = (s32[1,4]{1,0:T(1,128)S(1)}, s32[1,4]{1,0:T(1,128)}, u32[]{:S(2)}) copy-start(s32[1,4]{1,0:T(1,128)} %counts.1) | copy-start | bytes 52
  3.4 10.0 %collective-permute-start = (bf16[128,256]{1,0:T(8,128)(2,1)S(1)}, bf16[128,256]{1,0:T(8,128)(2,1)S(1)}, u32[]{:S(2)}, u32[]{:S(2)}) collective-permute-start(bf16[128,256]{1,0:T(8,128)(2,1)S(1)} %get-tuple-element.18), channel_id=1, source_target_pairs={{0,1},{1,2},{2,3},{3,0},{4,5},{5,6},{6,7},{7,4},{8,9},{9,10},{10,1... | collective-permute-start | bytes 196616 | tf_op jit(solution)/shard_map/ppermute | solution.py:241
  3.5 10.0 %collective-permute-start.1 = (bf16[128,256]{1,0:T(8,128)(2,1)S(1)}, bf16[128,256]{1,0:T(8,128)(2,1)S(1)}, u32[]{:S(2)}, u32[]{:S(2)}) collective-permute-start(bf16[128,256]{1,0:T(8,128)(2,1)S(1)} %get-tuple-element.19), channel_id=1, source_target_pairs={{0,2},{1,3},{2,0},{3,1},{4,6},{5,7},{6,4},{7,5},{8,10},{9,11},{10,... | collective-permute-start | bytes 196616 | tf_op jit(solution)/shard_map/ppermute | solution.py:241
  5.1 8.4 %collective-permute-start.2 = (bf16[128,256]{1,0:T(8,128)(2,1)S(1)}, bf16[128,256]{1,0:T(8,128)(2,1)S(1)}, u32[]{:S(2)}, u32[]{:S(2)}) collective-permute-start(bf16[128,256]{1,0:T(8,128)(2,1)S(1)} %get-tuple-element.20), channel_id=1, source_target_pairs={{0,3},{1,0},{2,1},{3,2},{4,7},{5,4},{6,5},{7,6},{8,11},{9,8},{10,9... | collective-permute-start | bytes 196616 | tf_op jit(solution)/shard_map/ppermute | solution.py:241
  6.4 1.2 %copy-start.3 = (bf16[128,4096]{1,0:T(8,128)(2,1)S(1)}, bf16[128,4096]{1,0:T(8,128)(2,1)}, u32[]{:S(2)}) copy-start(bf16[128,4096]{1,0:T(8,128)(2,1)} %weights.3) | copy-start | bytes 3145732
  7.7 0.7 %copy-start.5 = (s32[1,128]{1,0:T(1,128)S(1)}, s32[1,128]{1,0:T(1,128)}, u32[]{:S(2)}) copy-start(s32[1,128]{1,0:T(1,128)} %slots.3) | copy-start | bytes 1540
  8.3 0.7 %copy-start.6 = (s32[1,128]{1,0:T(1,128)S(1)}, s32[1,128]{1,0:T(1,128)}, u32[]{:S(2)}) copy-start(s32[1,128]{1,0:T(1,128)} %targets.3) | copy-start | bytes 1540
  14.3 3.6 %copy-start.4 = (bf16[128,4096]{1,0:T(8,128)(2,1)S(1)}, bf16[128,4096]{1,0:T(8,128)(2,1)}, u32[]{:S(2)}) copy-start(bf16[128,4096]{1,0:T(8,128)(2,1)} %weights.3) | copy-start | bytes 3145732
  14.3 3.6 %copy-start.7 = (s32[1,128]{1,0:T(1,128)S(1)}, s32[1,128]{1,0:T(1,128)}, u32[]{:S(2)}) copy-start(s32[1,128]{1,0:T(1,128)} %targets.3) | copy-start | bytes 1540
  14.4 14.9 %collective-permute-start.4 = (s16[1040,256]{1,0:T(8,128)(2,1)S(1)}, s16[1040,256]{1,0:T(8,128)(2,1)S(1)}, u32[]{:S(2)}, u32[]{:S(2)}) collective-permute-start(s16[1040,256]{1,0:T(8,128)(2,1)S(1)} %edge.3), channel_id=1, source_target_pairs={{0,1},{1,2},{2,3},{3,4},{4,5},{5,6},{6,7},{7,8},{8,9},{9,10},{10,1... | collective-permute-start | bytes 1597448 | tf_op jit(solution)/shard_map/ppermute | solution.py:241
  15.2 16.0 %collective-permute-start.3 = (s16[1040,256]{1,0:T(8,128)(2,1)S(1)}, s16[1040,256]{1,0:T(8,128)(2,1)S(1)}, u32[]{:S(2)}, u32[]{:S(2)}) collective-permute-start(s16[1040,256]{1,0:T(8,128)(2,1)S(1)} %edge.2), channel_id=1, source_target_pairs={{0,31},{1,0},{2,1},{3,2},{4,3},{5,4},{6,5},{7,6},{8,7},{9,8},{10,9... | collective-permute-start | bytes 1597448 | tf_op jit(solution)/shard_map/ppermute | solution.py:241

commit v2 on v1

--- a/solution.py
+++ b/solution.py
@@ -15,6 +15,7 @@
 GROUP = 64
 GROUPS = ROWS // GROUP
 FLOOR = 2.0**-110
+PITCH = BLOCK + 8
 VMEM = pl.BlockSpec(memory_space=pltpu.VMEM)
 SMEM = pl.BlockSpec(memory_space=pltpu.SMEM)
 ANY = pl.BlockSpec(memory_space=pl.ANY)
@@ -28,43 +29,61 @@
     return pl.CostEstimate(flops=flops, bytes_accessed=nbytes, transcendentals=0)
 
 
+def partner(own, k, members):
+    if members & (members - 1) == 0:
+        return lax.bitwise_xor(own, jnp.int32(k))
+    return lax.rem(own + k, members)
+
+
+def step_of(own, sender, members):
+    if members & (members - 1) == 0:
+        return lax.bitwise_xor(jnp.full_like(sender, own), sender)
+    return lax.rem(own - sender + members, members)
+
+
 def pick_kernel(members, capacity, ids, counts, source, *refs):
-    outs, sems = refs[:members], refs[members]
+    fed, refs = refs[:3], refs[3:]
+    picked, held, refs = refs[:members], refs[members : members + 3], refs[members + 3 :]
+    blocks, id_list, count_list, sems = refs
     own = lax.axis_index("blk")
-    copies = []
-    for k in range(members):
-        reader = lax.rem(own + k, members)
-        for j in range(capacity):
-            start = pl.multiple_of(ids[0, reader * capacity + j] * BLOCK, BLOCK)
-            copy = pltpu.make_async_copy(
-                source.at[pl.ds(start, BLOCK)],
-                outs[k].at[pl.ds(j * BLOCK, BLOCK)],
-                sems.at[k * capacity + j],
-            )
-            copy.start()
-            copies.append(copy)
+    copies = [
+        pltpu.make_async_copy(here, there, sems.at[n])
+        for n, (here, there) in enumerate(
+            zip((ids, counts, source) + fed, (id_list, count_list, blocks) + held)
+        )
+    ]
     for copy in copies:
+        copy.start()
+    for copy in copies[:3]:
         copy.wait()
     for k in range(members):
-        reader = lax.rem(own + k, members)
+        reader = partner(own, k, members)
         for j in range(capacity):
-
-            @pl.when(j >= counts[0, reader])
-            def _():
-                outs[k][pl.ds(j * BLOCK, BLOCK)] = jnp.zeros((BLOCK, COLS), jnp.bfloat16)
-
-
-def pick(members, capacity, send_ids, send_counts, source):
+            start = pl.multiple_of(id_list[0, reader * capacity + j] * BLOCK, BLOCK)
+            live = (j < count_list[0, reader]).astype(jnp.float32).astype(jnp.bfloat16)
+            picked[k][j * BLOCK : (j + 1) * BLOCK] = blocks[pl.ds(start, BLOCK)] * live
+    for copy in copies[3:]:
+        copy.wait()
+
+
+def pick(members, capacity, send_ids, send_counts, source, *fed):
     shape = (capacity * BLOCK, COLS)
-    return pl.pallas_call(
+    given = [pltpu.with_memory_space_constraint(x, pltpu.HBM) for x in (send_ids, send_counts, source) + fed]
+    results = pl.pallas_call(
         functools.partial(pick_kernel, members, capacity),
-        out_shape=[pltpu.VMEM(shape, jnp.bfloat16)] * members,
-        in_specs=[SMEM, SMEM, ANY],
-        out_specs=[VMEM] * members,
-        scratch_shapes=[pltpu.SemaphoreType.DMA((members * capacity,))],
+        out_shape=[pltpu.VMEM(shape, jnp.bfloat16)] * members + [pltpu.VMEM(x.shape, x.dtype) for x in fed],
+        in_specs=[ANY] * len(given),
+        out_specs=[VMEM] * (members + len(fed)),
+        scratch_shapes=[
+            pltpu.VMEM(source.shape, source.dtype),
+            pltpu.SMEM(send_ids.shape, jnp.int32),
+            pltpu.SMEM(send_counts.shape, jnp.int32),
+            pltpu.SemaphoreType.DMA((len(given),)),
+        ],
         compiler_params=params(),
         name="pick",
-    )(send_ids, send_counts, source)
+    )(*given)
+    return results[:members], results[members:]
 
 
 def spread_kernel(members, capacity, quarters, slots, targets, weights, *outs):
@@ -74,8 +93,7 @@
     count = len(quarters)
     slot = slots[...]
     sender = slot // capacity
-    shift = lax.rem(own - sender + members, members)
-    place = shift * capacity + slot % capacity
+    place = step_of(own, sender, members) * capacity + slot % capacity
     target = targets[...]
     rows = lax.broadcasted_iota(jnp.int32, (count * EB, tiles), 0)
     wanted = rows
@@ -118,7 +136,7 @@
                     outs[n][row, width + k * CHUNK : width + (k + 1) * CHUNK] = fine[part]
         return 0
 
-    lax.fori_loop(0, BLOCK // 2, step, 0, unroll=2)
+    lax.fori_loop(0, BLOCK // 2, step, 0, unroll=8)
 
 
 def spread(members, capacity, quarters, slots, targets, weights):
@@ -203,17 +221,23 @@
 def finish_kernel(half, own, message, *refs):
     out, rows, sems = refs[-3:]
     scale = jnp.exp2(message[ROWS : ROWS + GROUPS].astype(jnp.float32) - 15.0)
-    for i in range(BLOCK):
-        at = i * EB
-        g = at // GROUP
-        value = own[at : at + EB] + message[at : at + EB].astype(jnp.float32) * scale[g : g + 1]
+    targets = rows.reshape(COLS // 128, EB, PITCH, 128)
+    some = EB // 2
+    copies = []
+    for first in range(0, EB, some):
+        for i in range(BLOCK):
+            at = i * EB
+            g = at // GROUP
+            value = message[at : at + EB].astype(jnp.float32)[first : first + some]
+            value = own[at + first : at + first + some] + value * scale[g : g + 1]
+            for n in range(COLS // 128):
+                place = pl.ds(first * PITCH + i, some, stride=PITCH)
+                rows[n, place] = value[:, n * 128 : (n + 1) * 128]
         for n in range(COLS // 128):
-            rows[n, pl.ds(i, EB, stride=BLOCK)] = value[:, n * 128 : (n + 1) * 128]
-    copies = []
-    for n in range(COLS // 128):
-        there = out.at[pl.ds(half * ROWS, ROWS), pl.ds(n * 128, 128)]
-        copies.append(pltpu.make_async_copy(rows.at[n], there, sems.at[n]))
-        copies[n].start()
+            here = targets.at[n, pl.ds(first, some), pl.ds(0, BLOCK)]
+            there = out.at[pl.ds(half * EB + first, some), :, pl.ds(n * 128, 128)]
+            copies.append(pltpu.make_async_copy(here, there, sems.at[len(copies)]))
+            copies[-1].start()
     for copy in copies:
         copy.wait()
 
@@ -222,12 +246,12 @@
     given = [] if out is None else [out]
     return pl.pallas_call(
         functools.partial(finish_kernel, half),
-        out_shape=jax.ShapeDtypeStruct((2 * ROWS, COLS), jnp.float32),
+        out_shape=jax.ShapeDtypeStruct((2 * EB, BLOCK, COLS), jnp.float32),
         in_specs=[VMEM] * 2 + [ANY] * len(given),
         out_specs=ANY,
         scratch_shapes=[
-            pltpu.VMEM((COLS // 128, ROWS, 128), jnp.float32),
-            pltpu.SemaphoreType.DMA((COLS // 128,)),
+            pltpu.VMEM((COLS // 128, EB * PITCH, 128), jnp.float32),
+            pltpu.SemaphoreType.DMA((2 * COLS // 128,)),
         ],
         input_output_aliases={} if out is None else {2: 0},
         compiler_params=params(),
@@ -241,19 +265,28 @@
     return lax.ppermute(shard, axis, [(i, (i + by) % count) for i in range(count)])
 
 
+def exchanged(shard, k):
+    members = lax.axis_size("blk")
+    if members & (members - 1) == 0:
+        return lax.ppermute(shard, "blk", [(i, i ^ k) for i in range(members)])
+    return passed_along(shard, "blk", k)
+
+
 def body(source, send_ids, send_counts, tile_slot, tile_target, tile_weights):
     members = lax.axis_size("blk")
     capacity = send_ids.shape[1] // members
-    picked = pick(members, capacity, send_ids, send_counts, source)
-    blocks = [picked[0]] + [passed_along(picked[k], "blk", k) for k in range(1, members)]
-    tiles = (tile_slot, tile_target, tile_weights)
+    picked, tiles = pick(
+        members, capacity, send_ids, send_counts, source, tile_slot, tile_target, tile_weights
+    )
+    blocks = [picked[0]] + [exchanged(picked[k], k) for k in range(1, members)]
     lower, upper = spread(members, capacity, (0, 3), *tiles)
     first, second = spread(members, capacity, (1, 2), *tiles)
     from_prior = passed_along(edge(members, upper, blocks), ("grp", "blk"), 1)
     from_next = passed_along(edge(members, lower, blocks), ("grp", "blk"), -1)
     own_first, own_second = middle(members, first, second, blocks)
     out = finish(0, own_first, from_prior)
-    return finish(1, own_second, from_next, out)
+    out = finish(1, own_second, from_next, out)
+    return out.reshape(2 * ROWS, COLS)
 
 
 def solution(mesh):

time: 33.5 us -> 26.2 us (0.78)
  the two profiles are of different devices: /device:TPU:4 before, /device:TPU:5 now
where the time goes in v2:
time: 26.2 us; the launch traced here: 26.1 us
  waiting for transfers between devices  12.1 us (46%)
  Pallas kernels  10.1 us (39%)
  starting transfers between devices  3.87 us (15%)
    ppermute x2, waiting for transfers between devices, passed_along(): lax.ppermute(shard, axis, [(i, (i + by) % count) for i in range(count)])  10.3 us
    pallas_call x2, Pallas kernels, spread(): pl.pallas_call(functools.partial(spread_kernel, members, capacity, quarte...  3.47 us
    ppermute x3, starting transfers between devices, exchanged(): return lax.ppermute(shard, 'blk', [(i, i ^ k) for i in range(members)])  2.45 us
    pallas_call x2, Pallas kernels, finish(): pl.pallas_call(functools.partial(finish_kernel, half), out_shape=jax.Shap...  2.21 us
    ppermute x3, waiting for transfers between devices, exchanged(): return lax.ppermute(shard, 'blk', [(i, i ^ k) for i in range(members)])  1.81 us
    pallas_call x2, Pallas kernels, edge(): pl.pallas_call(functools.partial(edge_kernel, members), out_shape=pltpu.V...  1.66 us
    pallas_call x1, Pallas kernels, pick(): pl.pallas_call(functools.partial(pick_kernel, members, capacity), out_sha...  1.47 us
    ppermute x2, starting transfers between devices, passed_along(): lax.ppermute(shard, axis, [(i, (i + by) % count) for i in range(count)])  1.42 us
  transfers between devices with their start and end apart: 5, of which 4 were waited for; matrix products, arithmetic and copies ran while one was open for 0% of the time, Pallas kernels for 26%

profile of v2, /device:TPU:5, one launch (start us, length us, event | category | flops | bytes accessed | tf_op | source)
XLA Modules:
  0.0 26.1 jit_solution(14169720435160585885)
XLA Ops:
  0.0 1.5 %pick.1 = (bf16[128,256]{1,0:T(8,128)(2,1)S(1)}, bf16[128,256]{1,0:T(8,128)(2,1)S(1)}, bf16[128,256]{1,0:T(8,128)(2,1)S(1)}, bf16[128,256]{1,0:T(8,128)(2,1)S(1)...) custom-call(s32[1,8]{1,0:T(1,128)} %ids.1, s32[1,4]{1,0:T(1,128)} %counts.1, ...), custom_call_target="tpu_custom_call" | custom-call | tf_op jit(solution)/shard_map/pick/pallas_call | solution.py:72
  1.5 0.7 %collective-permute-start = (bf16[128,256]{1,0:T(8,128)(2,1)S(1)}, bf16[128,256]{1,0:T(8,128)(2,1)S(1)}, u32[]{:S(2)}, u32[]{:S(2)}) collective-permute-start(bf16[128,256]{1,0:T(8,128)(2,1)S(1)} %get-tuple-element.24), channel_id=1, source_target_pairs={{0,1},{1,0},{2,3},{3,2},{4,5},{5,4},{6,7},{7,6},{8,9},{9,8},{10,11... | collective-permute-start | bytes 196616 | tf_op jit(solution)/shard_map/ppermute | solution.py:271
  2.2 1.2 %collective-permute-start.1 = (bf16[128,256]{1,0:T(8,128)(2,1)S(1)}, bf16[128,256]{1,0:T(8,128)(2,1)S(1)}, u32[]{:S(2)}, u32[]{:S(2)}) collective-permute-start(bf16[128,256]{1,0:T(8,128)(2,1)S(1)} %get-tuple-element.25), channel_id=1, source_target_pairs={{0,2},{1,3},{2,0},{3,1},{4,6},{5,7},{6,4},{7,5},{8,10},{9,11},{10,... | collective-permute-start | bytes 196616 | tf_op jit(solution)/shard_map/ppermute | solution.py:271
  3.4 0.5 %collective-permute-start.2 = (bf16[128,256]{1,0:T(8,128)(2,1)S(1)}, bf16[128,256]{1,0:T(8,128)(2,1)S(1)}, u32[]{:S(2)}, u32[]{:S(2)}) collective-permute-start(bf16[128,256]{1,0:T(8,128)(2,1)S(1)} %get-tuple-element.26), channel_id=1, source_target_pairs={{0,3},{1,2},{2,1},{3,0},{4,7},{5,6},{6,5},{7,4},{8,11},{9,10},{10,... | collective-permute-start | bytes 196616 | tf_op jit(solution)/shard_map/ppermute | solution.py:271
  3.9 1.7 %spread.3 = (bf16[1024,1024]{1,0:T(8,128)(2,1)S(1)}, bf16[1024,1024]{1,0:T(8,128)(2,1)S(1)}) custom-call(s32[1,128]{1,0:T(1,128)S(1)} %get-tuple-element.18.slots, s32[1,128]{1,0:T(1,128)S(1)} %get-tuple-element.19.targets, bf16[128,4096]{1,0:T(8,128)(2,1)S(1)} %get-tuple-element.20.weights), custom_call_target="tpu_custom_call" | custom-call | flops 536870912 | bytes 6291456 | tf_op jit(solution)/shard_map/spread/pallas_call | solution.py:145
  5.7 0.0 collective-permute-done.refs_1_
  5.7 0.2 collective-permute-done.1.refs_2_
  5.9 1.6 %collective-permute-done.2.refs_3_ = bf16[128,256]{1,0:T(8,128)(2,1)S(1)} collective-permute-done((bf16[128,256]{1,0:T(8,128)(2,1)S(1)}, bf16[128,256]{1,0:T(8,128)(2,1)S(1)}, u32[]{:S(2)}, u32[]{:S(2)}) %collective-permute-start.2) | collective-permute-done | bytes 65568 | tf_op jit(solution)/shard_map/ppermute | solution.py:271
  7.5 0.8 %edge.3 = s16[1040,256]{1,0:T(8,128)(2,1)S(1)} custom-call(bf16[1024,1024]{1,0:T(8,128)(2,1)S(1)} %get-tuple-element.30.left, bf16[128,256]{1,0:T(8,128)(2,1)S(1)} %get-tuple-element.23.refs_0_, bf16[128,256]{1,0:T(8,128)(2,1)S(1)} %collective-permute-done.refs_1_, bf16[128,256]{1,0:T(8,128)(2,1)S(1)} %collective-permute-done.1.refs_2_, ...), custom_call_target="tpu_custom_call" | custom-call | flops 536870912 | bytes 2097152 | tf_op jit(solution)/shard_map/edge/pallas_call | solution.py:182
  8.3 1.4 %collective-permute-start.4 = (s16[1040,256]{1,0:T(8,128)(2,1)S(1)}, s16[1040,256]{1,0:T(8,128)(2,1)S(1)}, u32[]{:S(2)}, u32[]{:S(2)}) collective-permute-start(s16[1040,256]{1,0:T(8,128)(2,1)S(1)} %edge.3), channel_id=1, source_target_pairs={{0,1},{1,2},{2,3},{3,4},{4,5},{5,6},{6,7},{7,8},{8,9},{9,10},{10,1... | collective-permute-start | bytes 1597448 | tf_op jit(solution)/shard_map/ppermute | solution.py:265
  9.7 0.8 %edge.2 = s16[1040,256]{1,0:T(8,128)(2,1)S(1)} custom-call(bf16[1024,1024]{1,0:T(8,128)(2,1)S(1)} %get-tuple-element.28.left, bf16[128,256]{1,0:T(8,128)(2,1)S(1)} %get-tuple-element.23.refs_0_, bf16[128,256]{1,0:T(8,128)(2,1)S(1)} %collective-permute-done.refs_1_, bf16[128,256]{1,0:T(8,128)(2,1)S(1)} %collective-permute-done.1.refs_2_, ...), custom_call_target="tpu_custom_call" | custom-call | flops 536870912 | bytes 2097152 | tf_op jit(solution)/shard_map/edge/pallas_call | solution.py:182
  10.5 0.1 collective-permute-start.3
  10.6 1.7 %spread.2 = (bf16[1024,1024]{1,0:T(8,128)(2,1)S(1)}, bf16[1024,1024]{1,0:T(8,128)(2,1)S(1)}) custom-call(s32[1,128]{1,0:T(1,128)S(1)} %get-tuple-element.18.slots, s32[1,128]{1,0:T(1,128)S(1)} %get-tuple-element.19.targets, bf16[128,4096]{1,0:T(8,128)(2,1)S(1)} %get-tuple-element.20.weights), custom_call_target="tpu_custom_call" | custom-call | flops 536870912 | bytes 6291456 | tf_op jit(solution)/shard_map/spread/pallas_call | solution.py:145
  12.3 1.3 %middle.1 = (f32[1024,256]{1,0:T(8,128)S(1)}, f32[1024,256]{1,0:T(8,128)S(1)}) custom-call(bf16[1024,1024]{1,0:T(8,128)(2,1)S(1)} %get-tuple-element.21.first, bf16[1024,1024]{1,0:T(8,128)(2,1)S(1)} %get-tuple-element.22.second, bf16[128,256]{1,0:T(8,128)(2,1)S(1)} %get-tuple-element.23.refs_0_, bf16[128,256]{1,0:T(8,128)(2,1)S(1)} %collective-permute-done.refs_1_, ...), custom_call_target="tpu_custom_call" | custom-call | flops 1073741824 | bytes 4194304 | tf_op jit(solution)/shard_map/middle/pallas_call | solution.py:209
  13.6 5.2 %collective-permute-done.4.message = s16[1040,256]{1,0:T(8,128)(2,1)S(1)} collective-permute-done((s16[1040,256]{1,0:T(8,128)(2,1)S(1)}, s16[1040,256]{1,0:T(8,128)(2,1)S(1)}, u32[]{:S(2)}, u32[]{:S(2)}) %collective-permute-start.4) | collective-permute-done | bytes 532512 | tf_op jit(solution)/shard_map/ppermute | solution.py:265
  18.8 1.1 %finish.2.refs_0_ = f32[32,64,256]{2,1,0:T(8,128)} custom-call(f32[1024,256]{1,0:T(8,128)S(1)} %get-tuple-element.29.own, s16[1040,256]{1,0:T(8,128)(2,1)S(1)} %collective-permute-done.4.message), custom_call_target="tpu_custom_call" | custom-call | flops 786432 | bytes 2097152 | tf_op jit(solution)/shard_map/finish/pallas_call | solution.py:247
  19.9 5.1 %collective-permute-done.3.message = s16[1040,256]{1,0:T(8,128)(2,1)S(1)} collective-permute-done((s16[1040,256]{1,0:T(8,128)(2,1)S(1)}, s16[1040,256]{1,0:T(8,128)(2,1)S(1)}, u32[]{:S(2)}, u32[]{:S(2)}) %collective-permute-start.3) | collective-permute-done | bytes 532512 | tf_op jit(solution)/shard_map/ppermute | solution.py:265
  25.0 1.1 %finish.3 = f32[32,64,256]{2,1,0:T(8,128)} custom-call(f32[1024,256]{1,0:T(8,128)S(1)} %get-tuple-element.27.own, s16[1040,256]{1,0:T(8,128)(2,1)S(1)} %collective-permute-done.3.message, f32[32,64,256]{2,1,0:T(8,128)} %finish.2.refs_0_), custom_call_target="tpu_custom_call", output_to_operand_aliasing={{}: (2, {})} | custom-call | flops 786432 | bytes 2097152 | tf_op jit(solution)/shard_map/finish/pallas_call | solution.py:247
Async XLA Ops:
  1.5 4.2 %collective-permute-start = (bf16[128,256]{1,0:T(8,128)(2,1)S(1)}, bf16[128,256]{1,0:T(8,128)(2,1)S(1)}, u32[]{:S(2)}, u32[]{:S(2)}) collective-permute-start(bf16[128,256]{1,0:T(8,128)(2,1)S(1)} %get-tuple-element.24), channel_id=1, source_target_pairs={{0,1},{1,0},{2,3},{3,2},{4,5},{5,4},{6,7},{7,6},{8,9},{9,8},{10,11... | collective-permute-start | bytes 196616 | tf_op jit(solution)/shard_map/ppermute | solution.py:271
  2.2 3.7 %collective-permute-start.1 = (bf16[128,256]{1,0:T(8,128)(2,1)S(1)}, bf16[128,256]{1,0:T(8,128)(2,1)S(1)}, u32[]{:S(2)}, u32[]{:S(2)}) collective-permute-start(bf16[128,256]{1,0:T(8,128)(2,1)S(1)} %get-tuple-element.25), channel_id=1, source_target_pairs={{0,2},{1,3},{2,0},{3,1},{4,6},{5,7},{6,4},{7,5},{8,10},{9,11},{10,... | collective-permute-start | bytes 196616 | tf_op jit(solution)/shard_map/ppermute | solution.py:271
  3.4 4.0 %collective-permute-start.2 = (bf16[128,256]{1,0:T(8,128)(2,1)S(1)}, bf16[128,256]{1,0:T(8,128)(2,1)S(1)}, u32[]{:S(2)}, u32[]{:S(2)}) collective-permute-start(bf16[128,256]{1,0:T(8,128)(2,1)S(1)} %get-tuple-element.26), channel_id=1, source_target_pairs={{0,3},{1,2},{2,1},{3,0},{4,7},{5,6},{6,5},{7,4},{8,11},{9,10},{10,... | collective-permute-start | bytes 196616 | tf_op jit(solution)/shard_map/ppermute | solution.py:271
  8.3 10.4 %collective-permute-start.4 = (s16[1040,256]{1,0:T(8,128)(2,1)S(1)}, s16[1040,256]{1,0:T(8,128)(2,1)S(1)}, u32[]{:S(2)}, u32[]{:S(2)}) collective-permute-start(s16[1040,256]{1,0:T(8,128)(2,1)S(1)} %edge.3), channel_id=1, source_target_pairs={{0,1},{1,2},{2,3},{3,4},{4,5},{5,6},{6,7},{7,8},{8,9},{9,10},{10,1... | collective-permute-start | bytes 1597448 | tf_op jit(solution)/shard_map/ppermute | solution.py:265
  10.5 14.5 %collective-permute-start.3 = (s16[1040,256]{1,0:T(8,128)(2,1)S(1)}, s16[1040,256]{1,0:T(8,128)(2,1)S(1)}, u32[]{:S(2)}, u32[]{:S(2)}) collective-permute-start(s16[1040,256]{1,0:T(8,128)(2,1)S(1)} %edge.2), channel_id=1, source_target_pairs={{0,31},{1,0},{2,1},{3,2},{4,3},{5,4},{6,5},{7,6},{8,7},{9,8},{10,9... | collective-permute-start | bytes 1597448 | tf_op jit(solution)/shard_map/ppermute | solution.py:265

commit v3 on v2

--- a/solution.py
+++ b/solution.py
@@ -12,10 +12,8 @@
 EB = 16
 CHUNK = 2 * BLOCK
 ROWS = EB * BLOCK
-GROUP = 64
-GROUPS = ROWS // GROUP
+GROUP = 32
 FLOOR = 2.0**-110
-PITCH = BLOCK + 8
 VMEM = pl.BlockSpec(memory_space=pltpu.VMEM)
 SMEM = pl.BlockSpec(memory_space=pltpu.SMEM)
 ANY = pl.BlockSpec(memory_space=pl.ANY)
@@ -27,6 +25,10 @@
 
 def cost(flops, nbytes):
     return pl.CostEstimate(flops=flops, bytes_accessed=nbytes, transcendentals=0)
+
+
+def parity():
+    return lax.rem(lax.axis_index("grp") * lax.axis_size("blk") + lax.axis_index("blk"), 2)
 
 
 def partner(own, k, members):
@@ -97,8 +99,8 @@
     target = targets[...]
     rows = lax.broadcasted_iota(jnp.int32, (count * EB, tiles), 0)
     wanted = rows
-    for n, q in enumerate(quarters):
-        wanted = jnp.where(rows // EB == n, rows % EB + q * EB, wanted)
+    for n, (even, odd) in enumerate(quarters):
+        wanted = jnp.where(rows // EB == n, rows % EB + jnp.where(parity() == 1, odd, even) * EB, wanted)
     hit = target == wanted
     table = jnp.concatenate(
         [
@@ -153,7 +155,7 @@
     )(slots, targets, weights)
 
 
-def stack(blocks, both):
+def stack_kernel(blocks, both):
     rows = blocks[0].shape[0]
     for half in range(2):
         for k, block in enumerate(blocks):
@@ -161,12 +163,16 @@
             both[start : start + rows] = block[...]
 
 
-def edge_kernel(members, left, *refs):
-    blocks, message, both, powers = refs[:members], refs[members], refs[members + 1], refs[members + 2]
-    stack(blocks, both)
-    step = 4 * GROUP
-    for start in range(0, ROWS, step):
-        piece = jnp.dot(left[start : start + step], both[...], preferred_element_type=jnp.float32)
+def edge_kernel(first, count, blocks, left, *refs):
+    if blocks:
+        received, (message, both, powers) = refs[:blocks], refs[blocks:]
+        stack_kernel(received, both)
+    else:
+        both, message, powers = refs
+    step = min(count, 256)
+    for start in range(0, count, step):
+        rows = left[first + start : first + start + step]
+        piece = jnp.dot(rows, both[...], preferred_element_type=jnp.float32)
         for g in range(step // GROUP):
             rows = piece[g * GROUP : (g + 1) * GROUP]
             most = jnp.maximum(jnp.max(jnp.abs(rows), axis=0, keepdims=True), FLOOR)
@@ -175,28 +181,26 @@
             message[start + g * GROUP : start + (g + 1) * GROUP] = whole.astype(jnp.int16)
             at = start // GROUP + g
             powers[at : at + 1] = power.astype(jnp.int32)
-    message[ROWS : ROWS + GROUPS] = powers[...].astype(jnp.int16)
-
-
-def edge(members, left, blocks):
+    message[count : count + count // GROUP] = powers[...].astype(jnp.int16)
+
+
+def edge(first, count, left, *right):
+    out_shape = [pltpu.VMEM((count + count // GROUP, COLS), jnp.int16)]
+    if len(right) > 1:
+        out_shape.append(pltpu.VMEM((left.shape[1], COLS), jnp.bfloat16))
     return pl.pallas_call(
-        functools.partial(edge_kernel, members),
-        out_shape=pltpu.VMEM((ROWS + GROUPS, COLS), jnp.int16),
-        in_specs=[VMEM] * (1 + members),
-        out_specs=VMEM,
-        scratch_shapes=[
-            pltpu.VMEM((left.shape[1], COLS), jnp.bfloat16),
-            pltpu.VMEM((GROUPS, COLS), jnp.int32),
-        ],
-        compiler_params=params(),
-        cost_estimate=cost(2 * ROWS * left.shape[1] * COLS, 2 * 2**20),
+        functools.partial(edge_kernel, first, count, len(right) if len(right) > 1 else 0),
+        out_shape=out_shape,
+        in_specs=[VMEM] * (1 + len(right)),
+        out_specs=[VMEM] * len(out_shape),
+        scratch_shapes=[pltpu.VMEM((count // GROUP, COLS), jnp.int32)],
+        compiler_params=params(),
+        cost_estimate=cost(2 * count * left.shape[1] * COLS, 2 * 2**20),
         name="edge",
-    )(left, *blocks)
-
-
-def middle_kernel(members, first, second, *refs):
-    blocks, outs, both = refs[:members], refs[members : members + 2], refs[members + 2]
-    stack(blocks, both)
+    )(left, *right)
+
+
+def middle_kernel(first, second, both, *outs):
     step = 256
     for left, out in zip((first, second), outs):
         for start in range(0, ROWS, step):
@@ -205,57 +209,60 @@
             )
 
 
-def middle(members, first, second, blocks):
+def middle(first, second, both):
     return pl.pallas_call(
-        functools.partial(middle_kernel, members),
+        middle_kernel,
         out_shape=[pltpu.VMEM((ROWS, COLS), jnp.float32)] * 2,
-        in_specs=[VMEM] * (2 + members),
+        in_specs=[VMEM] * 3,
         out_specs=[VMEM] * 2,
-        scratch_shapes=[pltpu.VMEM((first.shape[1], COLS), jnp.bfloat16)],
         compiler_params=params(),
         cost_estimate=cost(4 * ROWS * first.shape[1] * COLS, 4 * 2**20),
         name="middle",
-    )(first, second, *blocks)
-
-
-def finish_kernel(half, own, message, *refs):
+    )(first, second, both)
+
+
+def finish_kernel(across, low, high, own, message, *refs):
     out, rows, sems = refs[-3:]
-    scale = jnp.exp2(message[ROWS : ROWS + GROUPS].astype(jnp.float32) - 15.0)
-    targets = rows.reshape(COLS // 128, EB, PITCH, 128)
+    half = parity() if across else 1 - parity()
+    count = (high - low) * EB
+    pitch = high - low + 8
+    scale = jnp.exp2(message[count : count + count // GROUP].astype(jnp.float32) - 15.0)
+    targets = rows.reshape(COLS // 128, EB, pitch, 128)
     some = EB // 2
     copies = []
     for first in range(0, EB, some):
-        for i in range(BLOCK):
+        for i in range(high - low):
             at = i * EB
             g = at // GROUP
             value = message[at : at + EB].astype(jnp.float32)[first : first + some]
-            value = own[at + first : at + first + some] + value * scale[g : g + 1]
+            at = (low + i) * EB + first
+            value = own[at : at + some] + value * scale[g : g + 1]
             for n in range(COLS // 128):
-                place = pl.ds(first * PITCH + i, some, stride=PITCH)
+                place = pl.ds(first * pitch + i, some, stride=pitch)
                 rows[n, place] = value[:, n * 128 : (n + 1) * 128]
         for n in range(COLS // 128):
-            here = targets.at[n, pl.ds(first, some), pl.ds(0, BLOCK)]
-            there = out.at[pl.ds(half * EB + first, some), :, pl.ds(n * 128, 128)]
+            here = targets.at[n, pl.ds(first, some), pl.ds(0, high - low)]
+            there = out.at[pl.ds(half * EB + first, some), pl.ds(low, high - low), pl.ds(n * 128, 128)]
             copies.append(pltpu.make_async_copy(here, there, sems.at[len(copies)]))
             copies[-1].start()
     for copy in copies:
         copy.wait()
 
 
-def finish(half, own, message, out=None):
+def finish(across, low, high, own, message, out=None):
     given = [] if out is None else [out]
     return pl.pallas_call(
-        functools.partial(finish_kernel, half),
+        functools.partial(finish_kernel, across, low, high),
         out_shape=jax.ShapeDtypeStruct((2 * EB, BLOCK, COLS), jnp.float32),
         in_specs=[VMEM] * 2 + [ANY] * len(given),
         out_specs=ANY,
         scratch_shapes=[
-            pltpu.VMEM((COLS // 128, EB * PITCH, 128), jnp.float32),
+            pltpu.VMEM((COLS // 128, EB * (high - low + 8), 128), jnp.float32),
             pltpu.SemaphoreType.DMA((2 * COLS // 128,)),
         ],
         input_output_aliases={} if out is None else {2: 0},
         compiler_params=params(),
-        cost_estimate=cost(3 * ROWS * COLS, 2 * 2**20),
+        cost_estimate=cost(3 * (high - low) * EB * COLS, 2 * 2**20),
         name="finish",
     )(own, message, *given)
 
@@ -270,6 +277,14 @@
     if members & (members - 1) == 0:
         return lax.ppermute(shard, "blk", [(i, i ^ k) for i in range(members)])
     return passed_along(shard, "blk", k)
+
+
+def ring_swap(shard, across):
+    axes = ("grp", "blk")
+    count = lax.axis_size(axes)
+    if across:
+        return lax.ppermute(shard, axes, [(i, (i + (1 if i % 2 else -1)) % count) for i in range(count)])
+    return lax.ppermute(shard, axes, [(i, i ^ 1) for i in range(count)])
 
 
 def body(source, send_ids, send_counts, tile_slot, tile_target, tile_weights):
@@ -279,13 +294,17 @@
         members, capacity, send_ids, send_counts, source, tile_slot, tile_target, tile_weights
     )
     blocks = [picked[0]] + [exchanged(picked[k], k) for k in range(1, members)]
-    lower, upper = spread(members, capacity, (0, 3), *tiles)
-    first, second = spread(members, capacity, (1, 2), *tiles)
-    from_prior = passed_along(edge(members, upper, blocks), ("grp", "blk"), 1)
-    from_next = passed_along(edge(members, lower, blocks), ("grp", "blk"), -1)
-    own_first, own_second = middle(members, first, second, blocks)
-    out = finish(0, own_first, from_prior)
-    out = finish(1, own_second, from_next, out)
+    left_across, left_chip = spread(members, capacity, ((0, 3), (3, 0)), *tiles)
+    own_left = spread(members, capacity, ((1, 2), (2, 1)), *tiles)
+    half = ROWS // 2
+    message_0, both = edge(0, half, left_across, *blocks)
+    message_0 = ring_swap(message_0, True)
+    message_1 = ring_swap(edge(half, half, left_across, both)[0], True)
+    message_chip = ring_swap(edge(0, ROWS, left_chip, both)[0], False)
+    own_across, own_chip = middle(*own_left, both)
+    out = finish(False, 0, BLOCK, own_chip, message_chip)
+    out = finish(True, 0, BLOCK // 2, own_across, message_0, out)
+    out = finish(True, BLOCK // 2, BLOCK, own_across, message_1, out)
     return out.reshape(2 * ROWS, COLS)
 
 

time: 26.2 us -> 26.8 us (1.023)
  the two profiles are of different devices: /device:TPU:5 before, /device:TPU:0 now
where the time goes in v3:
time: 26.8 us; the launch traced here: 26.6 us
  Pallas kernels  11 us (41%)
  starting transfers between devices  8.79 us (33%)
  waiting for transfers between devices  6.76 us (25%)
    ppermute x2, starting transfers between devices, ring_swap(): lax.ppermute(shard, axes, [(i, (i + (1 if i % 2 else -1)) % count) for i...  5.41 us
    ppermute x2, waiting for transfers between devices, ring_swap(): lax.ppermute(shard, axes, [(i, (i + (1 if i % 2 else -1)) % count) for i...  4.51 us
    pallas_call x2, Pallas kernels, spread(): pl.pallas_call(functools.partial(spread_kernel, members, capacity, quarte...  3.44 us
    ppermute x3, starting transfers between devices, exchanged(): return lax.ppermute(shard, 'blk', [(i, i ^ k) for i in range(members)])  3.15 us
    pallas_call x3, Pallas kernels, finish(): pl.pallas_call(functools.partial(finish_kernel, across, low, high), out_s...  2.89 us
    ppermute x3, waiting for transfers between devices, exchanged(): return lax.ppermute(shard, 'blk', [(i, i ^ k) for i in range(members)])  2.24 us
    pallas_call x3, Pallas kernels, edge(): pl.pallas_call(functools.partial(edge_kernel, first, count, len(right) if...  1.95 us
    pallas_call x1, Pallas kernels, pick(): pl.pallas_call(functools.partial(pick_kernel, members, capacity), out_sha...  1.47 us
  transfers between devices with their start and end apart: 6, of which 3 were waited for; matrix products, arithmetic and copies ran while one was open for 0% of the time, Pallas kernels for 27%

profile of v3, /device:TPU:0, one launch (start us, length us, event | category | flops | bytes accessed | tf_op | source)
XLA Modules:
  0.0 26.6 jit_solution(16792945568444680659)
XLA Ops:
  0.0 1.5 %pick.1 = (bf16[128,256]{1,0:T(8,128)(2,1)S(1)}, bf16[128,256]{1,0:T(8,128)(2,1)S(1)}, bf16[128,256]{1,0:T(8,128)(2,1)S(1)}, bf16[128,256]{1,0:T(8,128)(2,1)S(1)...) custom-call(s32[1,8]{1,0:T(1,128)} %ids.1, s32[1,4]{1,0:T(1,128)} %counts.1, ...), custom_call_target="tpu_custom_call" | custom-call | tf_op jit(solution)/shard_map/pick/pallas_call | solution.py:74
  1.5 0.5 %collective-permute-start = (bf16[128,256]{1,0:T(8,128)(2,1)S(1)}, bf16[128,256]{1,0:T(8,128)(2,1)S(1)}, u32[]{:S(2)}, u32[]{:S(2)}) collective-permute-start(bf16[128,256]{1,0:T(8,128)(2,1)S(1)} %get-tuple-element.27), channel_id=1, source_target_pairs={{0,1},{1,0},{2,3},{3,2},{4,5},{5,4},{6,7},{7,6},{8,9},{9,8},{10,11... | collective-permute-start | bytes 196616 | tf_op jit(solution)/shard_map/ppermute | solution.py:278
  2.0 2.6 %collective-permute-start.1 = (bf16[128,256]{1,0:T(8,128)(2,1)S(1)}, bf16[128,256]{1,0:T(8,128)(2,1)S(1)}, u32[]{:S(2)}, u32[]{:S(2)}) collective-permute-start(bf16[128,256]{1,0:T(8,128)(2,1)S(1)} %get-tuple-element.28), channel_id=1, source_target_pairs={{0,2},{1,3},{2,0},{3,1},{4,6},{5,7},{6,4},{7,5},{8,10},{9,11},{10,... | collective-permute-start | bytes 196616 | tf_op jit(solution)/shard_map/ppermute | solution.py:278
  4.6 0.1 collective-permute-start.2
  4.6 1.7 %spread.3 = (bf16[1024,1024]{1,0:T(8,128)(2,1)S(1)}, bf16[1024,1024]{1,0:T(8,128)(2,1)S(1)}) custom-call(s32[1,128]{1,0:T(1,128)S(1)} %get-tuple-element.20.slots, s32[1,128]{1,0:T(1,128)S(1)} %get-tuple-element.21.targets, bf16[128,4096]{1,0:T(8,128)(2,1)S(1)} %get-tuple-element.22.weights), custom_call_target="tpu_custom_call" | custom-call | flops 536870912 | bytes 6291456 | tf_op jit(solution)/shard_map/spread/pallas_call | solution.py:147
  6.4 0.0 collective-permute-done.refs_1_
  6.4 0.9 %collective-permute-done.1.refs_2_ = bf16[128,256]{1,0:T(8,128)(2,1)S(1)} collective-permute-done((bf16[128,256]{1,0:T(8,128)(2,1)S(1)}, bf16[128,256]{1,0:T(8,128)(2,1)S(1)}, u32[]{:S(2)}, u32[]{:S(2)}) %collective-permute-start.1) | collective-permute-done | bytes 65568 | tf_op jit(solution)/shard_map/ppermute | solution.py:278
  7.3 1.4 %collective-permute-done.2.refs_3_ = bf16[128,256]{1,0:T(8,128)(2,1)S(1)} collective-permute-done((bf16[128,256]{1,0:T(8,128)(2,1)S(1)}, bf16[128,256]{1,0:T(8,128)(2,1)S(1)}, u32[]{:S(2)}, u32[]{:S(2)}) %collective-permute-start.2) | collective-permute-done | bytes 65568 | tf_op jit(solution)/shard_map/ppermute | solution.py:278
  8.6 0.5 %edge.3 = (s16[528,256]{1,0:T(8,128)(2,1)S(1)}, bf16[1024,256]{1,0:T(8,128)(2,1)S(1)}) custom-call(bf16[1024,1024]{1,0:T(8,128)(2,1)S(1)} %get-tuple-element.25.left, bf16[128,256]{1,0:T(8,128)(2,1)S(1)} %get-tuple-element.26.refs_0_, bf16[128,256]{1,0:T(8,128)(2,1)S(1)} %collective-permute-done.refs_1_, ...), custom_call_target="tpu_custom_call" | custom-call | flops 268435456 | bytes 2097152 | tf_op jit(solution)/shard_map/edge/pallas_call | solution.py:191
  9.2 0.9 %edge.5 = s16[1056,256]{1,0:T(8,128)(2,1)S(1)} custom-call(bf16[1024,1024]{1,0:T(8,128)(2,1)S(1)} %get-tuple-element.34.left, bf16[1024,256]{1,0:T(8,128)(2,1)S(1)} %get-tuple-element.30.both.refs_0_), custom_call_target="tpu_custom_call" | custom-call | flops 536870912 | bytes 2097152 | tf_op jit(solution)/shard_map/edge/pallas_call | solution.py:191
  10.0 0.2 collective-permute-start.5
  10.3 5.3 %collective-permute-start.4 = (s16[528,256]{1,0:T(8,128)(2,1)S(1)}, s16[528,256]{1,0:T(8,128)(2,1)S(1)}, u32[]{:S(2)}, u32[]{:S(2)}) collective-permute-start(s16[528,256]{1,0:T(8,128)(2,1)S(1)} %get-tuple-element.32), channel_id=1, source_target_pairs={{0,31},{1,2},{2,1},{3,4},{4,3},{5,6},{6,5},{7,8},{8,7},{9,10},{10,... | collective-permute-start | bytes 811016 | tf_op jit(solution)/shard_map/ppermute | solution.py:286
  15.6 0.5 %edge.4 = s16[528,256]{1,0:T(8,128)(2,1)S(1)} custom-call(bf16[1024,1024]{1,0:T(8,128)(2,1)S(1)} %get-tuple-element.25.left, bf16[1024,256]{1,0:T(8,128)(2,1)S(1)} %get-tuple-element.30.both.refs_0_), custom_call_target="tpu_custom_call" | custom-call | flops 268435456 | bytes 2097152 | tf_op jit(solution)/shard_map/edge/pallas_call | solution.py:191
  16.1 0.1 collective-permute-start.3
  16.2 1.7 %spread.2 = (bf16[1024,1024]{1,0:T(8,128)(2,1)S(1)}, bf16[1024,1024]{1,0:T(8,128)(2,1)S(1)}) custom-call(s32[1,128]{1,0:T(1,128)S(1)} %get-tuple-element.20.slots, s32[1,128]{1,0:T(1,128)S(1)} %get-tuple-element.21.targets, bf16[128,4096]{1,0:T(8,128)(2,1)S(1)} %get-tuple-element.22.weights), custom_call_target="tpu_custom_call" | custom-call | flops 536870912 | bytes 6291456 | tf_op jit(solution)/shard_map/spread/pallas_call | solution.py:147
  17.9 1.2 %middle.1 = (f32[1024,256]{1,0:T(8,128)S(1)}, f32[1024,256]{1,0:T(8,128)S(1)}) custom-call(bf16[1024,1024]{1,0:T(8,128)(2,1)S(1)} %get-tuple-element.23.first, bf16[1024,1024]{1,0:T(8,128)(2,1)S(1)} %get-tuple-element.24.second, bf16[1024,256]{1,0:T(8,128)(2,1)S(1)} %get-tuple-element.30.both.refs_0_), custom_call_target="tpu_custom_call" | custom-call | flops 1073741824 | bytes 4194304 | tf_op jit(solution)/shard_map/middle/pallas_call | solution.py:213
  19.2 0.0 collective-permute-done.5.message
  19.2 1.1 %finish.3.refs_0_ = f32[32,64,256]{2,1,0:T(8,128)} custom-call(f32[1024,256]{1,0:T(8,128)S(1)} %get-tuple-element.33.own, s16[1056,256]{1,0:T(8,128)(2,1)S(1)} %collective-permute-done.5.message), custom_call_target="tpu_custom_call" | custom-call | flops 786432 | bytes 2097152 | tf_op jit(solution)/shard_map/finish/pallas_call | solution.py:254
  20.3 0.0 collective-permute-done.4.message
  20.4 0.9 %finish.4.refs_0_ = f32[32,64,256]{2,1,0:T(8,128)} custom-call(f32[1024,256]{1,0:T(8,128)S(1)} %get-tuple-element.31.own, s16[528,256]{1,0:T(8,128)(2,1)S(1)} %collective-permute-done.4.message, f32[32,64,256]{2,1,0:T(8,128)} %finish.3.refs_0_), custom_call_target="tpu_custom_call", output_to_operand_aliasing={{}: (2, {})} | custom-call | flops 393216 | bytes 2097152 | tf_op jit(solution)/shard_map/finish/pallas_call | solution.py:254
  21.2 4.5 %collective-permute-done.3.message = s16[528,256]{1,0:T(8,128)(2,1)S(1)} collective-permute-done((s16[528,256]{1,0:T(8,128)(2,1)S(1)}, s16[528,256]{1,0:T(8,128)(2,1)S(1)}, u32[]{:S(2)}, u32[]{:S(2)}) %collective-permute-start.3) | collective-permute-done | bytes 270368 | tf_op jit(solution)/shard_map/ppermute | solution.py:286
  25.8 0.9 %finish.5 = f32[32,64,256]{2,1,0:T(8,128)} custom-call(f32[1024,256]{1,0:T(8,128)S(1)} %get-tuple-element.31.own, s16[528,256]{1,0:T(8,128)(2,1)S(1)} %collective-permute-done.3.message, f32[32,64,256]{2,1,0:T(8,128)} %finish.4.refs_0_), custom_call_target="tpu_custom_call", output_to_operand_aliasing={{}: (2, {})} | custom-call | flops 393216 | bytes 2097152 | tf_op jit(solution)/shard_map/finish/pallas_call | solution.py:254
Async XLA Ops:
  1.5 4.9 %collective-permute-start = (bf16[128,256]{1,0:T(8,128)(2,1)S(1)}, bf16[128,256]{1,0:T(8,128)(2,1)S(1)}, u32[]{:S(2)}, u32[]{:S(2)}) collective-permute-start(bf16[128,256]{1,0:T(8,128)(2,1)S(1)} %get-tuple-element.27), channel_id=1, source_target_pairs={{0,1},{1,0},{2,3},{3,2},{4,5},{5,4},{6,7},{7,6},{8,9},{9,8},{10,11... | collective-permute-start | bytes 196616 | tf_op jit(solution)/shard_map/ppermute | solution.py:278
  2.0 5.3 %collective-permute-start.1 = (bf16[128,256]{1,0:T(8,128)(2,1)S(1)}, bf16[128,256]{1,0:T(8,128)(2,1)S(1)}, u32[]{:S(2)}, u32[]{:S(2)}) collective-permute-start(bf16[128,256]{1,0:T(8,128)(2,1)S(1)} %get-tuple-element.28), channel_id=1, source_target_pairs={{0,2},{1,3},{2,0},{3,1},{4,6},{5,7},{6,4},{7,5},{8,10},{9,11},{10,... | collective-permute-start | bytes 196616 | tf_op jit(solution)/shard_map/ppermute | solution.py:278
  4.6 4.0 %collective-permute-start.2 = (bf16[128,256]{1,0:T(8,128)(2,1)S(1)}, bf16[128,256]{1,0:T(8,128)(2,1)S(1)}, u32[]{:S(2)}, u32[]{:S(2)}) collective-permute-start(bf16[128,256]{1,0:T(8,128)(2,1)S(1)} %get-tuple-element.29), channel_id=1, source_target_pairs={{0,3},{1,2},{2,1},{3,0},{4,7},{5,6},{6,5},{7,4},{8,11},{9,10},{10,... | collective-permute-start | bytes 196616 | tf_op jit(solution)/shard_map/ppermute | solution.py:278
  10.0 9.2 %collective-permute-start.5 = (s16[1056,256]{1,0:T(8,128)(2,1)S(1)}, s16[1056,256]{1,0:T(8,128)(2,1)S(1)}, u32[]{:S(2)}, u32[]{:S(2)}) collective-permute-start(s16[1056,256]{1,0:T(8,128)(2,1)S(1)} %edge.5), channel_id=1, source_target_pairs={{0,1},{1,0},{2,3},{3,2},{4,5},{5,4},{6,7},{7,6},{8,9},{9,8},{10,11... | collective-permute-start | bytes 1622024 | tf_op jit(solution)/shard_map/ppermute | solution.py:287
  10.3 10.1 %collective-permute-start.4 = (s16[528,256]{1,0:T(8,128)(2,1)S(1)}, s16[528,256]{1,0:T(8,128)(2,1)S(1)}, u32[]{:S(2)}, u32[]{:S(2)}) collective-permute-start(s16[528,256]{1,0:T(8,128)(2,1)S(1)} %get-tuple-element.32), channel_id=1, source_target_pairs={{0,31},{1,2},{2,1},{3,4},{4,3},{5,6},{6,5},{7,8},{8,7},{9,10},{10,... | collective-permute-start | bytes 811016 | tf_op jit(solution)/shard_map/ppermute | solution.py:286
  16.1 9.7 %collective-permute-start.3 = (s16[528,256]{1,0:T(8,128)(2,1)S(1)}, s16[528,256]{1,0:T(8,128)(2,1)S(1)}, u32[]{:S(2)}, u32[]{:S(2)}) collective-permute-start(s16[528,256]{1,0:T(8,128)(2,1)S(1)} %edge.4), channel_id=1, source_target_pairs={{0,31},{1,2},{2,1},{3,4},{4,3},{5,6},{6,5},{7,8},{8,7},{9,10},{10,... | collective-permute-start | bytes 811016 | tf_op jit(solution)/shard_map/ppermute | solution.py:286

commit v4 on v3

--- a/solution.py
+++ b/solution.py
@@ -13,6 +13,8 @@
 CHUNK = 2 * BLOCK
 ROWS = EB * BLOCK
 GROUP = 32
+WHOLE = (ROWS,)
+PARTS = (ROWS // 2, ROWS // 2)
 FLOOR = 2.0**-110
 VMEM = pl.BlockSpec(memory_space=pltpu.VMEM)
 SMEM = pl.BlockSpec(memory_space=pltpu.SMEM)
@@ -163,12 +165,7 @@
             both[start : start + rows] = block[...]
 
 
-def edge_kernel(first, count, blocks, left, *refs):
-    if blocks:
-        received, (message, both, powers) = refs[:blocks], refs[blocks:]
-        stack_kernel(received, both)
-    else:
-        both, message, powers = refs
+def coded(left, first, count, both, message, powers):
     step = min(count, 256)
     for start in range(0, count, step):
         rows = left[first + start : first + start + step]
@@ -184,18 +181,32 @@
     message[count : count + count // GROUP] = powers[...].astype(jnp.int16)
 
 
-def edge(first, count, left, *right):
-    out_shape = [pltpu.VMEM((count + count // GROUP, COLS), jnp.int16)]
+def edge_kernel(parts, blocks, left, *refs):
+    received, refs = refs[:blocks], refs[blocks:]
+    messages, refs = refs[: len(parts)], refs[len(parts) :]
+    both, powers = refs[0], refs[1:]
+    if blocks > 1:
+        stack_kernel(received, both)
+    else:
+        both, powers = received[0], refs
+    first = 0
+    for count, message, power in zip(parts, messages, powers):
+        coded(left, first, count, both, message, power)
+        first += count
+
+
+def edge(parts, left, *right):
+    out_shape = [pltpu.VMEM((count + count // GROUP, COLS), jnp.int16) for count in parts]
     if len(right) > 1:
         out_shape.append(pltpu.VMEM((left.shape[1], COLS), jnp.bfloat16))
     return pl.pallas_call(
-        functools.partial(edge_kernel, first, count, len(right) if len(right) > 1 else 0),
+        functools.partial(edge_kernel, parts, len(right)),
         out_shape=out_shape,
         in_specs=[VMEM] * (1 + len(right)),
         out_specs=[VMEM] * len(out_shape),
-        scratch_shapes=[pltpu.VMEM((count // GROUP, COLS), jnp.int32)],
-        compiler_params=params(),
-        cost_estimate=cost(2 * count * left.shape[1] * COLS, 2 * 2**20),
+        scratch_shapes=[pltpu.VMEM((count // GROUP, COLS), jnp.int32) for count in parts],
+        compiler_params=params(),
+        cost_estimate=cost(2 * ROWS * left.shape[1] * COLS, 2 * 2**20),
         name="edge",
     )(left, *right)
 
@@ -221,50 +232,50 @@
     )(first, second, both)
 
 
-def finish_kernel(across, low, high, own, message, *refs):
-    out, rows, sems = refs[-3:]
+def finish_kernel(across, parts, own, *refs):
+    messages, (out, rows, sems) = refs[: len(parts)], refs[-3:]
     half = parity() if across else 1 - parity()
-    count = (high - low) * EB
-    pitch = high - low + 8
-    scale = jnp.exp2(message[count : count + count // GROUP].astype(jnp.float32) - 15.0)
+    pitch = BLOCK + 8
     targets = rows.reshape(COLS // 128, EB, pitch, 128)
     some = EB // 2
     copies = []
     for first in range(0, EB, some):
-        for i in range(high - low):
-            at = i * EB
-            g = at // GROUP
-            value = message[at : at + EB].astype(jnp.float32)[first : first + some]
-            at = (low + i) * EB + first
-            value = own[at : at + some] + value * scale[g : g + 1]
-            for n in range(COLS // 128):
-                place = pl.ds(first * pitch + i, some, stride=pitch)
-                rows[n, place] = value[:, n * 128 : (n + 1) * 128]
+        i = 0
+        for count, message in zip(parts, messages):
+            scale = jnp.exp2(message[count : count + count // GROUP].astype(jnp.float32) - 15.0)
+            for at in range(0, count, EB):
+                g = at // GROUP
+                value = message[at : at + EB].astype(jnp.float32)[first : first + some]
+                value = own[i * EB + first : i * EB + first + some] + value * scale[g : g + 1]
+                for n in range(COLS // 128):
+                    place = pl.ds(first * pitch + i, some, stride=pitch)
+                    rows[n, place] = value[:, n * 128 : (n + 1) * 128]
+                i += 1
         for n in range(COLS // 128):
-            here = targets.at[n, pl.ds(first, some), pl.ds(0, high - low)]
-            there = out.at[pl.ds(half * EB + first, some), pl.ds(low, high - low), pl.ds(n * 128, 128)]
+            here = targets.at[n, pl.ds(first, some), pl.ds(0, BLOCK)]
+            there = out.at[pl.ds(half * EB + first, some), :, pl.ds(n * 128, 128)]
             copies.append(pltpu.make_async_copy(here, there, sems.at[len(copies)]))
             copies[-1].start()
     for copy in copies:
         copy.wait()
 
 
-def finish(across, low, high, own, message, out=None):
+def finish(across, parts, own, messages, out=None):
     given = [] if out is None else [out]
     return pl.pallas_call(
-        functools.partial(finish_kernel, across, low, high),
+        functools.partial(finish_kernel, across, parts),
         out_shape=jax.ShapeDtypeStruct((2 * EB, BLOCK, COLS), jnp.float32),
-        in_specs=[VMEM] * 2 + [ANY] * len(given),
+        in_specs=[VMEM] * (1 + len(parts)) + [ANY] * len(given),
         out_specs=ANY,
         scratch_shapes=[
-            pltpu.VMEM((COLS // 128, EB * (high - low + 8), 128), jnp.float32),
+            pltpu.VMEM((COLS // 128, EB * (BLOCK + 8), 128), jnp.float32),
             pltpu.SemaphoreType.DMA((2 * COLS // 128,)),
         ],
-        input_output_aliases={} if out is None else {2: 0},
-        compiler_params=params(),
-        cost_estimate=cost(3 * (high - low) * EB * COLS, 2 * 2**20),
+        input_output_aliases={} if out is None else {1 + len(parts): 0},
+        compiler_params=params(),
+        cost_estimate=cost(3 * ROWS * COLS, 2 * 2**20),
         name="finish",
-    )(own, message, *given)
+    )(own, *messages, *given)
 
 
 def passed_along(shard, axis, by):
@@ -295,16 +306,14 @@
     )
     blocks = [picked[0]] + [exchanged(picked[k], k) for k in range(1, members)]
     left_across, left_chip = spread(members, capacity, ((0, 3), (3, 0)), *tiles)
+    message_across, both = edge(WHOLE, left_across, *blocks)
+    message_across = ring_swap(message_across, True)
+    messages_chip = [ring_swap(message, False) for message in edge(PARTS, left_chip, both)]
+    tiles, both = lax.optimization_barrier((tiles, both))
     own_left = spread(members, capacity, ((1, 2), (2, 1)), *tiles)
-    half = ROWS // 2
-    message_0, both = edge(0, half, left_across, *blocks)
-    message_0 = ring_swap(message_0, True)
-    message_1 = ring_swap(edge(half, half, left_across, both)[0], True)
-    message_chip = ring_swap(edge(0, ROWS, left_chip, both)[0], False)
     own_across, own_chip = middle(*own_left, both)
-    out = finish(False, 0, BLOCK, own_chip, message_chip)
-    out = finish(True, 0, BLOCK // 2, own_across, message_0, out)
-    out = finish(True, BLOCK // 2, BLOCK, own_across, message_1, out)
+    out = finish(False, PARTS, own_chip, messages_chip)
+    out = finish(True, WHOLE, own_across, [message_across], out)
     return out.reshape(2 * ROWS, COLS)
 
 

time: 26.8 us -> 24.8 us (0.925)
  the two profiles are of different devices: /device:TPU:0 before, /device:TPU:5 now
where the time goes in v4:
time: 24.8 us; the launch traced here: 24.4 us
  Pallas kernels  10.2 us (41%)
  waiting for transfers between devices  9.75 us (39%)
  starting transfers between devices  4.37 us (18%)
    ppermute x1, waiting for transfers between devices, ring_swap(): lax.ppermute(shard, axes, [(i, (i + (1 if i % 2 else -1)) % count) for i...  7.92 us
    pallas_call x2, Pallas kernels, spread(): pl.pallas_call(functools.partial(spread_kernel, members, capacity, quarte...  3.44 us
    ppermute x3, starting transfers between devices, exchanged(): return lax.ppermute(shard, 'blk', [(i, i ^ k) for i in range(members)])  2.45 us
    pallas_call x2, Pallas kernels, finish(): pl.pallas_call(functools.partial(finish_kernel, across, parts), out_shape...  2.23 us
    ppermute x3, waiting for transfers between devices, exchanged(): return lax.ppermute(shard, 'blk', [(i, i ^ k) for i in range(members)])  1.83 us
    pallas_call x2, Pallas kernels, edge(): pl.pallas_call(functools.partial(edge_kernel, parts, len(right)), out_sha...  1.78 us
    pallas_call x1, Pallas kernels, pick(): pl.pallas_call(functools.partial(pick_kernel, members, capacity), out_sha...  1.47 us
    ppermute x1, starting transfers between devices, ring_swap(): lax.ppermute(shard, axes, [(i, (i + (1 if i % 2 else -1)) % count) for i...  1.35 us
  transfers between devices with their start and end apart: 6, of which 3 were waited for; matrix products, arithmetic and copies ran while one was open for 0% of the time, Pallas kernels for 27%

profile of v4, /device:TPU:5, one launch (start us, length us, event | category | flops | bytes accessed | tf_op | source)
XLA Modules:
  0.0 24.4 jit_solution(7569394719016169662)
XLA Ops:
  0.0 1.5 %pick.1 = (bf16[128,256]{1,0:T(8,128)(2,1)S(1)}, bf16[128,256]{1,0:T(8,128)(2,1)S(1)}, bf16[128,256]{1,0:T(8,128)(2,1)S(1)}, bf16[128,256]{1,0:T(8,128)(2,1)S(1)...) custom-call(s32[1,8]{1,0:T(1,128)} %ids.1, s32[1,4]{1,0:T(1,128)} %counts.1, ...), custom_call_target="tpu_custom_call" | custom-call | tf_op jit(solution)/shard_map/pick/pallas_call | solution.py:76
  1.5 0.7 %collective-permute-start = (bf16[128,256]{1,0:T(8,128)(2,1)S(1)}, bf16[128,256]{1,0:T(8,128)(2,1)S(1)}, u32[]{:S(2)}, u32[]{:S(2)}) collective-permute-start(bf16[128,256]{1,0:T(8,128)(2,1)S(1)} %get-tuple-element.31), channel_id=1, source_target_pairs={{0,1},{1,0},{2,3},{3,2},{4,5},{5,4},{6,7},{7,6},{8,9},{9,8},{10,11... | collective-permute-start | bytes 196616 | tf_op jit(solution)/shard_map/ppermute | solution.py:289
  2.2 1.2 %collective-permute-start.1 = (bf16[128,256]{1,0:T(8,128)(2,1)S(1)}, bf16[128,256]{1,0:T(8,128)(2,1)S(1)}, u32[]{:S(2)}, u32[]{:S(2)}) collective-permute-start(bf16[128,256]{1,0:T(8,128)(2,1)S(1)} %get-tuple-element.32), channel_id=1, source_target_pairs={{0,2},{1,3},{2,0},{3,1},{4,6},{5,7},{6,4},{7,5},{8,10},{9,11},{10,... | collective-permute-start | bytes 196616 | tf_op jit(solution)/shard_map/ppermute | solution.py:289
  3.4 0.5 %collective-permute-start.2 = (bf16[128,256]{1,0:T(8,128)(2,1)S(1)}, bf16[128,256]{1,0:T(8,128)(2,1)S(1)}, u32[]{:S(2)}, u32[]{:S(2)}) collective-permute-start(bf16[128,256]{1,0:T(8,128)(2,1)S(1)} %get-tuple-element.33), channel_id=1, source_target_pairs={{0,3},{1,2},{2,1},{3,0},{4,7},{5,6},{6,5},{7,4},{8,11},{9,10},{10,... | collective-permute-start | bytes 196616 | tf_op jit(solution)/shard_map/ppermute | solution.py:289
  3.9 1.7 %spread.2 = (bf16[1024,1024]{1,0:T(8,128)(2,1)S(1)}, bf16[1024,1024]{1,0:T(8,128)(2,1)S(1)}) custom-call(s32[1,128]{1,0:T(1,128)S(1)} %get-tuple-element.35.slots, s32[1,128]{1,0:T(1,128)S(1)} %get-tuple-element.36.targets, bf16[128,4096]{1,0:T(8,128)(2,1)S(1)} %get-tuple-element.37.weights), custom_call_target="tpu_custom_call" | custom-call | flops 536870912 | bytes 6291456 | tf_op jit(solution)/shard_map/spread/pallas_call | solution.py:149
  5.7 0.0 collective-permute-done.refs_1_
  5.7 0.2 collective-permute-done.1.refs_2_
  5.9 1.6 %collective-permute-done.2.refs_3_ = bf16[128,256]{1,0:T(8,128)(2,1)S(1)} collective-permute-done((bf16[128,256]{1,0:T(8,128)(2,1)S(1)}, bf16[128,256]{1,0:T(8,128)(2,1)S(1)}, u32[]{:S(2)}, u32[]{:S(2)}) %collective-permute-start.2) | collective-permute-done | bytes 65568 | tf_op jit(solution)/shard_map/ppermute | solution.py:289
  7.5 0.9 %edge.2 = (s16[1056,256]{1,0:T(8,128)(2,1)S(1)}, bf16[1024,256]{1,0:T(8,128)(2,1)S(1)}) custom-call(bf16[1024,1024]{1,0:T(8,128)(2,1)S(1)} %get-tuple-element.29.left, bf16[128,256]{1,0:T(8,128)(2,1)S(1)} %get-tuple-element.30.refs_0_, bf16[128,256]{1,0:T(8,128)(2,1)S(1)} %collective-permute-done.refs_1_, ...), custom_call_target="tpu_custom_call" | custom-call | flops 536870912 | bytes 2097152 | tf_op jit(solution)/shard_map/edge/pallas_call | solution.py:202
  8.4 1.3 %collective-permute-start.3 = (s16[1056,256]{1,0:T(8,128)(2,1)S(1)}, s16[1056,256]{1,0:T(8,128)(2,1)S(1)}, u32[]{:S(2)}, u32[]{:S(2)}) collective-permute-start(s16[1056,256]{1,0:T(8,128)(2,1)S(1)} %get-tuple-element.42), channel_id=1, source_target_pairs={{0,31},{1,2},{2,1},{3,4},{4,3},{5,6},{6,5},{7,8},{8,7},{9,10},{10,... | collective-permute-start | bytes 1622024 | tf_op jit(solution)/shard_map/ppermute | solution.py:297
  9.7 0.9 %edge.3 = (s16[528,256]{1,0:T(8,128)(2,1)S(1)}, s16[528,256]{1,0:T(8,128)(2,1)S(1)}) custom-call(bf16[1024,1024]{1,0:T(8,128)(2,1)S(1)} %get-tuple-element.44.left, bf16[1024,256]{1,0:T(8,128)(2,1)S(1)} %get-tuple-element.40.both.refs_0_), custom_call_target="tpu_custom_call" | custom-call | flops 536870912 | bytes 2097152 | tf_op jit(solution)/shard_map/edge/pallas_call | solution.py:202
  10.6 0.3 %collective-permute-start.4 = (s16[528,256]{1,0:T(8,128)(2,1)S(1)}, s16[528,256]{1,0:T(8,128)(2,1)S(1)}, u32[]{:S(2)}, u32[]{:S(2)}) collective-permute-start(s16[528,256]{1,0:T(8,128)(2,1)S(1)} %get-tuple-element.45), channel_id=1, source_target_pairs={{0,1},{1,0},{2,3},{3,2},{4,5},{5,4},{6,7},{7,6},{8,9},{9,8},{10,11... | collective-permute-start | bytes 811016 | tf_op jit(solution)/shard_map/ppermute | solution.py:298
  10.9 0.3 %collective-permute-start.5 = (s16[528,256]{1,0:T(8,128)(2,1)S(1)}, s16[528,256]{1,0:T(8,128)(2,1)S(1)}, u32[]{:S(2)}, u32[]{:S(2)}) collective-permute-start(s16[528,256]{1,0:T(8,128)(2,1)S(1)} %get-tuple-element.46), channel_id=1, source_target_pairs={{0,1},{1,0},{2,3},{3,2},{4,5},{5,4},{6,7},{7,6},{8,9},{9,8},{10,11... | collective-permute-start | bytes 811016 | tf_op jit(solution)/shard_map/ppermute | solution.py:298
  11.2 1.7 %spread.3 = (bf16[1024,1024]{1,0:T(8,128)(2,1)S(1)}, bf16[1024,1024]{1,0:T(8,128)(2,1)S(1)}) custom-call(s32[1,128]{1,0:T(1,128)S(1)} %get-tuple-element.35.slots, s32[1,128]{1,0:T(1,128)S(1)} %get-tuple-element.36.targets, bf16[128,4096]{1,0:T(8,128)(2,1)S(1)} %get-tuple-element.37.weights), custom_call_target="tpu_custom_call" | custom-call | flops 536870912 | bytes 6291456 | tf_op jit(solution)/shard_map/spread/pallas_call | solution.py:149
  12.9 1.3 %middle.1 = (f32[1024,256]{1,0:T(8,128)S(1)}, f32[1024,256]{1,0:T(8,128)S(1)}) custom-call(bf16[1024,1024]{1,0:T(8,128)(2,1)S(1)} %get-tuple-element.38.first, bf16[1024,1024]{1,0:T(8,128)(2,1)S(1)} %get-tuple-element.39.second, bf16[1024,256]{1,0:T(8,128)(2,1)S(1)} %get-tuple-element.40.both.refs_0_), custom_call_target="tpu_custom_call" | custom-call | flops 1073741824 | bytes 4194304 | tf_op jit(solution)/shard_map/middle/pallas_call | solution.py:224
  14.2 0.0 collective-permute-done.4.refs_0_
  14.2 0.0 collective-permute-done.5.refs_1_
  14.2 1.1 %finish.2.refs_1_ = f32[32,64,256]{2,1,0:T(8,128)} custom-call(f32[1024,256]{1,0:T(8,128)S(1)} %get-tuple-element.43.own, s16[528,256]{1,0:T(8,128)(2,1)S(1)} %collective-permute-done.4.refs_0_, s16[528,256]{1,0:T(8,128)(2,1)S(1)} %collective-permute-done.5.refs_1_), custom_call_target="tpu_custom_call" | custom-call | flops 786432 | bytes 2097152 | tf_op jit(solution)/shard_map/finish/pallas_call | solution.py:265
  15.3 7.9 %collective-permute-done.3.refs_0_ = s16[1056,256]{1,0:T(8,128)(2,1)S(1)} collective-permute-done((s16[1056,256]{1,0:T(8,128)(2,1)S(1)}, s16[1056,256]{1,0:T(8,128)(2,1)S(1)}, u32[]{:S(2)}, u32[]{:S(2)}) %collective-permute-start.3) | collective-permute-done | bytes 540704 | tf_op jit(solution)/shard_map/ppermute | solution.py:297
  23.3 1.1 %finish.3 = f32[32,64,256]{2,1,0:T(8,128)} custom-call(f32[1024,256]{1,0:T(8,128)S(1)} %get-tuple-element.41.own, s16[1056,256]{1,0:T(8,128)(2,1)S(1)} %collective-permute-done.3.refs_0_, f32[32,64,256]{2,1,0:T(8,128)} %finish.2.refs_1_), custom_call_target="tpu_custom_call", output_to_operand_aliasing={{}: (2, {})} | custom-call | flops 786432 | bytes 2097152 | tf_op jit(solution)/shard_map/finish/pallas_call | solution.py:265
Async XLA Ops:
  1.5 4.2 %collective-permute-start = (bf16[128,256]{1,0:T(8,128)(2,1)S(1)}, bf16[128,256]{1,0:T(8,128)(2,1)S(1)}, u32[]{:S(2)}, u32[]{:S(2)}) collective-permute-start(bf16[128,256]{1,0:T(8,128)(2,1)S(1)} %get-tuple-element.31), channel_id=1, source_target_pairs={{0,1},{1,0},{2,3},{3,2},{4,5},{5,4},{6,7},{7,6},{8,9},{9,8},{10,11... | collective-permute-start | bytes 196616 | tf_op jit(solution)/shard_map/ppermute | solution.py:289
  2.2 3.7 %collective-permute-start.1 = (bf16[128,256]{1,0:T(8,128)(2,1)S(1)}, bf16[128,256]{1,0:T(8,128)(2,1)S(1)}, u32[]{:S(2)}, u32[]{:S(2)}) collective-permute-start(bf16[128,256]{1,0:T(8,128)(2,1)S(1)} %get-tuple-element.32), channel_id=1, source_target_pairs={{0,2},{1,3},{2,0},{3,1},{4,6},{5,7},{6,4},{7,5},{8,10},{9,11},{10,... | collective-permute-start | bytes 196616 | tf_op jit(solution)/shard_map/ppermute | solution.py:289
  3.4 4.0 %collective-permute-start.2 = (bf16[128,256]{1,0:T(8,128)(2,1)S(1)}, bf16[128,256]{1,0:T(8,128)(2,1)S(1)}, u32[]{:S(2)}, u32[]{:S(2)}) collective-permute-start(bf16[128,256]{1,0:T(8,128)(2,1)S(1)} %get-tuple-element.33), channel_id=1, source_target_pairs={{0,3},{1,2},{2,1},{3,0},{4,7},{5,6},{6,5},{7,4},{8,11},{9,10},{10,... | collective-permute-start | bytes 196616 | tf_op jit(solution)/shard_map/ppermute | solution.py:289
  8.4 14.9 %collective-permute-start.3 = (s16[1056,256]{1,0:T(8,128)(2,1)S(1)}, s16[1056,256]{1,0:T(8,128)(2,1)S(1)}, u32[]{:S(2)}, u32[]{:S(2)}) collective-permute-start(s16[1056,256]{1,0:T(8,128)(2,1)S(1)} %get-tuple-element.42), channel_id=1, source_target_pairs={{0,31},{1,2},{2,1},{3,4},{4,3},{5,6},{6,5},{7,8},{8,7},{9,10},{10,... | collective-permute-start | bytes 1622024 | tf_op jit(solution)/shard_map/ppermute | solution.py:297
  10.6 3.6 %collective-permute-start.4 = (s16[528,256]{1,0:T(8,128)(2,1)S(1)}, s16[528,256]{1,0:T(8,128)(2,1)S(1)}, u32[]{:S(2)}, u32[]{:S(2)}) collective-permute-start(s16[528,256]{1,0:T(8,128)(2,1)S(1)} %get-tuple-element.45), channel_id=1, source_target_pairs={{0,1},{1,0},{2,3},{3,2},{4,5},{5,4},{6,7},{7,6},{8,9},{9,8},{10,11... | collective-permute-start | bytes 811016 | tf_op jit(solution)/shard_map/ppermute | solution.py:298
  10.9 3.3 %collective-permute-start.5 = (s16[528,256]{1,0:T(8,128)(2,1)S(1)}, s16[528,256]{1,0:T(8,128)(2,1)S(1)}, u32[]{:S(2)}, u32[]{:S(2)}) collective-permute-start(s16[528,256]{1,0:T(8,128)(2,1)S(1)} %get-tuple-element.46), channel_id=1, source_target_pairs={{0,1},{1,0},{2,3},{3,2},{4,5},{5,4},{6,7},{7,6},{8,9},{9,8},{10,11... | collective-permute-start | bytes 811016 | tf_op jit(solution)/shard_map/ppermute | solution.py:298

commit v5 on v4

--- a/solution.py
+++ b/solution.py
@@ -13,6 +13,8 @@
 CHUNK = 2 * BLOCK
 ROWS = EB * BLOCK
 GROUP = 32
+EARLY = 2
+SLABS = 4
 WHOLE = (ROWS,)
 PARTS = (ROWS // 2, ROWS // 2)
 FLOOR = 2.0**-110
@@ -46,19 +48,15 @@
 
 
 def pick_kernel(members, capacity, ids, counts, source, *refs):
-    fed, refs = refs[:3], refs[3:]
-    picked, held, refs = refs[:members], refs[members : members + 3], refs[members + 3 :]
-    blocks, id_list, count_list, sems = refs
+    picked, (blocks, id_list, count_list, sems) = refs[:members], refs[members:]
     own = lax.axis_index("blk")
     copies = [
         pltpu.make_async_copy(here, there, sems.at[n])
-        for n, (here, there) in enumerate(
-            zip((ids, counts, source) + fed, (id_list, count_list, blocks) + held)
-        )
+        for n, (here, there) in enumerate(((ids, id_list), (counts, count_list), (source, blocks)))
     ]
     for copy in copies:
         copy.start()
-    for copy in copies[:3]:
+    for copy in copies:
         copy.wait()
     for k in range(members):
         reader = partner(own, k, members)
@@ -66,34 +64,49 @@
             start = pl.multiple_of(id_list[0, reader * capacity + j] * BLOCK, BLOCK)
             live = (j < count_list[0, reader]).astype(jnp.float32).astype(jnp.bfloat16)
             picked[k][j * BLOCK : (j + 1) * BLOCK] = blocks[pl.ds(start, BLOCK)] * live
-    for copy in copies[3:]:
-        copy.wait()
-
-
-def pick(members, capacity, send_ids, send_counts, source, *fed):
+
+
+def in_hbm(*arrays):
+    return [pltpu.with_memory_space_constraint(x, pltpu.HBM) for x in arrays]
+
+
+def pick(members, capacity, send_ids, send_counts, source):
     shape = (capacity * BLOCK, COLS)
-    given = [pltpu.with_memory_space_constraint(x, pltpu.HBM) for x in (send_ids, send_counts, source) + fed]
-    results = pl.pallas_call(
+    return pl.pallas_call(
         functools.partial(pick_kernel, members, capacity),
-        out_shape=[pltpu.VMEM(shape, jnp.bfloat16)] * members + [pltpu.VMEM(x.shape, x.dtype) for x in fed],
-        in_specs=[ANY] * len(given),
-        out_specs=[VMEM] * (members + len(fed)),
+        out_shape=[pltpu.VMEM(shape, jnp.bfloat16)] * members,
+        in_specs=[ANY] * 3,
+        out_specs=[VMEM] * members,
         scratch_shapes=[
             pltpu.VMEM(source.shape, source.dtype),
             pltpu.SMEM(send_ids.shape, jnp.int32),
             pltpu.SMEM(send_counts.shape, jnp.int32),
-            pltpu.SemaphoreType.DMA((len(given),)),
+            pltpu.SemaphoreType.DMA((3,)),
         ],
         compiler_params=params(),
         name="pick",
-    )(*given)
-    return results[:members], results[members:]
-
-
-def spread_kernel(members, capacity, quarters, slots, targets, weights, *outs):
+    )(*in_hbm(send_ids, send_counts, source))
+
+
+def lanes_of(k, members):
+    if k < EARLY:
+        return k * CHUNK, (EARLY + k) * CHUNK
+    return (EARLY + k) * CHUNK, (members + k) * CHUNK
+
+
+def spread_kernel(members, capacity, quarters, *refs):
+    here, outs, (slots, targets, weights, sems) = refs[:3], refs[3:-4], refs[-4:]
+    slab = weights.shape[1] // SLABS
+    copies = [pltpu.make_async_copy(here[n], (slots, targets)[n], sems.at[n]) for n in range(2)]
+    for n in range(SLABS):
+        part = (slice(None), pl.ds(n * slab, slab))
+        copies.append(pltpu.make_async_copy(here[2].at[part], weights.at[part], sems.at[2 + n]))
+    for copy in copies:
+        copy.start()
+    for copy in copies[:2]:
+        copy.wait()
     own = lax.axis_index("blk")
     tiles = weights.shape[0]
-    width = members * CHUNK
     count = len(quarters)
     slot = slots[...]
     sender = slot // capacity
@@ -136,11 +149,14 @@
                 for h in range(2):
                     row = pl.ds(pl.multiple_of((2 * c + h) * EB, EB), EB)
                     part = (slice(top, top + EB), slice(h * CHUNK, (h + 1) * CHUNK))
-                    outs[n][row, k * CHUNK : (k + 1) * CHUNK] = coarse[part]
-                    outs[n][row, width + k * CHUNK : width + (k + 1) * CHUNK] = fine[part]
+                    for lanes, value in zip(lanes_of(k, members), (coarse, fine)):
+                        outs[n][row, lanes : lanes + CHUNK] = value[part]
         return 0
 
-    lax.fori_loop(0, BLOCK // 2, step, 0, unroll=8)
+    each = slab // CHUNK
+    for n in range(SLABS):
+        copies[2 + n].wait()
+        lax.fori_loop(n * each, (n + 1) * each, step, 0, unroll=each)
 
 
 def spread(members, capacity, quarters, slots, targets, weights):
@@ -149,15 +165,21 @@
     return pl.pallas_call(
         functools.partial(spread_kernel, members, capacity, quarters),
         out_shape=[pltpu.VMEM(shape, jnp.bfloat16)] * len(quarters),
-        in_specs=[VMEM] * 3,
+        in_specs=[ANY] * 3,
         out_specs=[VMEM] * len(quarters),
+        scratch_shapes=[
+            pltpu.VMEM(slots.shape, jnp.int32),
+            pltpu.VMEM(targets.shape, jnp.int32),
+            pltpu.VMEM(weights.shape, weights.dtype),
+            pltpu.SemaphoreType.DMA((2 + SLABS,)),
+        ],
         compiler_params=params(),
         cost_estimate=cost(2 * members * EB * len(quarters) * 2 * tiles * 8192, 6 * 2**20),
         name="spread",
-    )(slots, targets, weights)
-
-
-def stack_kernel(blocks, both):
+    )(*in_hbm(slots, targets, weights))
+
+
+def stacked(blocks, both):
     rows = blocks[0].shape[0]
     for half in range(2):
         for k, block in enumerate(blocks):
@@ -165,71 +187,109 @@
             both[start : start + rows] = block[...]
 
 
-def coded(left, first, count, both, message, powers):
-    step = min(count, 256)
-    for start in range(0, count, step):
-        rows = left[first + start : first + start + step]
-        piece = jnp.dot(rows, both[...], preferred_element_type=jnp.float32)
-        for g in range(step // GROUP):
-            rows = piece[g * GROUP : (g + 1) * GROUP]
-            most = jnp.maximum(jnp.max(jnp.abs(rows), axis=0, keepdims=True), FLOOR)
-            power = jnp.floor(jnp.log2(most) + 0.001) + 1.0
-            whole = jnp.round(rows * jnp.exp2(15.0 - power)).astype(jnp.int32)
-            message[start + g * GROUP : start + (g + 1) * GROUP] = whole.astype(jnp.int16)
-            at = start // GROUP + g
-            powers[at : at + 1] = power.astype(jnp.int32)
+def early_kernel(left, *refs):
+    blocks, (sums, both) = refs[:-2], refs[-2:]
+    stacked(blocks, both)
+    sums[...] = jnp.dot(left[:, : both.shape[0]], both[...], preferred_element_type=jnp.float32)
+
+
+def early(left, blocks):
+    depth = 2 * EARLY * CHUNK
+    return pl.pallas_call(
+        early_kernel,
+        out_shape=[pltpu.VMEM((ROWS, COLS), jnp.float32), pltpu.VMEM((depth, COLS), jnp.bfloat16)],
+        in_specs=[VMEM] * (1 + len(blocks)),
+        out_specs=[VMEM] * 2,
+        compiler_params=params(),
+        cost_estimate=cost(2 * ROWS * depth * COLS, 2 * 2**20),
+        name="early",
+    )(left, *blocks)
+
+
+def coded(piece, message, powers):
+    count = piece.shape[0]
+    for g in range(count // GROUP):
+        rows = piece[g * GROUP : (g + 1) * GROUP]
+        most = jnp.maximum(jnp.max(jnp.abs(rows), axis=0, keepdims=True), FLOOR)
+        power = jnp.floor(jnp.log2(most) + 0.001) + 1.0
+        whole = jnp.round(rows * jnp.exp2(15.0 - power)).astype(jnp.int32)
+        message[g * GROUP : (g + 1) * GROUP] = whole.astype(jnp.int16)
+        powers[g : g + 1] = power.astype(jnp.int32)
     message[count : count + count // GROUP] = powers[...].astype(jnp.int16)
 
 
-def edge_kernel(parts, blocks, left, *refs):
-    received, refs = refs[:blocks], refs[blocks:]
-    messages, refs = refs[: len(parts)], refs[len(parts) :]
-    both, powers = refs[0], refs[1:]
-    if blocks > 1:
-        stack_kernel(received, both)
-    else:
-        both, powers = received[0], refs
-    first = 0
-    for count, message, power in zip(parts, messages, powers):
-        coded(left, first, count, both, message, power)
-        first += count
-
-
-def edge(parts, left, *right):
-    out_shape = [pltpu.VMEM((count + count // GROUP, COLS), jnp.int16) for count in parts]
-    if len(right) > 1:
-        out_shape.append(pltpu.VMEM((left.shape[1], COLS), jnp.bfloat16))
-    return pl.pallas_call(
-        functools.partial(edge_kernel, parts, len(right)),
-        out_shape=out_shape,
-        in_specs=[VMEM] * (1 + len(right)),
-        out_specs=[VMEM] * len(out_shape),
-        scratch_shapes=[pltpu.VMEM((count // GROUP, COLS), jnp.int32) for count in parts],
+def product(left, first, later):
+    both = jnp.concatenate([first[...], later[...]], axis=0)
+    return jnp.dot(left, both, preferred_element_type=jnp.float32)
+
+
+def across_kernel(left, sums, *refs):
+    blocks, (message, both, powers) = refs[:-3], refs[-3:]
+    stacked(blocks, both)
+    start = left.shape[1] - both.shape[0]
+    piece = jnp.dot(left[:, start:], both[...], preferred_element_type=jnp.float32)
+    coded(sums[...] + piece, message, powers)
+
+
+def message_of(count):
+    return pltpu.VMEM((count + count // GROUP, COLS), jnp.int16)
+
+
+def powers_of(count):
+    return pltpu.VMEM((count // GROUP, COLS), jnp.int32)
+
+
+def across_edge(left, sums, blocks):
+    depth = 2 * len(blocks) * CHUNK
+    return pl.pallas_call(
+        across_kernel,
+        out_shape=[message_of(ROWS), pltpu.VMEM((depth, COLS), jnp.bfloat16)],
+        in_specs=[VMEM] * (2 + len(blocks)),
+        out_specs=[VMEM] * 2,
+        scratch_shapes=[powers_of(ROWS)],
+        compiler_params=params(),
+        cost_estimate=cost(2 * ROWS * depth * COLS, 2 * 2**20),
+        name="across",
+    )(left, sums, *blocks)
+
+
+def chip_kernel(parts, left, first, later, *refs):
+    start = 0
+    for count, message, powers in zip(parts, refs[: len(parts)], refs[len(parts) :]):
+        coded(product(left[start : start + count], first, later), message, powers)
+        start += count
+
+
+def chip_edge(parts, left, first, later):
+    return pl.pallas_call(
+        functools.partial(chip_kernel, parts),
+        out_shape=[message_of(count) for count in parts],
+        in_specs=[VMEM] * 3,
+        out_specs=[VMEM] * len(parts),
+        scratch_shapes=[powers_of(count) for count in parts],
         compiler_params=params(),
         cost_estimate=cost(2 * ROWS * left.shape[1] * COLS, 2 * 2**20),
-        name="edge",
-    )(left, *right)
-
-
-def middle_kernel(first, second, both, *outs):
+        name="chip",
+    )(left, first, later)
+
+
+def middle_kernel(left_0, left_1, first, later, *outs):
     step = 256
-    for left, out in zip((first, second), outs):
+    for left, out in zip((left_0, left_1), outs):
         for start in range(0, ROWS, step):
-            out[start : start + step] = jnp.dot(
-                left[start : start + step], both[...], preferred_element_type=jnp.float32
-            )
-
-
-def middle(first, second, both):
+            out[start : start + step] = product(left[start : start + step], first, later)
+
+
+def middle(left_0, left_1, first, later):
     return pl.pallas_call(
         middle_kernel,
         out_shape=[pltpu.VMEM((ROWS, COLS), jnp.float32)] * 2,
-        in_specs=[VMEM] * 3,
+        in_specs=[VMEM] * 4,
         out_specs=[VMEM] * 2,
         compiler_params=params(),
-        cost_estimate=cost(4 * ROWS * first.shape[1] * COLS, 4 * 2**20),
+        cost_estimate=cost(4 * ROWS * left_0.shape[1] * COLS, 4 * 2**20),
         name="middle",
-    )(first, second, both)
+    )(left_0, left_1, first, later)
 
 
 def finish_kernel(across, parts, own, *refs):
@@ -301,17 +361,18 @@
 def body(source, send_ids, send_counts, tile_slot, tile_target, tile_weights):
     members = lax.axis_size("blk")
     capacity = send_ids.shape[1] // members
-    picked, tiles = pick(
-        members, capacity, send_ids, send_counts, source, tile_slot, tile_target, tile_weights
-    )
-    blocks = [picked[0]] + [exchanged(picked[k], k) for k in range(1, members)]
+    picked = pick(members, capacity, send_ids, send_counts, source)
+    later_blocks = [exchanged(picked[k], k) for k in range(EARLY, members)]
+    early_blocks = [picked[0]] + [exchanged(picked[k], k) for k in range(1, EARLY)]
+    tiles = (tile_slot, tile_target, tile_weights)
     left_across, left_chip = spread(members, capacity, ((0, 3), (3, 0)), *tiles)
-    message_across, both = edge(WHOLE, left_across, *blocks)
+    sums, first = early(left_across, early_blocks)
+    message_across, later = across_edge(left_across, sums, later_blocks)
     message_across = ring_swap(message_across, True)
-    messages_chip = [ring_swap(message, False) for message in edge(PARTS, left_chip, both)]
-    tiles, both = lax.optimization_barrier((tiles, both))
+    messages_chip = [ring_swap(message, False) for message in chip_edge(PARTS, left_chip, first, later)]
+    tiles, later = lax.optimization_barrier((tiles, later))
     own_left = spread(members, capacity, ((1, 2), (2, 1)), *tiles)
-    own_across, own_chip = middle(*own_left, both)
+    own_across, own_chip = middle(*own_left, first, later)
     out = finish(False, PARTS, own_chip, messages_chip)
     out = finish(True, WHOLE, own_across, [message_across], out)
     return out.reshape(2 * ROWS, COLS)

time: 24.8 us -> 24.1 us (0.972)
  waiting for transfers between devices: 9.75 us -> 7.31 us
  Pallas kernels: 10.2 us -> 11.9 us
    pallas_call x2, Pallas kernels: 3.44 us -> 5.45 us  [spread(): pl.pallas_call(functools.partial(spread_kernel, members, capacity, quarte...]
    ppermute x3, waiting for transfers between devices: 1.83 us -> 0.37 us  [exchanged(): return lax.ppermute(shard, 'blk', [(i, i ^ k) for i in range(members)])]
    ppermute x1, waiting for transfers between devices: 7.92 us -> 6.93 us  [ring_swap(): lax.ppermute(shard, axes, [(i, (i + (1 if i % 2 else -1)) % count) for i...]
    pallas_call x1, Pallas kernels: 1.47 us -> 1.1 us  [pick(): pl.pallas_call(functools.partial(pick_kernel, members, capacity), out_sha...]
    pallas_call x2 -> x3, Pallas kernels: 1.78 us -> 1.85 us  [the longest x1 0.87 us: chip_edge(): pl.pallas_call(functools.partial(chip_kernel, parts), out_shape=[message_...]
  transfers between devices with their start and end apart: 6 -> 6, of which waited for: 3 -> 2; matrix products, arithmetic and copies ran while one was open for 0% -> 0% of each run, Pallas kernels for 27% -> 38%
where the time goes in v5:
time: 24.1 us; the launch traced here: 23.7 us
  Pallas kernels  11.9 us (49%)
  waiting for transfers between devices  7.31 us (30%)
  starting transfers between devices  4.39 us (18%)
    ppermute x1, waiting for transfers between devices, ring_swap(): lax.ppermute(shard, axes, [(i, (i + (1 if i % 2 else -1)) % count) for i...  6.93 us
    pallas_call x2, Pallas kernels, spread(): pl.pallas_call(functools.partial(spread_kernel, members, capacity, quarte...  5.45 us
    ppermute x3, starting transfers between devices, exchanged(): return lax.ppermute(shard, 'blk', [(i, i ^ k) for i in range(members)])  2.45 us
    pallas_call x2, Pallas kernels, finish(): pl.pallas_call(functools.partial(finish_kernel, across, parts), out_shape...  2.23 us
    ppermute x1, starting transfers between devices, ring_swap(): lax.ppermute(shard, axes, [(i, (i + (1 if i % 2 else -1)) % count) for i...  1.36 us
    pallas_call x1, Pallas kernels, middle(): pl.pallas_call(middle_kernel, out_shape=[pltpu.VMEM((ROWS, COLS), jnp.flo...  1.25 us
    pallas_call x1, Pallas kernels, pick(): pl.pallas_call(functools.partial(pick_kernel, members, capacity), out_sha...  1.1 us
    pallas_call x1, Pallas kernels, chip_edge(): pl.pallas_call(functools.partial(chip_kernel, parts), out_shape=[message_...  0.87 us
  transfers between devices with their start and end apart: 6, of which 2 were waited for; matrix products, arithmetic and copies ran while one was open for 0% of the time, Pallas kernels for 38%

profile of v5, /device:TPU:5, one launch (start us, length us, event | category | flops | bytes accessed | tf_op | source)
XLA Modules:
  0.0 23.7 jit_solution(5531009499916125505)
XLA Ops:
  0.0 1.1 %pick.1 = (bf16[128,256]{1,0:T(8,128)(2,1)S(1)}, bf16[128,256]{1,0:T(8,128)(2,1)S(1)}, bf16[128,256]{1,0:T(8,128)(2,1)S(1)}, bf16[128,256]{1,0:T(8,128)(2,1)S(1)}) custom-call(s32[1,8]{1,0:T(1,128)} %ids.1, s32[1,4]{1,0:T(1,128)} %counts.1, bf16[1024,256]{1,0:T(8,128)(2,1)} %source.1), custom_call_target="tpu_custom_call" | custom-call | tf_op jit(solution)/shard_map/pick/pallas_call | solution.py:75
  1.1 0.7 %collective-permute-start = (bf16[128,256]{1,0:T(8,128)(2,1)S(1)}, bf16[128,256]{1,0:T(8,128)(2,1)S(1)}, u32[]{:S(2)}, u32[]{:S(2)}) collective-permute-start(bf16[128,256]{1,0:T(8,128)(2,1)S(1)} %get-tuple-element.27), channel_id=1, source_target_pairs={{0,1},{1,0},{2,3},{3,2},{4,5},{5,4},{6,7},{7,6},{8,9},{9,8},{10,11... | collective-permute-start | bytes 196616 | tf_op jit(solution)/shard_map/ppermute | solution.py:349
  1.9 1.2 %collective-permute-start.1 = (bf16[128,256]{1,0:T(8,128)(2,1)S(1)}, bf16[128,256]{1,0:T(8,128)(2,1)S(1)}, u32[]{:S(2)}, u32[]{:S(2)}) collective-permute-start(bf16[128,256]{1,0:T(8,128)(2,1)S(1)} %get-tuple-element.29), channel_id=1, source_target_pairs={{0,2},{1,3},{2,0},{3,1},{4,6},{5,7},{6,4},{7,5},{8,10},{9,11},{10,... | collective-permute-start | bytes 196616 | tf_op jit(solution)/shard_map/ppermute | solution.py:349
  3.1 0.5 %collective-permute-start.2 = (bf16[128,256]{1,0:T(8,128)(2,1)S(1)}, bf16[128,256]{1,0:T(8,128)(2,1)S(1)}, u32[]{:S(2)}, u32[]{:S(2)}) collective-permute-start(bf16[128,256]{1,0:T(8,128)(2,1)S(1)} %get-tuple-element.30), channel_id=1, source_target_pairs={{0,3},{1,2},{2,1},{3,0},{4,7},{5,6},{6,5},{7,4},{8,11},{9,10},{10,... | collective-permute-start | bytes 196616 | tf_op jit(solution)/shard_map/ppermute | solution.py:349
  3.6 2.7 %spread.2 = (bf16[1024,1024]{1,0:T(8,128)(2,1)S(1)}, bf16[1024,1024]{1,0:T(8,128)(2,1)S(1)}) custom-call(s32[1,128]{1,0:T(1,128)} %refs_0_.2, s32[1,128]{1,0:T(1,128)} %refs_1_.2, bf16[128,4096]{1,0:T(8,128)(2,1)} %refs_2_.2), custom_call_target="tpu_custom_call" | custom-call | flops 536870912 | bytes 6291456 | tf_op jit(solution)/shard_map/spread/pallas_call | solution.py:165
  6.3 0.0 collective-permute-done.refs_1_
  6.3 0.4 %early.1 = (f32[1024,256]{1,0:T(8,128)S(1)}, bf16[512,256]{1,0:T(8,128)(2,1)S(1)}) custom-call(bf16[1024,1024]{1,0:T(8,128)(2,1)S(1)} %get-tuple-element.25.left, bf16[128,256]{1,0:T(8,128)(2,1)S(1)} %get-tuple-element.26.refs_0_, bf16[128,256]{1,0:T(8,128)(2,1)S(1)} %collective-permute-done.refs_1_), custom_call_target="tpu_custom_call" | custom-call | flops 268435456 | bytes 2097152 | tf_op jit(solution)/shard_map/early/pallas_call | solution.py:198
  6.7 0.0 collective-permute-done.1.refs_0_
  6.8 0.4 %collective-permute-done.2.refs_1_ = bf16[128,256]{1,0:T(8,128)(2,1)S(1)} collective-permute-done((bf16[128,256]{1,0:T(8,128)(2,1)S(1)}, bf16[128,256]{1,0:T(8,128)(2,1)S(1)}, u32[]{:S(2)}, u32[]{:S(2)}) %collective-permute-start.2) | collective-permute-done | bytes 65568 | tf_op jit(solution)/shard_map/ppermute | solution.py:349
  7.1 0.5 %across.1 = (s16[1056,256]{1,0:T(8,128)(2,1)S(1)}, bf16[512,256]{1,0:T(8,128)(2,1)S(1)}) custom-call(bf16[1024,1024]{1,0:T(8,128)(2,1)S(1)} %get-tuple-element.25.left, f32[1024,256]{1,0:T(8,128)S(1)} %get-tuple-element.28.sums, bf16[128,256]{1,0:T(8,128)(2,1)S(1)} %collective-permute-done.1.refs_0_, bf16[128,256]{1,0:T(8,128)(2,1)S(1)} %collective-permute-done.2.refs_1_), custom_call_target="tpu_custom_call" | custom-call | flops 268435456 | bytes 2097152 | tf_op jit(solution)/shard_map/across/pallas_call | solution.py:244
  7.7 1.4 %collective-permute-start.3 = (s16[1056,256]{1,0:T(8,128)(2,1)S(1)}, s16[1056,256]{1,0:T(8,128)(2,1)S(1)}, u32[]{:S(2)}, u32[]{:S(2)}) collective-permute-start(s16[1056,256]{1,0:T(8,128)(2,1)S(1)} %get-tuple-element.40), channel_id=1, source_target_pairs={{0,31},{1,2},{2,1},{3,4},{4,3},{5,6},{6,5},{7,8},{8,7},{9,10},{10,... | collective-permute-start | bytes 1622024 | tf_op jit(solution)/shard_map/ppermute | solution.py:357
  9.0 0.9 %chip.1 = (s16[528,256]{1,0:T(8,128)(2,1)S(1)}, s16[528,256]{1,0:T(8,128)(2,1)S(1)}) custom-call(bf16[1024,1024]{1,0:T(8,128)(2,1)S(1)} %get-tuple-element.42.left, bf16[512,256]{1,0:T(8,128)(2,1)S(1)} %get-tuple-element.37.first, bf16[512,256]{1,0:T(8,128)(2,1)S(1)} %get-tuple-element.38.later), custom_call_target="tpu_custom_call" | custom-call | flops 536870912 | bytes 2097152 | tf_op jit(solution)/shard_map/chip/pallas_call | solution.py:264
  9.9 0.3 %collective-permute-start.4 = (s16[528,256]{1,0:T(8,128)(2,1)S(1)}, s16[528,256]{1,0:T(8,128)(2,1)S(1)}, u32[]{:S(2)}, u32[]{:S(2)}) collective-permute-start(s16[528,256]{1,0:T(8,128)(2,1)S(1)} %get-tuple-element.43), channel_id=1, source_target_pairs={{0,1},{1,0},{2,3},{3,2},{4,5},{5,4},{6,7},{7,6},{8,9},{9,8},{10,11... | collective-permute-start | bytes 811016 | tf_op jit(solution)/shard_map/ppermute | solution.py:358
  10.2 0.3 %collective-permute-start.5 = (s16[528,256]{1,0:T(8,128)(2,1)S(1)}, s16[528,256]{1,0:T(8,128)(2,1)S(1)}, u32[]{:S(2)}, u32[]{:S(2)}) collective-permute-start(s16[528,256]{1,0:T(8,128)(2,1)S(1)} %get-tuple-element.44), channel_id=1, source_target_pairs={{0,1},{1,0},{2,3},{3,2},{4,5},{5,4},{6,7},{7,6},{8,9},{9,8},{10,11... | collective-permute-start | bytes 811016 | tf_op jit(solution)/shard_map/ppermute | solution.py:358
  10.5 2.7 %spread.3 = (bf16[1024,1024]{1,0:T(8,128)(2,1)S(1)}, bf16[1024,1024]{1,0:T(8,128)(2,1)S(1)}) custom-call(s32[1,128]{1,0:T(1,128)} %refs_0_.2, s32[1,128]{1,0:T(1,128)} %refs_1_.2, bf16[128,4096]{1,0:T(8,128)(2,1)} %refs_2_.2), custom_call_target="tpu_custom_call" | custom-call | flops 536870912 | bytes 6291456 | tf_op jit(solution)/shard_map/spread/pallas_call | solution.py:165
  13.2 1.2 %middle.1 = (f32[1024,256]{1,0:T(8,128)S(1)}, f32[1024,256]{1,0:T(8,128)S(1)}) custom-call(bf16[1024,1024]{1,0:T(8,128)(2,1)S(1)} %get-tuple-element.35.left_0, bf16[1024,1024]{1,0:T(8,128)(2,1)S(1)} %get-tuple-element.36.left_1, bf16[512,256]{1,0:T(8,128)(2,1)S(1)} %get-tuple-element.37.first, bf16[512,256]{1,0:T(8,128)(2,1)S(1)} %get-tuple-element.38.later), custom_call_target="tpu_custom_call" | custom-call | flops 1073741824 | bytes 4194304 | tf_op jit(solution)/shard_map/middle/pallas_call | solution.py:284
  14.5 0.0 collective-permute-done.4.refs_0_
  14.5 0.0 collective-permute-done.5.refs_1_
  14.5 1.1 %finish.2.refs_1_ = f32[32,64,256]{2,1,0:T(8,128)} custom-call(f32[1024,256]{1,0:T(8,128)S(1)} %get-tuple-element.41.own, s16[528,256]{1,0:T(8,128)(2,1)S(1)} %collective-permute-done.4.refs_0_, s16[528,256]{1,0:T(8,128)(2,1)S(1)} %collective-permute-done.5.refs_1_), custom_call_target="tpu_custom_call" | custom-call | flops 786432 | bytes 2097152 | tf_op jit(solution)/shard_map/finish/pallas_call | solution.py:325
  15.6 6.9 %collective-permute-done.3.refs_0_ = s16[1056,256]{1,0:T(8,128)(2,1)S(1)} collective-permute-done((s16[1056,256]{1,0:T(8,128)(2,1)S(1)}, s16[1056,256]{1,0:T(8,128)(2,1)S(1)}, u32[]{:S(2)}, u32[]{:S(2)}) %collective-permute-start.3) | collective-permute-done | bytes 540704 | tf_op jit(solution)/shard_map/ppermute | solution.py:357
  22.5 1.1 %finish.3 = f32[32,64,256]{2,1,0:T(8,128)} custom-call(f32[1024,256]{1,0:T(8,128)S(1)} %get-tuple-element.39.own, s16[1056,256]{1,0:T(8,128)(2,1)S(1)} %collective-permute-done.3.refs_0_, f32[32,64,256]{2,1,0:T(8,128)} %finish.2.refs_1_), custom_call_target="tpu_custom_call", output_to_operand_aliasing={{}: (2, {})} | custom-call | flops 786432 | bytes 2097152 | tf_op jit(solution)/shard_map/finish/pallas_call | solution.py:325
Async XLA Ops:
  1.1 5.2 %collective-permute-start = (bf16[128,256]{1,0:T(8,128)(2,1)S(1)}, bf16[128,256]{1,0:T(8,128)(2,1)S(1)}, u32[]{:S(2)}, u32[]{:S(2)}) collective-permute-start(bf16[128,256]{1,0:T(8,128)(2,1)S(1)} %get-tuple-element.27), channel_id=1, source_target_pairs={{0,1},{1,0},{2,3},{3,2},{4,5},{5,4},{6,7},{7,6},{8,9},{9,8},{10,11... | collective-permute-start | bytes 196616 | tf_op jit(solution)/shard_map/ppermute | solution.py:349
  1.9 4.9 %collective-permute-start.1 = (bf16[128,256]{1,0:T(8,128)(2,1)S(1)}, bf16[128,256]{1,0:T(8,128)(2,1)S(1)}, u32[]{:S(2)}, u32[]{:S(2)}) collective-permute-start(bf16[128,256]{1,0:T(8,128)(2,1)S(1)} %get-tuple-element.29), channel_id=1, source_target_pairs={{0,2},{1,3},{2,0},{3,1},{4,6},{5,7},{6,4},{7,5},{8,10},{9,11},{10,... | collective-permute-start | bytes 196616 | tf_op jit(solution)/shard_map/ppermute | solution.py:349
  3.1 4.0 %collective-permute-start.2 = (bf16[128,256]{1,0:T(8,128)(2,1)S(1)}, bf16[128,256]{1,0:T(8,128)(2,1)S(1)}, u32[]{:S(2)}, u32[]{:S(2)}) collective-permute-start(bf16[128,256]{1,0:T(8,128)(2,1)S(1)} %get-tuple-element.30), channel_id=1, source_target_pairs={{0,3},{1,2},{2,1},{3,0},{4,7},{5,6},{6,5},{7,4},{8,11},{9,10},{10,... | collective-permute-start | bytes 196616 | tf_op jit(solution)/shard_map/ppermute | solution.py:349
  7.7 14.9 %collective-permute-start.3 = (s16[1056,256]{1,0:T(8,128)(2,1)S(1)}, s16[1056,256]{1,0:T(8,128)(2,1)S(1)}, u32[]{:S(2)}, u32[]{:S(2)}) collective-permute-start(s16[1056,256]{1,0:T(8,128)(2,1)S(1)} %get-tuple-element.40), channel_id=1, source_target_pairs={{0,31},{1,2},{2,1},{3,4},{4,3},{5,6},{6,5},{7,8},{8,7},{9,10},{10,... | collective-permute-start | bytes 1622024 | tf_op jit(solution)/shard_map/ppermute | solution.py:357
  9.9 4.6 %collective-permute-start.4 = (s16[528,256]{1,0:T(8,128)(2,1)S(1)}, s16[528,256]{1,0:T(8,128)(2,1)S(1)}, u32[]{:S(2)}, u32[]{:S(2)}) collective-permute-start(s16[528,256]{1,0:T(8,128)(2,1)S(1)} %get-tuple-element.43), channel_id=1, source_target_pairs={{0,1},{1,0},{2,3},{3,2},{4,5},{5,4},{6,7},{7,6},{8,9},{9,8},{10,11... | collective-permute-start | bytes 811016 | tf_op jit(solution)/shard_map/ppermute | solution.py:358
  10.2 4.3 %collective-permute-start.5 = (s16[528,256]{1,0:T(8,128)(2,1)S(1)}, s16[528,256]{1,0:T(8,128)(2,1)S(1)}, u32[]{:S(2)}, u32[]{:S(2)}) collective-permute-start(s16[528,256]{1,0:T(8,128)(2,1)S(1)} %get-tuple-element.44), channel_id=1, source_target_pairs={{0,1},{1,0},{2,3},{3,2},{4,5},{5,4},{6,7},{7,6},{8,9},{9,8},{10,11... | collective-permute-start | bytes 811016 | tf_op jit(solution)/shard_map/ppermute | solution.py:358

commit v6 on v5

--- a/solution.py
+++ b/solution.py
@@ -12,9 +12,10 @@
 EB = 16
 CHUNK = 2 * BLOCK
 ROWS = EB * BLOCK
-GROUP = 32
+GROUP = 64
 EARLY = 2
 SLABS = 4
+RING = ("grp", "blk")
 WHOLE = (ROWS,)
 PARTS = (ROWS // 2, ROWS // 2)
 FLOOR = 2.0**-110
@@ -48,7 +49,7 @@
 
 
 def pick_kernel(members, capacity, ids, counts, source, *refs):
-    picked, (blocks, id_list, count_list, sems) = refs[:members], refs[members:]
+    picked, (blocks, id_list, count_list, sems) = list(refs[:-4]), refs[-4:]
     own = lax.axis_index("blk")
     copies = [
         pltpu.make_async_copy(here, there, sems.at[n])
@@ -58,12 +59,17 @@
         copy.start()
     for copy in copies:
         copy.wait()
+    at = 0
     for k in range(members):
         reader = partner(own, k, members)
         for j in range(capacity):
             start = pl.multiple_of(id_list[0, reader * capacity + j] * BLOCK, BLOCK)
             live = (j < count_list[0, reader]).astype(jnp.float32).astype(jnp.bfloat16)
-            picked[k][j * BLOCK : (j + 1) * BLOCK] = blocks[pl.ds(start, BLOCK)] * live
+            if at == picked[0].shape[0]:
+                picked.pop(0)
+                at = 0
+            picked[0][at : at + BLOCK] = blocks[pl.ds(start, BLOCK)] * live
+            at += BLOCK
 
 
 def in_hbm(*arrays):
@@ -71,12 +77,14 @@
 
 
 def pick(members, capacity, send_ids, send_counts, source):
-    shape = (capacity * BLOCK, COLS)
+    whole = pltpu.VMEM((capacity * BLOCK, COLS), jnp.bfloat16)
+    single = pltpu.VMEM((BLOCK, COLS), jnp.bfloat16)
+    out_shape = [whole] + [single] * (EARLY - 1) * capacity + [whole] * (members - EARLY)
     return pl.pallas_call(
         functools.partial(pick_kernel, members, capacity),
-        out_shape=[pltpu.VMEM(shape, jnp.bfloat16)] * members,
+        out_shape=out_shape,
         in_specs=[ANY] * 3,
-        out_specs=[VMEM] * members,
+        out_specs=[VMEM] * len(out_shape),
         scratch_shapes=[
             pltpu.VMEM(source.shape, source.dtype),
             pltpu.SMEM(send_ids.shape, jnp.int32),
@@ -180,11 +188,10 @@
 
 
 def stacked(blocks, both):
-    rows = blocks[0].shape[0]
-    for half in range(2):
-        for k, block in enumerate(blocks):
-            start = (half * len(blocks) + k) * rows
-            both[start : start + rows] = block[...]
+    start = 0
+    for block in 2 * blocks:
+        both[start : start + block.shape[0]] = block[...]
+        start += block.shape[0]
 
 
 def early_kernel(left, *refs):
@@ -201,13 +208,15 @@
         in_specs=[VMEM] * (1 + len(blocks)),
         out_specs=[VMEM] * 2,
         compiler_params=params(),
-        cost_estimate=cost(2 * ROWS * depth * COLS, 2 * 2**20),
+        cost_estimate=cost(0, 2**10),
         name="early",
     )(left, *blocks)
 
 
 def coded(piece, message, powers):
     count = piece.shape[0]
+    if count // GROUP < powers.shape[0]:
+        powers[...] = jnp.zeros_like(powers)
     for g in range(count // GROUP):
         rows = piece[g * GROUP : (g + 1) * GROUP]
         most = jnp.maximum(jnp.max(jnp.abs(rows), axis=0, keepdims=True), FLOOR)
@@ -215,7 +224,7 @@
         whole = jnp.round(rows * jnp.exp2(15.0 - power)).astype(jnp.int32)
         message[g * GROUP : (g + 1) * GROUP] = whole.astype(jnp.int16)
         powers[g : g + 1] = power.astype(jnp.int32)
-    message[count : count + count // GROUP] = powers[...].astype(jnp.int16)
+    message[count : count + powers.shape[0]] = powers[...].astype(jnp.int16)
 
 
 def product(left, first, later):
@@ -223,33 +232,47 @@
     return jnp.dot(left, both, preferred_element_type=jnp.float32)
 
 
-def across_kernel(left, sums, *refs):
-    blocks, (message, both, powers) = refs[:-3], refs[-3:]
-    stacked(blocks, both)
-    start = left.shape[1] - both.shape[0]
-    piece = jnp.dot(left[:, start:], both[...], preferred_element_type=jnp.float32)
-    coded(sums[...] + piece, message, powers)
+def send_kernel(odd, left, sums, *refs):
+    blocks, message, refs = refs[: -3 if odd else -2], refs[-3 if odd else -2], refs[-2 if odd else -1 :]
+    if odd:
+        both, powers = refs
+        stacked(blocks, both)
+    else:
+        both, powers = blocks[0], refs[0]
+
+    @pl.when(parity() == (1 if odd else 0))
+    def _():
+        start = left.shape[1] - both.shape[0]
+        piece = jnp.dot(left[:, start:], both[...], preferred_element_type=jnp.float32)
+        coded(sums[...] + piece, message, powers)
+
+
+def scales(count):
+    return max(count // GROUP, 16)
 
 
 def message_of(count):
-    return pltpu.VMEM((count + count // GROUP, COLS), jnp.int16)
+    return pltpu.VMEM((count + scales(count), COLS), jnp.int16)
 
 
 def powers_of(count):
-    return pltpu.VMEM((count // GROUP, COLS), jnp.int32)
-
-
-def across_edge(left, sums, blocks):
-    depth = 2 * len(blocks) * CHUNK
-    return pl.pallas_call(
-        across_kernel,
-        out_shape=[message_of(ROWS), pltpu.VMEM((depth, COLS), jnp.bfloat16)],
+    return pltpu.VMEM((scales(count), COLS), jnp.int32)
+
+
+def send_edge(odd, left, sums, *blocks):
+    depth = 2 * sum(block.shape[0] for block in blocks) if odd else blocks[0].shape[0]
+    out_shape = [message_of(ROWS)]
+    if odd:
+        out_shape.append(pltpu.VMEM((depth, COLS), jnp.bfloat16))
+    return pl.pallas_call(
+        functools.partial(send_kernel, odd),
+        out_shape=out_shape,
         in_specs=[VMEM] * (2 + len(blocks)),
-        out_specs=[VMEM] * 2,
+        out_specs=[VMEM] * len(out_shape),
         scratch_shapes=[powers_of(ROWS)],
         compiler_params=params(),
         cost_estimate=cost(2 * ROWS * depth * COLS, 2 * 2**20),
-        name="across",
+        name="send_odd" if odd else "send_even",
     )(left, sums, *blocks)
 
 
@@ -292,9 +315,7 @@
     )(left_0, left_1, first, later)
 
 
-def finish_kernel(across, parts, own, *refs):
-    messages, (out, rows, sems) = refs[: len(parts)], refs[-3:]
-    half = parity() if across else 1 - parity()
+def finish_half(half, parts, own, messages, out, rows, sems):
     pitch = BLOCK + 8
     targets = rows.reshape(COLS // 128, EB, pitch, 128)
     some = EB // 2
@@ -302,7 +323,7 @@
     for first in range(0, EB, some):
         i = 0
         for count, message in zip(parts, messages):
-            scale = jnp.exp2(message[count : count + count // GROUP].astype(jnp.float32) - 15.0)
+            scale = jnp.exp2(message[count : count + scales(count)].astype(jnp.float32) - 15.0)
             for at in range(0, count, EB):
                 g = at // GROUP
                 value = message[at : at + EB].astype(jnp.float32)[first : first + some]
@@ -320,10 +341,21 @@
         copy.wait()
 
 
-def finish(across, parts, own, messages, out=None):
+def finish_kernel(role, parts, own, *refs):
+    messages, rest = refs[: len(parts)], refs[-3:]
+    if role is None:
+        finish_half(1 - parity(), parts, own, messages, *rest)
+        return
+
+    @pl.when(parity() == role)
+    def _():
+        finish_half(role, parts, own, messages, *rest)
+
+
+def finish(role, parts, own, messages, out=None):
     given = [] if out is None else [out]
     return pl.pallas_call(
-        functools.partial(finish_kernel, across, parts),
+        functools.partial(finish_kernel, role, parts),
         out_shape=jax.ShapeDtypeStruct((2 * EB, BLOCK, COLS), jnp.float32),
         in_specs=[VMEM] * (1 + len(parts)) + [ANY] * len(given),
         out_specs=ANY,
@@ -350,31 +382,37 @@
     return passed_along(shard, "blk", k)
 
 
-def ring_swap(shard, across):
-    axes = ("grp", "blk")
-    count = lax.axis_size(axes)
-    if across:
-        return lax.ppermute(shard, axes, [(i, (i + (1 if i % 2 else -1)) % count) for i in range(count)])
-    return lax.ppermute(shard, axes, [(i, i ^ 1) for i in range(count)])
+def ring_pairs():
+    count = lax.axis_size(RING)
+    odd = [(i, (i + 1) % count) for i in range(1, count, 2)]
+    return odd, [(there, here) for here, there in odd]
+
+
+def chip_swap(shard):
+    count = lax.axis_size(RING)
+    return lax.ppermute(shard, RING, [(i, i ^ 1) for i in range(count)])
 
 
 def body(source, send_ids, send_counts, tile_slot, tile_target, tile_weights):
     members = lax.axis_size("blk")
     capacity = send_ids.shape[1] // members
     picked = pick(members, capacity, send_ids, send_counts, source)
-    later_blocks = [exchanged(picked[k], k) for k in range(EARLY, members)]
-    early_blocks = [picked[0]] + [exchanged(picked[k], k) for k in range(1, EARLY)]
+    later_blocks = [exchanged(picked[k - members], k) for k in range(EARLY, members)]
+    early_blocks = [picked[0]] + [exchanged(picked[1 + n], 1 + n // capacity) for n in range((EARLY - 1) * capacity)]
     tiles = (tile_slot, tile_target, tile_weights)
     left_across, left_chip = spread(members, capacity, ((0, 3), (3, 0)), *tiles)
     sums, first = early(left_across, early_blocks)
-    message_across, later = across_edge(left_across, sums, later_blocks)
-    message_across = ring_swap(message_across, True)
-    messages_chip = [ring_swap(message, False) for message in chip_edge(PARTS, left_chip, first, later)]
+    from_odd, from_even = ring_pairs()
+    message_odd, later = send_edge(True, left_across, sums, *later_blocks)
+    message_odd = lax.ppermute(message_odd, RING, from_odd)
+    message_even = lax.ppermute(send_edge(False, left_across, sums, later)[0], RING, from_even)
+    messages_chip = [chip_swap(message) for message in chip_edge(PARTS, left_chip, first, later)]
     tiles, later = lax.optimization_barrier((tiles, later))
     own_left = spread(members, capacity, ((1, 2), (2, 1)), *tiles)
     own_across, own_chip = middle(*own_left, first, later)
-    out = finish(False, PARTS, own_chip, messages_chip)
-    out = finish(True, WHOLE, own_across, [message_across], out)
+    out = finish(None, PARTS, own_chip, messages_chip)
+    out = finish(0, WHOLE, own_across, [message_odd], out)
+    out = finish(1, WHOLE, own_across, [message_even], out)
     return out.reshape(2 * ROWS, COLS)
 
 

time: 24.1 us -> 27 us (1.12); the launches traced: 23.7 us -> 26.8 us
  starting transfers between devices: 4.39 us -> 9.37 us
  waiting for transfers between devices: 7.31 us -> 5.48 us
    ppermute x3 -> x4, starting transfers between devices: 1.94 us -> 6.48 us  [the longest x2 2.65 us: chip_swap(): return lax.ppermute(shard, RING, [(i, i ^ 1) for i in range(count)])]
    ppermute x3 -> x4, waiting for transfers between devices: 6.93 us -> 5.46 us  [the longest x1 5.46 us: body(): lax.ppermute(send_edge(False, left_across, sums, later)[0], RING, from_even)]
    ppermute x3 -> x4, starting transfers between devices: 2.45 us -> 2.88 us  [exchanged(): return lax.ppermute(shard, 'blk', [(i, i ^ k) for i in range(members)])]
    ppermute x3 -> x4, waiting for transfers between devices: 0.37 us -> 0.01 us  [exchanged(): return lax.ppermute(shard, 'blk', [(i, i ^ k) for i in range(members)])]
    pallas_call x3 -> x5, Pallas kernels: 2.76 us -> 2.78 us  [the longest x3 2.26 us: finish(): pl.pallas_call(functools.partial(finish_kernel, role, parts), out_shape=j...]
  transfers between devices with their start and end apart: 6 -> 8, of which waited for: 2 -> 1; matrix products, arithmetic and copies ran while one was open for 0% -> 0% of each run, Pallas kernels for 38% -> 34%
where the time goes in v6:
time: 27 us; the launch traced here: 26.8 us
  Pallas kernels  11.9 us (44%)
  starting transfers between devices  9.37 us (35%)
  waiting for transfers between devices  5.48 us (20%)
    ppermute x1, waiting for transfers between devices, body(): lax.ppermute(send_edge(False, left_across, sums, later)[0], RING, from_even)  5.46 us
    pallas_call x2, Pallas kernels, spread(): pl.pallas_call(functools.partial(spread_kernel, members, capacity, quarte...  5.45 us
    ppermute x4, starting transfers between devices, exchanged(): return lax.ppermute(shard, 'blk', [(i, i ^ k) for i in range(members)])  2.88 us
    ppermute x2, starting transfers between devices, chip_swap(): return lax.ppermute(shard, RING, [(i, i ^ 1) for i in range(count)])  2.65 us
    ppermute x1, starting transfers between devices, body(): message_odd = lax.ppermute(message_odd, RING, from_odd)  2.54 us
    pallas_call x3, Pallas kernels, finish(): pl.pallas_call(functools.partial(finish_kernel, role, parts), out_shape=j...  2.26 us
    ppermute x1, starting transfers between devices, body(): lax.ppermute(send_edge(False, left_across, sums, later)[0], RING, from_even)  1.29 us
    pallas_call x1, Pallas kernels, middle(): pl.pallas_call(middle_kernel, out_shape=[pltpu.VMEM((ROWS, COLS), jnp.flo...  1.24 us
  transfers between devices with their start and end apart: 8, of which 1 were waited for; matrix products, arithmetic and copies ran while one was open for 0% of the time, Pallas kernels for 34%

profile of v6, /device:TPU:5, one launch (start us, length us, event | category | flops | bytes accessed | tf_op | source)
XLA Modules:
  0.0 26.8 jit_solution(327615613315421392)
XLA Ops:
  0.0 1.1 %pick.1 = (bf16[128,256]{1,0:T(8,128)(2,1)S(1)}, bf16[64,256]{1,0:T(8,128)(2,1)S(1)}, bf16[64,256]{1,0:T(8,128)(2,1)S(1)}, bf16[128,256]{1,0:T(8,128)(2,1)S(1)}, bf16[128,256]{1,0:T(8,128)(2,1)S(1)}) custom-call(s32[1,8]{1,0:T(1,128)} %ids.1, s32[1,4]{1,0:T(1,128)} %counts.1, bf16[1024,256]{1,0:T(8,128)(2,1)} %source.1), custom_call_target="tpu_custom_call" | custom-call | tf_op jit(solution)/shard_map/pick/pallas_call | solution.py:83
  1.1 1.3 %collective-permute-start.2 = (bf16[128,256]{1,0:T(8,128)(2,1)S(1)}, bf16[128,256]{1,0:T(8,128)(2,1)S(1)}, u32[]{:S(2)}, u32[]{:S(2)}) collective-permute-start(bf16[128,256]{1,0:T(8,128)(2,1)S(1)} %get-tuple-element.31), channel_id=1, source_target_pairs={{0,2},{1,3},{2,0},{3,1},{4,6},{5,7},{6,4},{7,5},{8,10},{9,11},{10,... | collective-permute-start | bytes 196616 | tf_op jit(solution)/shard_map/ppermute | solution.py:381
  2.4 1.1 %collective-permute-start.3 = (bf16[128,256]{1,0:T(8,128)(2,1)S(1)}, bf16[128,256]{1,0:T(8,128)(2,1)S(1)}, u32[]{:S(2)}, u32[]{:S(2)}) collective-permute-start(bf16[128,256]{1,0:T(8,128)(2,1)S(1)} %get-tuple-element.32), channel_id=1, source_target_pairs={{0,3},{1,2},{2,1},{3,0},{4,7},{5,6},{6,5},{7,4},{8,11},{9,10},{10,... | collective-permute-start | bytes 196616 | tf_op jit(solution)/shard_map/ppermute | solution.py:381
  3.5 0.0 collective-permute-start
  3.5 0.5 %collective-permute-start.1 = (bf16[64,256]{1,0:T(8,128)(2,1)S(1)}, bf16[64,256]{1,0:T(8,128)(2,1)S(1)}, u32[]{:S(2)}, u32[]{:S(2)}) collective-permute-start(bf16[64,256]{1,0:T(8,128)(2,1)S(1)} %get-tuple-element.29), channel_id=1, source_target_pairs={{0,1},{1,0},{2,3},{3,2},{4,5},{5,4},{6,7},{7,6},{8,9},{9,8},{10,11... | collective-permute-start | bytes 98312 | tf_op jit(solution)/shard_map/ppermute | solution.py:381
  4.0 2.7 %spread.2 = (bf16[1024,1024]{1,0:T(8,128)(2,1)S(1)}, bf16[1024,1024]{1,0:T(8,128)(2,1)S(1)}) custom-call(s32[1,128]{1,0:T(1,128)} %refs_0_.2, s32[1,128]{1,0:T(1,128)} %refs_1_.2, bf16[128,4096]{1,0:T(8,128)(2,1)} %refs_2_.2), custom_call_target="tpu_custom_call" | custom-call | flops 536870912 | bytes 6291456 | tf_op jit(solution)/shard_map/spread/pallas_call | solution.py:173
  6.7 0.0 collective-permute-done.refs_1_
  6.7 0.0 collective-permute-done.1.refs_2_
  6.8 0.4 %early.1 = (f32[1024,256]{1,0:T(8,128)S(1)}, bf16[512,256]{1,0:T(8,128)(2,1)S(1)}) custom-call(bf16[1024,1024]{1,0:T(8,128)(2,1)S(1)} %get-tuple-element.26.left, bf16[128,256]{1,0:T(8,128)(2,1)S(1)} %get-tuple-element.27.refs_0_, bf16[64,256]{1,0:T(8,128)(2,1)S(1)} %collective-permute-done.refs_1_, bf16[64,256]{1,0:T(8,128)(2,1)S(1)} %collective-permute-done.1.refs_2_), custom_call_target="tpu_custom_call" | custom-call | bytes 1024 | tf_op jit(solution)/shard_map/early/pallas_call | solution.py:205
  7.2 0.0 collective-permute-done.2.refs_0_
  7.2 0.0 collective-permute-done.3.refs_1_
  7.2 0.5 %send_odd.1 = (s16[1040,256]{1,0:T(8,128)(2,1)S(1)}, bf16[512,256]{1,0:T(8,128)(2,1)S(1)}) custom-call(bf16[1024,1024]{1,0:T(8,128)(2,1)S(1)} %get-tuple-element.26.left, f32[1024,256]{1,0:T(8,128)S(1)} %get-tuple-element.30.sums, bf16[128,256]{1,0:T(8,128)(2,1)S(1)} %collective-permute-done.2.refs_0_, bf16[128,256]{1,0:T(8,128)(2,1)S(1)} %collective-permute-done.3.refs_1_), custom_call_target="tpu_custom_call" | custom-call | flops 268435456 | bytes 2097152 | tf_op jit(solution)/shard_map/send_odd/pallas_call | solution.py:267
  7.7 2.5 %collective-permute-start.5 = (s16[1040,256]{1,0:T(8,128)(2,1)S(1)}, s16[1040,256]{1,0:T(8,128)(2,1)S(1)}, u32[]{:S(2)}, u32[]{:S(2)}) collective-permute-start(s16[1040,256]{1,0:T(8,128)(2,1)S(1)} %get-tuple-element.42), channel_id=1, source_target_pairs={{1,2},{3,4},{5,6},{7,8},{9,10},{11,12},{13,14},{15,16},{17,18},{19... | collective-permute-start | bytes 1597448 | tf_op jit(solution)/shard_map/ppermute | solution.py:407
  10.3 1.3 %collective-permute-start.4 = (s16[1040,256]{1,0:T(8,128)(2,1)S(1)}, s16[1040,256]{1,0:T(8,128)(2,1)S(1)}, u32[]{:S(2)}, u32[]{:S(2)}) collective-permute-start(s16[1040,256]{1,0:T(8,128)(2,1)S(1)} %send_even.1), channel_id=1, source_target_pairs={{2,1},{4,3},{6,5},{8,7},{10,9},{12,11},{14,13},{16,15},{18,17},{20... | collective-permute-start | bytes 1597448 | tf_op jit(solution)/shard_map/ppermute | solution.py:408
  11.6 0.8 %chip.1 = (s16[528,256]{1,0:T(8,128)(2,1)S(1)}, s16[528,256]{1,0:T(8,128)(2,1)S(1)}) custom-call(bf16[1024,1024]{1,0:T(8,128)(2,1)S(1)} %get-tuple-element.44.left, bf16[512,256]{1,0:T(8,128)(2,1)S(1)} %get-tuple-element.39.first, bf16[512,256]{1,0:T(8,128)(2,1)S(1)} %get-tuple-element.40.later.refs_0_), custom_call_target="tpu_custom_call" | custom-call | flops 536870912 | bytes 2097152 | tf_op jit(solution)/shard_map/chip/pallas_call | solution.py:287
  12.4 2.6 %collective-permute-start.6 = (s16[528,256]{1,0:T(8,128)(2,1)S(1)}, s16[528,256]{1,0:T(8,128)(2,1)S(1)}, u32[]{:S(2)}, u32[]{:S(2)}) collective-permute-start(s16[528,256]{1,0:T(8,128)(2,1)S(1)} %get-tuple-element.45), channel_id=1, source_target_pairs={{0,1},{1,0},{2,3},{3,2},{4,5},{5,4},{6,7},{7,6},{8,9},{9,8},{10,11... | collective-permute-start | bytes 811016 | tf_op jit(solution)/shard_map/ppermute | solution.py:393
  15.0 0.1 collective-permute-start.7
  15.1 2.7 %spread.3 = (bf16[1024,1024]{1,0:T(8,128)(2,1)S(1)}, bf16[1024,1024]{1,0:T(8,128)(2,1)S(1)}) custom-call(s32[1,128]{1,0:T(1,128)} %refs_0_.2, s32[1,128]{1,0:T(1,128)} %refs_1_.2, bf16[128,4096]{1,0:T(8,128)(2,1)} %refs_2_.2), custom_call_target="tpu_custom_call" | custom-call | flops 536870912 | bytes 6291456 | tf_op jit(solution)/shard_map/spread/pallas_call | solution.py:173
  17.8 1.2 %middle.1 = (f32[1024,256]{1,0:T(8,128)S(1)}, f32[1024,256]{1,0:T(8,128)S(1)}) custom-call(bf16[1024,1024]{1,0:T(8,128)(2,1)S(1)} %get-tuple-element.37.left_0, bf16[1024,1024]{1,0:T(8,128)(2,1)S(1)} %get-tuple-element.38.left_1, bf16[512,256]{1,0:T(8,128)(2,1)S(1)} %get-tuple-element.39.first, bf16[512,256]{1,0:T(8,128)(2,1)S(1)} %get-tuple-element.40.later.refs_0_), custom_call_target="tpu_custom_call" | custom-call | flops 1073741824 | bytes 4194304 | tf_op jit(solution)/shard_map/middle/pallas_call | solution.py:307
  19.1 0.0 collective-permute-done.6.refs_0_
  19.1 0.0 collective-permute-done.7.refs_1_
  19.1 1.1 %finish.3.refs_1_ = f32[32,64,256]{2,1,0:T(8,128)} custom-call(f32[1024,256]{1,0:T(8,128)S(1)} %get-tuple-element.43.own, s16[528,256]{1,0:T(8,128)(2,1)S(1)} %collective-permute-done.6.refs_0_, s16[528,256]{1,0:T(8,128)(2,1)S(1)} %collective-permute-done.7.refs_1_), custom_call_target="tpu_custom_call" | custom-call | flops 786432 | bytes 2097152 | tf_op jit(solution)/shard_map/finish/pallas_call | solution.py:357
  20.2 0.0 collective-permute-done.5.refs_0_
  20.2 0.1 finish.4.refs_1_
  20.3 5.5 %collective-permute-done.4.refs_0_ = s16[1040,256]{1,0:T(8,128)(2,1)S(1)} collective-permute-done((s16[1040,256]{1,0:T(8,128)(2,1)S(1)}, s16[1040,256]{1,0:T(8,128)(2,1)S(1)}, u32[]{:S(2)}, u32[]{:S(2)}) %collective-permute-start.4) | collective-permute-done | bytes 532512 | tf_op jit(solution)/shard_map/ppermute | solution.py:408
  25.7 1.1 %finish.5 = f32[32,64,256]{2,1,0:T(8,128)} custom-call(f32[1024,256]{1,0:T(8,128)S(1)} %get-tuple-element.41.own, s16[1040,256]{1,0:T(8,128)(2,1)S(1)} %collective-permute-done.4.refs_0_, f32[32,64,256]{2,1,0:T(8,128)} %finish.4.refs_1_), custom_call_target="tpu_custom_call", output_to_operand_aliasing={{}: (2, {})} | custom-call | flops 786432 | bytes 2097152 | tf_op jit(solution)/shard_map/finish/pallas_call | solution.py:357
  (1 shorter events, 0.0 us)
Async XLA Ops:
  1.1 6.1 %collective-permute-start.2 = (bf16[128,256]{1,0:T(8,128)(2,1)S(1)}, bf16[128,256]{1,0:T(8,128)(2,1)S(1)}, u32[]{:S(2)}, u32[]{:S(2)}) collective-permute-start(bf16[128,256]{1,0:T(8,128)(2,1)S(1)} %get-tuple-element.31), channel_id=1, source_target_pairs={{0,2},{1,3},{2,0},{3,1},{4,6},{5,7},{6,4},{7,5},{8,10},{9,11},{10,... | collective-permute-start | bytes 196616 | tf_op jit(solution)/shard_map/ppermute | solution.py:381
  2.4 4.8 %collective-permute-start.3 = (bf16[128,256]{1,0:T(8,128)(2,1)S(1)}, bf16[128,256]{1,0:T(8,128)(2,1)S(1)}, u32[]{:S(2)}, u32[]{:S(2)}) collective-permute-start(bf16[128,256]{1,0:T(8,128)(2,1)S(1)} %get-tuple-element.32), channel_id=1, source_target_pairs={{0,3},{1,2},{2,1},{3,0},{4,7},{5,6},{6,5},{7,4},{8,11},{9,10},{10,... | collective-permute-start | bytes 196616 | tf_op jit(solution)/shard_map/ppermute | solution.py:381
  3.5 3.2 %collective-permute-start = (bf16[64,256]{1,0:T(8,128)(2,1)S(1)}, bf16[64,256]{1,0:T(8,128)(2,1)S(1)}, u32[]{:S(2)}, u32[]{:S(2)}) collective-permute-start(bf16[64,256]{1,0:T(8,128)(2,1)S(1)} %get-tuple-element.28), channel_id=1, source_target_pairs={{0,1},{1,0},{2,3},{3,2},{4,5},{5,4},{6,7},{7,6},{8,9},{9,8},{10,11... | collective-permute-start | bytes 98312 | tf_op jit(solution)/shard_map/ppermute | solution.py:381
  3.5 3.3 %collective-permute-start.1 = (bf16[64,256]{1,0:T(8,128)(2,1)S(1)}, bf16[64,256]{1,0:T(8,128)(2,1)S(1)}, u32[]{:S(2)}, u32[]{:S(2)}) collective-permute-start(bf16[64,256]{1,0:T(8,128)(2,1)S(1)} %get-tuple-element.29), channel_id=1, source_target_pairs={{0,1},{1,0},{2,3},{3,2},{4,5},{5,4},{6,7},{7,6},{8,9},{9,8},{10,11... | collective-permute-start | bytes 98312 | tf_op jit(solution)/shard_map/ppermute | solution.py:381
  7.7 12.5 %collective-permute-start.5 = (s16[1040,256]{1,0:T(8,128)(2,1)S(1)}, s16[1040,256]{1,0:T(8,128)(2,1)S(1)}, u32[]{:S(2)}, u32[]{:S(2)}) collective-permute-start(s16[1040,256]{1,0:T(8,128)(2,1)S(1)} %get-tuple-element.42), channel_id=1, source_target_pairs={{1,2},{3,4},{5,6},{7,8},{9,10},{11,12},{13,14},{15,16},{17,18},{19... | collective-permute-start | bytes 1597448 | tf_op jit(solution)/shard_map/ppermute | solution.py:407
  10.3 15.4 %collective-permute-start.4 = (s16[1040,256]{1,0:T(8,128)(2,1)S(1)}, s16[1040,256]{1,0:T(8,128)(2,1)S(1)}, u32[]{:S(2)}, u32[]{:S(2)}) collective-permute-start(s16[1040,256]{1,0:T(8,128)(2,1)S(1)} %send_even.1), channel_id=1, source_target_pairs={{2,1},{4,3},{6,5},{8,7},{10,9},{12,11},{14,13},{16,15},{18,17},{20... | collective-permute-start | bytes 1597448 | tf_op jit(solution)/shard_map/ppermute | solution.py:408
  12.4 6.6 %collective-permute-start.6 = (s16[528,256]{1,0:T(8,128)(2,1)S(1)}, s16[528,256]{1,0:T(8,128)(2,1)S(1)}, u32[]{:S(2)}, u32[]{:S(2)}) collective-permute-start(s16[528,256]{1,0:T(8,128)(2,1)S(1)} %get-tuple-element.45), channel_id=1, source_target_pairs={{0,1},{1,0},{2,3},{3,2},{4,5},{5,4},{6,7},{7,6},{8,9},{9,8},{10,11... | collective-permute-start | bytes 811016 | tf_op jit(solution)/shard_map/ppermute | solution.py:393
  15.0 4.1 %collective-permute-start.7 = (s16[528,256]{1,0:T(8,128)(2,1)S(1)}, s16[528,256]{1,0:T(8,128)(2,1)S(1)}, u32[]{:S(2)}, u32[]{:S(2)}) collective-permute-start(s16[528,256]{1,0:T(8,128)(2,1)S(1)} %get-tuple-element.46), channel_id=1, source_target_pairs={{0,1},{1,0},{2,3},{3,2},{4,5},{5,4},{6,7},{7,6},{8,9},{9,8},{10,11... | collective-permute-start | bytes 811016 | tf_op jit(solution)/shard_map/ppermute | solution.py:393

commit v7 on v6

--- a/solution.py
+++ b/solution.py
@@ -77,9 +77,7 @@
 
 
 def pick(members, capacity, send_ids, send_counts, source):
-    whole = pltpu.VMEM((capacity * BLOCK, COLS), jnp.bfloat16)
-    single = pltpu.VMEM((BLOCK, COLS), jnp.bfloat16)
-    out_shape = [whole] + [single] * (EARLY - 1) * capacity + [whole] * (members - EARLY)
+    out_shape = [pltpu.VMEM((capacity * BLOCK, COLS), jnp.bfloat16)] * members
     return pl.pallas_call(
         functools.partial(pick_kernel, members, capacity),
         out_shape=out_shape,
@@ -208,7 +206,7 @@
         in_specs=[VMEM] * (1 + len(blocks)),
         out_specs=[VMEM] * 2,
         compiler_params=params(),
-        cost_estimate=cost(0, 2**10),
+        cost_estimate=cost(2 * ROWS * depth * COLS, 2 * 2**20),
         name="early",
     )(left, *blocks)
 
@@ -382,12 +380,6 @@
     return passed_along(shard, "blk", k)
 
 
-def ring_pairs():
-    count = lax.axis_size(RING)
-    odd = [(i, (i + 1) % count) for i in range(1, count, 2)]
-    return odd, [(there, here) for here, there in odd]
-
-
 def chip_swap(shard):
     count = lax.axis_size(RING)
     return lax.ppermute(shard, RING, [(i, i ^ 1) for i in range(count)])
@@ -397,15 +389,14 @@
     members = lax.axis_size("blk")
     capacity = send_ids.shape[1] // members
     picked = pick(members, capacity, send_ids, send_counts, source)
-    later_blocks = [exchanged(picked[k - members], k) for k in range(EARLY, members)]
-    early_blocks = [picked[0]] + [exchanged(picked[1 + n], 1 + n // capacity) for n in range((EARLY - 1) * capacity)]
+    blocks = [picked[0]] + [exchanged(picked[k], k) for k in range(1, members)]
+    early_blocks, later_blocks = blocks[:EARLY], blocks[EARLY:]
     tiles = (tile_slot, tile_target, tile_weights)
     left_across, left_chip = spread(members, capacity, ((0, 3), (3, 0)), *tiles)
     sums, first = early(left_across, early_blocks)
-    from_odd, from_even = ring_pairs()
     message_odd, later = send_edge(True, left_across, sums, *later_blocks)
-    message_odd = lax.ppermute(message_odd, RING, from_odd)
-    message_even = lax.ppermute(send_edge(False, left_across, sums, later)[0], RING, from_even)
+    message_odd = passed_along(message_odd, RING, 1)
+    message_even = passed_along(send_edge(False, left_across, sums, later)[0], RING, -1)
     messages_chip = [chip_swap(message) for message in chip_edge(PARTS, left_chip, first, later)]
     tiles, later = lax.optimization_barrier((tiles, later))
     own_left = spread(members, capacity, ((1, 2), (2, 1)), *tiles)

time: 27 us -> 24.3 us (0.900)
  starting transfers between devices: 9.37 us -> 5.16 us
  waiting for transfers between devices: 5.48 us -> 6.94 us
    ppermute x2, starting transfers between devices: 3.84 us -> 1.1 us  [passed_along(): lax.ppermute(shard, axis, [(i, (i + by) % count) for i in range(count)])]
    ppermute x2, waiting for transfers between devices: 5.46 us -> 6.56 us  [passed_along(): lax.ppermute(shard, axis, [(i, (i + by) % count) for i in range(count)])]
    ppermute x2, starting transfers between devices: 2.65 us -> 1.61 us  [chip_swap(): return lax.ppermute(shard, RING, [(i, i ^ 1) for i in range(count)])]
    ppermute x4 -> x3, starting transfers between devices: 2.88 us -> 2.45 us  [exchanged(): return lax.ppermute(shard, 'blk', [(i, i ^ k) for i in range(members)])]
    ppermute x4 -> x3, waiting for transfers between devices: 0.01 us -> 0.37 us  [exchanged(): return lax.ppermute(shard, 'blk', [(i, i ^ k) for i in range(members)])]
  transfers between devices with their start and end apart: 8 -> 7, of which waited for: 1 -> 3; matrix products, arithmetic and copies ran while one was open for 0% -> 0% of each run, Pallas kernels for 34% -> 38%
where the time goes in v7:
time: 24.3 us; the launch traced here: 24 us
  Pallas kernels  11.8 us (49%)
  waiting for transfers between devices  6.94 us (29%)
  starting transfers between devices  5.16 us (21%)
    ppermute x2, waiting for transfers between devices, passed_along(): lax.ppermute(shard, axis, [(i, (i + by) % count) for i in range(count)])  6.56 us
    pallas_call x2, Pallas kernels, spread(): pl.pallas_call(functools.partial(spread_kernel, members, capacity, quarte...  5.45 us
    ppermute x3, starting transfers between devices, exchanged(): return lax.ppermute(shard, 'blk', [(i, i ^ k) for i in range(members)])  2.45 us
    pallas_call x3, Pallas kernels, finish(): pl.pallas_call(functools.partial(finish_kernel, role, parts), out_shape=j...  2.24 us
    ppermute x2, starting transfers between devices, chip_swap(): return lax.ppermute(shard, RING, [(i, i ^ 1) for i in range(count)])  1.61 us
    pallas_call x1, Pallas kernels, middle(): pl.pallas_call(middle_kernel, out_shape=[pltpu.VMEM((ROWS, COLS), jnp.flo...  1.25 us
    pallas_call x1, Pallas kernels, pick(): pl.pallas_call(functools.partial(pick_kernel, members, capacity), out_sha...  1.1 us
    ppermute x2, starting transfers between devices, passed_along(): lax.ppermute(shard, axis, [(i, (i + by) % count) for i in range(count)])  1.1 us
  transfers between devices with their start and end apart: 7, of which 3 were waited for; matrix products, arithmetic and copies ran while one was open for 0% of the time, Pallas kernels for 38%

profile of v7, /device:TPU:5, one launch (start us, length us, event | category | flops | bytes accessed | tf_op | source)
XLA Modules:
  0.0 24.0 jit_solution(2651164702414317974)
XLA Ops:
  0.0 1.1 %pick.1 = (bf16[128,256]{1,0:T(8,128)(2,1)S(1)}, bf16[128,256]{1,0:T(8,128)(2,1)S(1)}, bf16[128,256]{1,0:T(8,128)(2,1)S(1)}, bf16[128,256]{1,0:T(8,128)(2,1)S(1)}) custom-call(s32[1,8]{1,0:T(1,128)} %ids.1, s32[1,4]{1,0:T(1,128)} %counts.1, bf16[1024,256]{1,0:T(8,128)(2,1)} %source.1), custom_call_target="tpu_custom_call" | custom-call | tf_op jit(solution)/shard_map/pick/pallas_call | solution.py:81
  1.1 0.7 %collective-permute-start = (bf16[128,256]{1,0:T(8,128)(2,1)S(1)}, bf16[128,256]{1,0:T(8,128)(2,1)S(1)}, u32[]{:S(2)}, u32[]{:S(2)}) collective-permute-start(bf16[128,256]{1,0:T(8,128)(2,1)S(1)} %get-tuple-element.27), channel_id=1, source_target_pairs={{0,1},{1,0},{2,3},{3,2},{4,5},{5,4},{6,7},{7,6},{8,9},{9,8},{10,11... | collective-permute-start | bytes 196616 | tf_op jit(solution)/shard_map/ppermute | solution.py:379
  1.9 1.2 %collective-permute-start.1 = (bf16[128,256]{1,0:T(8,128)(2,1)S(1)}, bf16[128,256]{1,0:T(8,128)(2,1)S(1)}, u32[]{:S(2)}, u32[]{:S(2)}) collective-permute-start(bf16[128,256]{1,0:T(8,128)(2,1)S(1)} %get-tuple-element.29), channel_id=1, source_target_pairs={{0,2},{1,3},{2,0},{3,1},{4,6},{5,7},{6,4},{7,5},{8,10},{9,11},{10,... | collective-permute-start | bytes 196616 | tf_op jit(solution)/shard_map/ppermute | solution.py:379
  3.1 0.5 %collective-permute-start.2 = (bf16[128,256]{1,0:T(8,128)(2,1)S(1)}, bf16[128,256]{1,0:T(8,128)(2,1)S(1)}, u32[]{:S(2)}, u32[]{:S(2)}) collective-permute-start(bf16[128,256]{1,0:T(8,128)(2,1)S(1)} %get-tuple-element.30), channel_id=1, source_target_pairs={{0,3},{1,2},{2,1},{3,0},{4,7},{5,6},{6,5},{7,4},{8,11},{9,10},{10,... | collective-permute-start | bytes 196616 | tf_op jit(solution)/shard_map/ppermute | solution.py:379
  3.6 2.7 %spread.2 = (bf16[1024,1024]{1,0:T(8,128)(2,1)S(1)}, bf16[1024,1024]{1,0:T(8,128)(2,1)S(1)}) custom-call(s32[1,128]{1,0:T(1,128)} %refs_0_.2, s32[1,128]{1,0:T(1,128)} %refs_1_.2, bf16[128,4096]{1,0:T(8,128)(2,1)} %refs_2_.2), custom_call_target="tpu_custom_call" | custom-call | flops 536870912 | bytes 6291456 | tf_op jit(solution)/shard_map/spread/pallas_call | solution.py:171
  6.3 0.0 collective-permute-done.refs_1_
  6.3 0.4 %early.1 = (f32[1024,256]{1,0:T(8,128)S(1)}, bf16[512,256]{1,0:T(8,128)(2,1)S(1)}) custom-call(bf16[1024,1024]{1,0:T(8,128)(2,1)S(1)} %get-tuple-element.25.left, bf16[128,256]{1,0:T(8,128)(2,1)S(1)} %get-tuple-element.26.refs_0_, bf16[128,256]{1,0:T(8,128)(2,1)S(1)} %collective-permute-done.refs_1_), custom_call_target="tpu_custom_call" | custom-call | flops 268435456 | bytes 2097152 | tf_op jit(solution)/shard_map/early/pallas_call | solution.py:203
  6.7 0.0 collective-permute-done.1.refs_0_
  6.8 0.4 %collective-permute-done.2.refs_1_ = bf16[128,256]{1,0:T(8,128)(2,1)S(1)} collective-permute-done((bf16[128,256]{1,0:T(8,128)(2,1)S(1)}, bf16[128,256]{1,0:T(8,128)(2,1)S(1)}, u32[]{:S(2)}, u32[]{:S(2)}) %collective-permute-start.2) | collective-permute-done | bytes 65568 | tf_op jit(solution)/shard_map/ppermute | solution.py:379
  7.1 0.5 %send_odd.1 = (s16[1040,256]{1,0:T(8,128)(2,1)S(1)}, bf16[512,256]{1,0:T(8,128)(2,1)S(1)}) custom-call(bf16[1024,1024]{1,0:T(8,128)(2,1)S(1)} %get-tuple-element.25.left, f32[1024,256]{1,0:T(8,128)S(1)} %get-tuple-element.28.sums, bf16[128,256]{1,0:T(8,128)(2,1)S(1)} %collective-permute-done.1.refs_0_, bf16[128,256]{1,0:T(8,128)(2,1)S(1)} %collective-permute-done.2.refs_1_), custom_call_target="tpu_custom_call" | custom-call | flops 268435456 | bytes 2097152 | tf_op jit(solution)/shard_map/send_odd/pallas_call | solution.py:265
  7.6 0.9 %collective-permute-start.4 = (s16[1040,256]{1,0:T(8,128)(2,1)S(1)}, s16[1040,256]{1,0:T(8,128)(2,1)S(1)}, u32[]{:S(2)}, u32[]{:S(2)}) collective-permute-start(s16[1040,256]{1,0:T(8,128)(2,1)S(1)} %get-tuple-element.40), channel_id=1, source_target_pairs={{0,1},{1,2},{2,3},{3,4},{4,5},{5,6},{6,7},{7,8},{8,9},{9,10},{10,1... | collective-permute-start | bytes 1597448 | tf_op jit(solution)/shard_map/ppermute | solution.py:373
  8.5 0.2 collective-permute-start.3
  8.7 0.8 %chip.1 = (s16[528,256]{1,0:T(8,128)(2,1)S(1)}, s16[528,256]{1,0:T(8,128)(2,1)S(1)}) custom-call(bf16[1024,1024]{1,0:T(8,128)(2,1)S(1)} %get-tuple-element.42.left, bf16[512,256]{1,0:T(8,128)(2,1)S(1)} %get-tuple-element.37.first, bf16[512,256]{1,0:T(8,128)(2,1)S(1)} %get-tuple-element.38.later.refs_0_), custom_call_target="tpu_custom_call" | custom-call | flops 536870912 | bytes 2097152 | tf_op jit(solution)/shard_map/chip/pallas_call | solution.py:285
  9.6 1.5 %collective-permute-start.5 = (s16[528,256]{1,0:T(8,128)(2,1)S(1)}, s16[528,256]{1,0:T(8,128)(2,1)S(1)}, u32[]{:S(2)}, u32[]{:S(2)}) collective-permute-start(s16[528,256]{1,0:T(8,128)(2,1)S(1)} %get-tuple-element.43), channel_id=1, source_target_pairs={{0,1},{1,0},{2,3},{3,2},{4,5},{5,4},{6,7},{7,6},{8,9},{9,8},{10,11... | collective-permute-start | bytes 811016 | tf_op jit(solution)/shard_map/ppermute | solution.py:385
  11.1 0.1 collective-permute-start.6
  11.2 2.7 %spread.3 = (bf16[1024,1024]{1,0:T(8,128)(2,1)S(1)}, bf16[1024,1024]{1,0:T(8,128)(2,1)S(1)}) custom-call(s32[1,128]{1,0:T(1,128)} %refs_0_.2, s32[1,128]{1,0:T(1,128)} %refs_1_.2, bf16[128,4096]{1,0:T(8,128)(2,1)} %refs_2_.2), custom_call_target="tpu_custom_call" | custom-call | flops 536870912 | bytes 6291456 | tf_op jit(solution)/shard_map/spread/pallas_call | solution.py:171
  13.9 1.2 %middle.1 = (f32[1024,256]{1,0:T(8,128)S(1)}, f32[1024,256]{1,0:T(8,128)S(1)}) custom-call(bf16[1024,1024]{1,0:T(8,128)(2,1)S(1)} %get-tuple-element.35.left_0, bf16[1024,1024]{1,0:T(8,128)(2,1)S(1)} %get-tuple-element.36.left_1, bf16[512,256]{1,0:T(8,128)(2,1)S(1)} %get-tuple-element.37.first, bf16[512,256]{1,0:T(8,128)(2,1)S(1)} %get-tuple-element.38.later.refs_0_), custom_call_target="tpu_custom_call" | custom-call | flops 1073741824 | bytes 4194304 | tf_op jit(solution)/shard_map/middle/pallas_call | solution.py:305
  15.2 0.0 collective-permute-done.5.refs_0_
  15.2 0.0 collective-permute-done.6.refs_1_
  15.2 1.1 %finish.3.refs_1_ = f32[32,64,256]{2,1,0:T(8,128)} custom-call(f32[1024,256]{1,0:T(8,128)S(1)} %get-tuple-element.41.own, s16[528,256]{1,0:T(8,128)(2,1)S(1)} %collective-permute-done.5.refs_0_, s16[528,256]{1,0:T(8,128)(2,1)S(1)} %collective-permute-done.6.refs_1_), custom_call_target="tpu_custom_call" | custom-call | flops 786432 | bytes 2097152 | tf_op jit(solution)/shard_map/finish/pallas_call | solution.py:355
  16.3 2.2 %collective-permute-done.4.refs_0_ = s16[1040,256]{1,0:T(8,128)(2,1)S(1)} collective-permute-done((s16[1040,256]{1,0:T(8,128)(2,1)S(1)}, s16[1040,256]{1,0:T(8,128)(2,1)S(1)}, u32[]{:S(2)}, u32[]{:S(2)}) %collective-permute-start.4) | collective-permute-done | bytes 532512 | tf_op jit(solution)/shard_map/ppermute | solution.py:373
  18.5 4.4 %collective-permute-done.3.refs_0_ = s16[1040,256]{1,0:T(8,128)(2,1)S(1)} collective-permute-done((s16[1040,256]{1,0:T(8,128)(2,1)S(1)}, s16[1040,256]{1,0:T(8,128)(2,1)S(1)}, u32[]{:S(2)}, u32[]{:S(2)}) %collective-permute-start.3) | collective-permute-done | bytes 532512 | tf_op jit(solution)/shard_map/ppermute | solution.py:373
  22.9 1.1 %finish.5 = f32[32,64,256]{2,1,0:T(8,128)} custom-call(f32[1024,256]{1,0:T(8,128)S(1)} %get-tuple-element.39.own, s16[1040,256]{1,0:T(8,128)(2,1)S(1)} %collective-permute-done.3.refs_0_, f32[32,64,256]{2,1,0:T(8,128)} %finish.4.refs_1_), custom_call_target="tpu_custom_call", output_to_operand_aliasing={{}: (2, {})} | custom-call | flops 786432 | bytes 2097152 | tf_op jit(solution)/shard_map/finish/pallas_call | solution.py:355
  (2 shorter events, 0.0 us)
Async XLA Ops:
  1.1 5.2 %collective-permute-start = (bf16[128,256]{1,0:T(8,128)(2,1)S(1)}, bf16[128,256]{1,0:T(8,128)(2,1)S(1)}, u32[]{:S(2)}, u32[]{:S(2)}) collective-permute-start(bf16[128,256]{1,0:T(8,128)(2,1)S(1)} %get-tuple-element.27), channel_id=1, source_target_pairs={{0,1},{1,0},{2,3},{3,2},{4,5},{5,4},{6,7},{7,6},{8,9},{9,8},{10,11... | collective-permute-start | bytes 196616 | tf_op jit(solution)/shard_map/ppermute | solution.py:379
  1.9 4.9 %collective-permute-start.1 = (bf16[128,256]{1,0:T(8,128)(2,1)S(1)}, bf16[128,256]{1,0:T(8,128)(2,1)S(1)}, u32[]{:S(2)}, u32[]{:S(2)}) collective-permute-start(bf16[128,256]{1,0:T(8,128)(2,1)S(1)} %get-tuple-element.29), channel_id=1, source_target_pairs={{0,2},{1,3},{2,0},{3,1},{4,6},{5,7},{6,4},{7,5},{8,10},{9,11},{10,... | collective-permute-start | bytes 196616 | tf_op jit(solution)/shard_map/ppermute | solution.py:379
  3.1 4.0 %collective-permute-start.2 = (bf16[128,256]{1,0:T(8,128)(2,1)S(1)}, bf16[128,256]{1,0:T(8,128)(2,1)S(1)}, u32[]{:S(2)}, u32[]{:S(2)}) collective-permute-start(bf16[128,256]{1,0:T(8,128)(2,1)S(1)} %get-tuple-element.30), channel_id=1, source_target_pairs={{0,3},{1,2},{2,1},{3,0},{4,7},{5,6},{6,5},{7,4},{8,11},{9,10},{10,... | collective-permute-start | bytes 196616 | tf_op jit(solution)/shard_map/ppermute | solution.py:379
  7.6 10.8 %collective-permute-start.4 = (s16[1040,256]{1,0:T(8,128)(2,1)S(1)}, s16[1040,256]{1,0:T(8,128)(2,1)S(1)}, u32[]{:S(2)}, u32[]{:S(2)}) collective-permute-start(s16[1040,256]{1,0:T(8,128)(2,1)S(1)} %get-tuple-element.40), channel_id=1, source_target_pairs={{0,1},{1,2},{2,3},{3,4},{4,5},{5,6},{6,7},{7,8},{8,9},{9,10},{10,1... | collective-permute-start | bytes 1597448 | tf_op jit(solution)/shard_map/ppermute | solution.py:373
  8.5 14.4 %collective-permute-start.3 = (s16[1040,256]{1,0:T(8,128)(2,1)S(1)}, s16[1040,256]{1,0:T(8,128)(2,1)S(1)}, u32[]{:S(2)}, u32[]{:S(2)}) collective-permute-start(s16[1040,256]{1,0:T(8,128)(2,1)S(1)} %send_even.1), channel_id=1, source_target_pairs={{0,31},{1,0},{2,1},{3,2},{4,3},{5,4},{6,5},{7,6},{8,7},{9,8},{10,9... | collective-permute-start | bytes 1597448 | tf_op jit(solution)/shard_map/ppermute | solution.py:373
  9.6 5.6 %collective-permute-start.5 = (s16[528,256]{1,0:T(8,128)(2,1)S(1)}, s16[528,256]{1,0:T(8,128)(2,1)S(1)}, u32[]{:S(2)}, u32[]{:S(2)}) collective-permute-start(s16[528,256]{1,0:T(8,128)(2,1)S(1)} %get-tuple-element.43), channel_id=1, source_target_pairs={{0,1},{1,0},{2,3},{3,2},{4,5},{5,4},{6,7},{7,6},{8,9},{9,8},{10,11... | collective-permute-start | bytes 811016 | tf_op jit(solution)/shard_map/ppermute | solution.py:385
  11.1 4.1 %collective-permute-start.6 = (s16[528,256]{1,0:T(8,128)(2,1)S(1)}, s16[528,256]{1,0:T(8,128)(2,1)S(1)}, u32[]{:S(2)}, u32[]{:S(2)}) collective-permute-start(s16[528,256]{1,0:T(8,128)(2,1)S(1)} %get-tuple-element.44), channel_id=1, source_target_pairs={{0,1},{1,0},{2,3},{3,2},{4,5},{5,4},{6,7},{7,6},{8,9},{9,8},{10,11... | collective-permute-start | bytes 811016 | tf_op jit(solution)/shard_map/ppermute | solution.py:385

commit v8 on v5

v8 whole, which is shorter than its diff:
```python
import functools

import jax
import jax.numpy as jnp
from jax import lax
from jax.experimental import pallas as pl
from jax.experimental.pallas import tpu as pltpu
from jax.sharding import PartitionSpec as P

COLS = 256
BLOCK = 64
EB = 16
CHUNK = 2 * BLOCK
ROWS = EB * BLOCK
GROUP = 64
EARLY = 2
ACROSS = (ROWS,)
PARTS = (ROWS // 2, ROWS // 2)
FLOOR = 2.0**-110
VMEM = pl.BlockSpec(memory_space=pltpu.VMEM)
SMEM = pl.BlockSpec(memory_space=pltpu.SMEM)
ANY = pl.BlockSpec(memory_space=pl.ANY)


def params():
    return pltpu.CompilerParams(vmem_limit_bytes=40 * 1024 * 1024)


def cost(flops, nbytes):
    return pl.CostEstimate(flops=flops, bytes_accessed=nbytes, transcendentals=0)


def parity():
    return lax.rem(lax.axis_index("grp") * lax.axis_size("blk") + lax.axis_index("blk"), 2)


def pick_kernel(members, capacity, ids, counts, source, slots, targets, *refs):
    picked, (slot_list, target_list, blocks, id_list, count_list, sems) = refs[:members], refs[members:]
    own = lax.axis_index("blk")
    pairs = (
        (ids, id_list),
        (counts, count_list),
        (source, blocks),
        (slots, slot_list),
        (targets, target_list),
    )
    copies = [pltpu.make_async_copy(here, there, sems.at[n]) for n, (here, there) in enumerate(pairs)]
    for copy in copies:
        copy.start()
    for copy in copies[:3]:
        copy.wait()
    for k in range(members):
        reader = lax.rem(own + k, members)
        for j in range(capacity):
            start = pl.multiple_of(id_list[0, reader * capacity + j] * BLOCK, BLOCK)
            live = (j < count_list[0, reader]).astype(jnp.float32).astype(jnp.bfloat16)
            picked[k][j * BLOCK : (j + 1) * BLOCK] = blocks[pl.ds(start, BLOCK)] * live
    for copy in copies[3:]:
        copy.wait()


def in_hbm(*arrays):
    return [pltpu.with_memory_space_constraint(x, pltpu.HBM) for x in arrays]


def pick(members, capacity, send_ids, send_counts, source, slots, targets):
    shape = (capacity * BLOCK, COLS)
    results = pl.pallas_call(
        functools.partial(pick_kernel, members, capacity),
        out_shape=[pltpu.VMEM(shape, jnp.bfloat16)] * members
        + [pltpu.VMEM(slots.shape, jnp.int32), pltpu.VMEM(targets.shape, jnp.int32)],
        in_specs=[ANY] * 5,
        out_specs=[VMEM] * (members + 2),
        scratch_shapes=[
            pltpu.VMEM(source.shape, source.dtype),
            pltpu.SMEM(send_ids.shape, jnp.int32),
            pltpu.SMEM(send_counts.shape, jnp.int32),
            pltpu.SemaphoreType.DMA((5,)),
        ],
        compiler_params=params(),
        name="pick",
    )(*in_hbm(send_ids, send_counts, source, slots, targets))
    return results[:members], results[members:]


def lanes_of(k, members):
    if k < EARLY:
        return k * CHUNK, (EARLY + k) * CHUNK
    return (EARLY + k) * CHUNK, (members + k) * CHUNK


def spread_kernel(members, capacity, quarters, slots, targets, weights, *refs):
    outs, (held, sems) = refs[:-2], refs[-2:]
    half = weights.shape[1] // 2
    parts = [held.at[:, pl.ds(n * half, half)] for n in range(2)]
    copies = [pltpu.make_async_copy(weights.at[:, pl.ds(n * half, half)], parts[n], sems.at[n]) for n in range(2)]
    for copy in copies:
        copy.start()
    own = lax.axis_index("blk")
    tiles = weights.shape[0]
    count = len(quarters)
    slot = slots[...]
    sender = slot // capacity
    place = lax.rem(own - sender + members, members) * capacity + slot % capacity
    target = targets[...]
    rows = lax.broadcasted_iota(jnp.int32, (count * EB, tiles), 0)
    wanted = rows
    for n, (even, odd) in enumerate(quarters):
        wanted = jnp.where(rows // EB == n, rows % EB + jnp.where(parity() == 1, odd, even) * EB, wanted)
    hit = target == wanted
    table = jnp.concatenate(
        [
            jnp.concatenate(
                [(hit & (place == k * capacity + j)).astype(jnp.float32) for j in range(capacity)], axis=1
            )
            for k in range(members)
        ],
        axis=0,
    ).astype(jnp.bfloat16)
    left = (lax.broadcasted_iota(jnp.int32, (1, CHUNK), 1) < BLOCK).astype(jnp.float32)
    low = left.astype(jnp.bfloat16)
    high = (1.0 - left).astype(jnp.bfloat16)

    def step(part, first, c, _):
        x = part[:, pl.ds(pl.multiple_of(c * CHUNK, CHUNK), CHUNK)]
        c = c + first
        swapped = jnp.concatenate([x[:, BLOCK:], x[:, :BLOCK]], axis=1)
        right = jnp.concatenate(
            [
                jnp.concatenate([x * low, swapped * low], axis=1),
                jnp.concatenate([swapped * high, x * high], axis=1),
            ],
            axis=0,
        )
        sums = jnp.dot(table, right, preferred_element_type=jnp.float32)
        coarse = sums.astype(jnp.bfloat16)
        fine = (sums - coarse.astype(jnp.float32)).astype(jnp.bfloat16)
        for k in range(members):
            for n in range(count):
                top = (k * count + n) * EB
                for h in range(2):
                    row = pl.ds(pl.multiple_of((2 * c + h) * EB, EB), EB)
                    part = (slice(top, top + EB), slice(h * CHUNK, (h + 1) * CHUNK))
                    for lanes, value in zip(lanes_of(k, members), (coarse, fine)):
                        outs[n][row, lanes : lanes + CHUNK] = value[part]
        return 0

    each = half // CHUNK
    for n in range(2):
        copies[n].wait()
        lax.fori_loop(0, each, functools.partial(step, parts[n], n * each), 0, unroll=each)


def spread(members, capacity, quarters, slots, targets, weights):
    shape = (ROWS, 2 * members * CHUNK)
    tiles = weights.shape[0]
    return pl.pallas_call(
        functools.partial(spread_kernel, members, capacity, quarters),
        out_shape=[pltpu.VMEM(shape, jnp.bfloat16)] * len(quarters),
        in_specs=[VMEM] * 2 + [ANY],
        out_specs=[VMEM] * len(quarters),
        scratch_shapes=[
            pltpu.VMEM(weights.shape, weights.dtype),
            pltpu.SemaphoreType.DMA((2,)),
        ],
        compiler_params=params(),
        cost_estimate=cost(2 * members * EB * len(quarters) * 2 * tiles * 8192, 6 * 2**20),
        name="spread",
    )(slots, targets, *in_hbm(weights))


def stacked(blocks, both):
    rows = blocks[0].shape[0]
    for half in range(2):
        for k, block in enumerate(blocks):
            start = (half * len(blocks) + k) * rows
            both[start : start + rows] = block[...]


def early_kernel(left, *refs):
    blocks, (sums, both) = refs[:-2], refs[-2:]
    stacked(blocks, both)
    sums[...] = jnp.dot(left[:, : both.shape[0]], both[...], preferred_element_type=jnp.float32)


def early(left, blocks):
    depth = 2 * EARLY * CHUNK
    return pl.pallas_call(
        early_kernel,
        out_shape=[pltpu.VMEM((ROWS, COLS), jnp.float32), pltpu.VMEM((depth, COLS), jnp.bfloat16)],
        in_specs=[VMEM] * (1 + len(blocks)),
        out_specs=[VMEM] * 2,
        compiler_params=params(),
        cost_estimate=cost(2 * ROWS * depth * COLS, 2 * 2**20),
        name="early",
    )(left, *blocks)


def coded(piece, message, powers):
    count = piece.shape[0]
    if count // GROUP < powers.shape[0]:
        powers[...] = jnp.zeros_like(powers)
    for g in range(count // GROUP):
        rows = piece[g * GROUP : (g + 1) * GROUP]
        most = jnp.maximum(jnp.max(jnp.abs(rows), axis=0, keepdims=True), FLOOR)
        power = jnp.floor(jnp.log2(most) + 0.001) + 1.0
        whole = jnp.round(rows * jnp.exp2(15.0 - power)).astype(jnp.int32)
        message[g * GROUP : (g + 1) * GROUP] = whole.astype(jnp.int16)
        powers[g : g + 1] = power.astype(jnp.int32)
    message[count : count + powers.shape[0]] = powers[...].astype(jnp.int16)


def product(left, first, later):
    both = jnp.concatenate([first[...], later[...]], axis=0)
    return jnp.dot(left, both, preferred_element_type=jnp.float32)


def across_kernel(parts, left, sums, *refs):
    blocks, refs = refs[: -2 * len(parts) - 1], refs[-2 * len(parts) - 1 :]
    messages, both, powers = refs[: len(parts)], refs[len(parts)], refs[len(parts) + 1 :]
    stacked(blocks, both)
    start = left.shape[1] - both.shape[0]
    piece = sums[...] + jnp.dot(left[:, start:], both[...], preferred_element_type=jnp.float32)
    first = 0
    for count, message, power in zip(parts, messages, powers):
        coded(piece[first : first + count], message, power)
        first += count


def scales(count):
    return max(count // GROUP, 16)


def message_of(count):
    return pltpu.VMEM((count + scales(count), COLS), jnp.int16)


def powers_of(count):
    return pltpu.VMEM((scales(count), COLS), jnp.int32)


def across_edge(parts, left, sums, blocks):
    depth = 2 * len(blocks) * CHUNK
    return pl.pallas_call(
        functools.partial(across_kernel, parts),
        out_shape=[message_of(count) for count in parts] + [pltpu.VMEM((depth, COLS), jnp.bfloat16)],
        in_specs=[VMEM] * (2 + len(blocks)),
        out_specs=[VMEM] * (len(parts) + 1),
        scratch_shapes=[powers_of(count) for count in parts],
        compiler_params=params(),
        cost_estimate=cost(2 * ROWS * depth * COLS, 2 * 2**20),
        name="across",
    )(left, sums, *blocks)


def chip_kernel(parts, left, first, later, *refs):
    start = 0
    for count, message, powers in zip(parts, refs[: len(parts)], refs[len(parts) :]):
        coded(product(left[start : start + count], first, later), message, powers)
        start += count


def chip_edge(parts, left, first, later):
    return pl.pallas_call(
        functools.partial(chip_kernel, parts),
        out_shape=[message_of(count) for count in parts],
        in_specs=[VMEM] * 3,
        out_specs=[VMEM] * len(parts),
        scratch_shapes=[powers_of(count) for count in parts],
        compiler_params=params(),
        cost_estimate=cost(2 * ROWS * left.shape[1] * COLS, 2 * 2**20),
        name="chip",
    )(left, first, later)


def middle_kernel(left_0, left_1, first, later, *outs):
    step = 256
    for left, out in zip((left_0, left_1), outs):
        for start in range(0, ROWS, step):
            out[start : start + step] = product(left[start : start + step], first, later)


def middle(left_0, left_1, first, later):
    return pl.pallas_call(
        middle_kernel,
        out_shape=[pltpu.VMEM((ROWS, COLS), jnp.float32)] * 2,
        in_specs=[VMEM] * 4,
        out_specs=[VMEM] * 2,
        compiler_params=params(),
        cost_estimate=cost(4 * ROWS * left_0.shape[1] * COLS, 4 * 2**20),
        name="middle",
    )(left_0, left_1, first, later)


def finish_kernel(across, low, parts, own, *refs):
    messages, (out, rows, sems) = refs[: len(parts)], refs[-3:]
    half = parity() if across else 1 - parity()
    high = low + sum(parts) // EB
    pitch = high - low + 8
    targets = rows.reshape(COLS // 128, EB, pitch, 128)
    some = EB // 2
    copies = []
    for first in range(0, EB, some):
        i = low
        for count, message in zip(parts, messages):
            scale = jnp.exp2(message[count : count + scales(count)].astype(jnp.float32) - 15.0)
            for at in range(0, count, EB):
                g = at // GROUP
                value = message[at : at + EB].astype(jnp.float32)[first : first + some]
                value = own[i * EB + first : i * EB + first + some] + value * scale[g : g + 1]
                for n in range(COLS // 128):
                    place = pl.ds(first * pitch + i - low, some, stride=pitch)
                    rows[n, place] = value[:, n * 128 : (n + 1) * 128]
                i += 1
        for n in range(COLS // 128):
            here = targets.at[n, pl.ds(first, some), pl.ds(0, high - low)]
            there = out.at[pl.ds(half * EB + first, some), pl.ds(low, high - low), pl.ds(n * 128, 128)]
            copies.append(pltpu.make_async_copy(here, there, sems.at[len(copies)]))
            copies[-1].start()
    for copy in copies:
        copy.wait()


def finish(across, low, parts, own, messages, out=None):
    given = [] if out is None else [out]
    pitch = sum(parts) // EB + 8
    return pl.pallas_call(
        functools.partial(finish_kernel, across, low, parts),
        out_shape=jax.ShapeDtypeStruct((2 * EB, BLOCK, COLS), jnp.float32),
        in_specs=[VMEM] * (1 + len(parts)) + [ANY] * len(given),
        out_specs=ANY,
        scratch_shapes=[
            pltpu.VMEM((COLS // 128, EB * pitch, 128), jnp.float32),
            pltpu.SemaphoreType.DMA((2 * COLS // 128,)),
        ],
        input_output_aliases={} if out is None else {1 + len(parts): 0},
        compiler_params=params(),
        cost_estimate=cost(3 * sum(parts) * COLS, 2 * 2**20 * sum(parts) // ROWS),
        name="finish",
    )(own, *messages, *given)


def passed_along(shard, axis, by):
    count = lax.axis_size(axis)
    return lax.ppermute(shard, axis, [(i, (i + by) % count) for i in range(count)])


def ring_swap(shard, across):
    axes = ("grp", "blk")
    count = lax.axis_size(axes)
    if across:
        return lax.ppermute(shard, axes, [(i, (i + (1 if i % 2 else -1)) % count) for i in range(count)])
    return lax.ppermute(shard, axes, [(i, i ^ 1) for i in range(count)])


def body(source, send_ids, send_counts, tile_slot, tile_target, tile_weights):
    members = lax.axis_size("blk")
    capacity = send_ids.shape[1] // members
    picked, tiles = pick(
        members, capacity, send_ids, send_counts, source, tile_slot, tile_target
    )
    blocks = [picked[0]] + [passed_along(picked[k], "blk", k) for k in range(1, members)]
    (left_across,) = spread(members, capacity, ((0, 3),), *tiles, tile_weights)
    sums, first = early(left_across, blocks[:EARLY])
    message_across, later = across_edge(ACROSS, left_across, sums, blocks[EARLY:])
    message_across = ring_swap(message_across, True)
    tiles, later = lax.optimization_barrier((tiles, later))
    left_chip, *own_left = spread(members, capacity, ((3, 0), (1, 2), (2, 1)), *tiles, tile_weights)
    messages_chip = [ring_swap(message, False) for message in chip_edge(PARTS, left_chip, first, later)]
    own_across, own_chip = middle(*own_left, first, later)
    out = finish(False, 0, PARTS, own_chip, messages_chip)
    out = finish(True, 0, ACROSS, own_across, [message_across], out)
    return out.reshape(2 * ROWS, COLS)


def solution(mesh):
    spec = P(("grp", "blk"), None)
    return jax.shard_map(body, mesh=mesh, in_specs=(spec,) * 6, out_specs=spec, check_vma=False)
```

time: 24.1 us -> 23.4 us (0.971)
  starting transfers between devices: 4.39 us -> 4.06 us
  Pallas kernels: 11.9 us -> 11.6 us
    ppermute x1, waiting for transfers between devices: 6.93 us -> 6.31 us  [ring_swap(): lax.ppermute(shard, axes, [(i, (i + (1 if i % 2 else -1)) % count) for i...]
    ppermute x3, waiting for transfers between devices: 0.37 us -> 0.81 us  [passed_along(): lax.ppermute(shard, axis, [(i, (i + by) % count) for i in range(count)])]
    ppermute x1, starting transfers between devices: 1.36 us -> 1.06 us  [ring_swap(): lax.ppermute(shard, axes, [(i, (i + (1 if i % 2 else -1)) % count) for i...]
  transfers between devices with their start and end apart: 6 -> 6, of which waited for: 2 -> 4; matrix products, arithmetic and copies ran while one was open for 0% -> 0% of each run, Pallas kernels for 38% -> 38%
where the time goes in v8:
time: 23.4 us; the launch traced here: 23.1 us
  Pallas kernels  11.6 us (50%)
  waiting for transfers between devices  7.33 us (31%)
  starting transfers between devices  4.06 us (17%)
    ppermute x1, waiting for transfers between devices, ring_swap(): lax.ppermute(shard, axes, [(i, (i + (1 if i % 2 else -1)) % count) for i...  6.31 us
    pallas_call x2, Pallas kernels, spread(): pl.pallas_call(functools.partial(spread_kernel, members, capacity, quarte...  5.27 us
    ppermute x3, starting transfers between devices, passed_along(): lax.ppermute(shard, axis, [(i, (i + by) % count) for i in range(count)])  2.3 us
    pallas_call x2, Pallas kernels, finish(): pl.pallas_call(functools.partial(finish_kernel, across, low, parts), out_...  2.2 us
    pallas_call x1, Pallas kernels, middle(): pl.pallas_call(middle_kernel, out_shape=[pltpu.VMEM((ROWS, COLS), jnp.flo...  1.26 us
    pallas_call x1, Pallas kernels, pick(): pl.pallas_call(functools.partial(pick_kernel, members, capacity), out_sha...  1.13 us
    ppermute x1, starting transfers between devices, ring_swap(): lax.ppermute(shard, axes, [(i, (i + (1 if i % 2 else -1)) % count) for i...  1.06 us
    pallas_call x1, Pallas kernels, chip_edge(): pl.pallas_call(functools.partial(chip_kernel, parts), out_shape=[message_...  0.83 us
  transfers between devices with their start and end apart: 6, of which 4 were waited for; matrix products, arithmetic and copies ran while one was open for 0% of the time, Pallas kernels for 38%

profile of v8, /device:TPU:5, one launch (start us, length us, event | category | flops | bytes accessed | tf_op | source)
XLA Modules:
  0.0 23.1 jit_solution(15659505902811295686)
XLA Ops:
  0.0 1.1 %pick.1 = (bf16[128,256]{1,0:T(8,128)(2,1)S(1)}, bf16[128,256]{1,0:T(8,128)(2,1)S(1)}, bf16[128,256]{1,0:T(8,128)(2,1)S(1)}, bf16[128,256]{1,0:T(8,128)(2,1)S(1)...) custom-call(s32[1,8]{1,0:T(1,128)} %ids.1, s32[1,4]{1,0:T(1,128)} %counts.1, bf16[1024,256]{1,0:T(8,128)(2,1)} %source.1, ...), custom_call_target="tpu_custom_call" | custom-call | tf_op jit(solution)/shard_map/pick/pallas_call | solution.py:68
  1.1 1.8 %collective-permute-start = (bf16[128,256]{1,0:T(8,128)(2,1)S(1)}, bf16[128,256]{1,0:T(8,128)(2,1)S(1)}, u32[]{:S(2)}, u32[]{:S(2)}) collective-permute-start(bf16[128,256]{1,0:T(8,128)(2,1)S(1)} %get-tuple-element.28), channel_id=1, source_target_pairs={{0,1},{1,2},{2,3},{3,0},{4,5},{5,6},{6,7},{7,4},{8,9},{9,10},{10,1... | collective-permute-start | bytes 196616 | tf_op jit(solution)/shard_map/ppermute | solution.py:345
  3.0 0.3 %collective-permute-start.1 = (bf16[128,256]{1,0:T(8,128)(2,1)S(1)}, bf16[128,256]{1,0:T(8,128)(2,1)S(1)}, u32[]{:S(2)}, u32[]{:S(2)}) collective-permute-start(bf16[128,256]{1,0:T(8,128)(2,1)S(1)} %get-tuple-element.30), channel_id=1, source_target_pairs={{0,2},{1,3},{2,0},{3,1},{4,6},{5,7},{6,4},{7,5},{8,10},{9,11},{10,... | collective-permute-start | bytes 196616 | tf_op jit(solution)/shard_map/ppermute | solution.py:345
  3.2 0.2 collective-permute-start.2
  3.4 2.3 %spread.2.left = bf16[1024,1024]{1,0:T(8,128)(2,1)S(1)} custom-call(s32[1,128]{1,0:T(1,128)S(1)} %get-tuple-element.33.slots, s32[1,128]{1,0:T(1,128)S(1)} %get-tuple-element.34.targets, bf16[128,4096]{1,0:T(8,128)(2,1)} %weights.3), custom_call_target="tpu_custom_call" | custom-call | flops 268435456 | bytes 6291456 | tf_op jit(solution)/shard_map/spread/pallas_call | solution.py:157
  5.7 0.0 collective-permute-done.refs_1_
  5.7 0.4 %early.1 = (f32[1024,256]{1,0:T(8,128)S(1)}, bf16[512,256]{1,0:T(8,128)(2,1)S(1)}) custom-call(bf16[1024,1024]{1,0:T(8,128)(2,1)S(1)} %spread.2.left, bf16[128,256]{1,0:T(8,128)(2,1)S(1)} %get-tuple-element.27.refs_0_, bf16[128,256]{1,0:T(8,128)(2,1)S(1)} %collective-permute-done.refs_1_), custom_call_target="tpu_custom_call" | custom-call | flops 268435456 | bytes 2097152 | tf_op jit(solution)/shard_map/early/pallas_call | solution.py:188
  6.2 0.2 collective-permute-done.1.refs_0_
  6.4 0.6 %collective-permute-done.2.refs_1_ = bf16[128,256]{1,0:T(8,128)(2,1)S(1)} collective-permute-done((bf16[128,256]{1,0:T(8,128)(2,1)S(1)}, bf16[128,256]{1,0:T(8,128)(2,1)S(1)}, u32[]{:S(2)}, u32[]{:S(2)}) %collective-permute-start.2) | collective-permute-done | bytes 65568 | tf_op jit(solution)/shard_map/ppermute | solution.py:345
  7.0 0.5 %across.1 = (s16[1040,256]{1,0:T(8,128)(2,1)S(1)}, bf16[512,256]{1,0:T(8,128)(2,1)S(1)}) custom-call(bf16[1024,1024]{1,0:T(8,128)(2,1)S(1)} %spread.2.left, f32[1024,256]{1,0:T(8,128)S(1)} %get-tuple-element.29.sums, bf16[128,256]{1,0:T(8,128)(2,1)S(1)} %collective-permute-done.1.refs_0_, bf16[128,256]{1,0:T(8,128)(2,1)S(1)} %collective-permute-done.2.refs_1_), custom_call_target="tpu_custom_call" | custom-call | flops 268435456 | bytes 2097152 | tf_op jit(solution)/shard_map/across/pallas_call | solution.py:244
  7.5 1.1 %collective-permute-start.3 = (s16[1040,256]{1,0:T(8,128)(2,1)S(1)}, s16[1040,256]{1,0:T(8,128)(2,1)S(1)}, u32[]{:S(2)}, u32[]{:S(2)}) collective-permute-start(s16[1040,256]{1,0:T(8,128)(2,1)S(1)} %get-tuple-element.40), channel_id=1, source_target_pairs={{0,31},{1,2},{2,1},{3,4},{4,3},{5,6},{6,5},{7,8},{8,7},{9,10},{10,... | collective-permute-start | bytes 1597448 | tf_op jit(solution)/shard_map/ppermute | solution.py:352
  8.5 3.0 %spread.3 = (bf16[1024,1024]{1,0:T(8,128)(2,1)S(1)}, bf16[1024,1024]{1,0:T(8,128)(2,1)S(1)}, bf16[1024,1024]{1,0:T(8,128)(2,1)S(1)}) custom-call(s32[1,128]{1,0:T(1,128)S(1)} %get-tuple-element.33.slots, s32[1,128]{1,0:T(1,128)S(1)} %get-tuple-element.34.targets, bf16[128,4096]{1,0:T(8,128)(2,1)} %weights.3), custom_call_target="tpu_custom_call" | custom-call | flops 805306368 | bytes 6291456 | tf_op jit(solution)/shard_map/spread/pallas_call | solution.py:157
  11.5 0.8 %chip.1 = (s16[528,256]{1,0:T(8,128)(2,1)S(1)}, s16[528,256]{1,0:T(8,128)(2,1)S(1)}) custom-call(bf16[1024,1024]{1,0:T(8,128)(2,1)S(1)} %get-tuple-element.42.left, bf16[512,256]{1,0:T(8,128)(2,1)S(1)} %get-tuple-element.37.first, bf16[512,256]{1,0:T(8,128)(2,1)S(1)} %get-tuple-element.38.later), custom_call_target="tpu_custom_call" | custom-call | flops 536870912 | bytes 2097152 | tf_op jit(solution)/shard_map/chip/pallas_call | solution.py:264
  12.4 0.6 %collective-permute-start.4 = (s16[528,256]{1,0:T(8,128)(2,1)S(1)}, s16[528,256]{1,0:T(8,128)(2,1)S(1)}, u32[]{:S(2)}, u32[]{:S(2)}) collective-permute-start(s16[528,256]{1,0:T(8,128)(2,1)S(1)} %get-tuple-element.43), channel_id=1, source_target_pairs={{0,1},{1,0},{2,3},{3,2},{4,5},{5,4},{6,7},{7,6},{8,9},{9,8},{10,11... | collective-permute-start | bytes 811016 | tf_op jit(solution)/shard_map/ppermute | solution.py:353
  13.0 0.1 collective-permute-start.5
  13.1 1.3 %middle.1 = (f32[1024,256]{1,0:T(8,128)S(1)}, f32[1024,256]{1,0:T(8,128)S(1)}) custom-call(bf16[1024,1024]{1,0:T(8,128)(2,1)S(1)} %get-tuple-element.35.left_0, bf16[1024,1024]{1,0:T(8,128)(2,1)S(1)} %get-tuple-element.36.left_1, bf16[512,256]{1,0:T(8,128)(2,1)S(1)} %get-tuple-element.37.first, bf16[512,256]{1,0:T(8,128)(2,1)S(1)} %get-tuple-element.38.later), custom_call_target="tpu_custom_call" | custom-call | flops 1073741824 | bytes 4194304 | tf_op jit(solution)/shard_map/middle/pallas_call | solution.py:284
  14.3 0.0 collective-permute-done.4.refs_0_
  14.3 0.2 collective-permute-done.5.refs_1_
  14.5 1.1 %finish.2.refs_1_ = f32[32,64,256]{2,1,0:T(8,128)} custom-call(f32[1024,256]{1,0:T(8,128)S(1)} %get-tuple-element.41.own, s16[528,256]{1,0:T(8,128)(2,1)S(1)} %collective-permute-done.4.refs_0_, s16[528,256]{1,0:T(8,128)(2,1)S(1)} %collective-permute-done.5.refs_1_), custom_call_target="tpu_custom_call" | custom-call | flops 786432 | bytes 2097152 | tf_op jit(solution)/shard_map/finish/pallas_call | solution.py:327
  15.7 6.3 %collective-permute-done.3.refs_0_ = s16[1040,256]{1,0:T(8,128)(2,1)S(1)} collective-permute-done((s16[1040,256]{1,0:T(8,128)(2,1)S(1)}, s16[1040,256]{1,0:T(8,128)(2,1)S(1)}, u32[]{:S(2)}, u32[]{:S(2)}) %collective-permute-start.3) | collective-permute-done | bytes 532512 | tf_op jit(solution)/shard_map/ppermute | solution.py:352
  22.0 1.1 %finish.3 = f32[32,64,256]{2,1,0:T(8,128)} custom-call(f32[1024,256]{1,0:T(8,128)S(1)} %get-tuple-element.39.own, s16[1040,256]{1,0:T(8,128)(2,1)S(1)} %collective-permute-done.3.refs_0_, f32[32,64,256]{2,1,0:T(8,128)} %finish.2.refs_1_), custom_call_target="tpu_custom_call", output_to_operand_aliasing={{}: (2, {})} | custom-call | flops 786432 | bytes 2097152 | tf_op jit(solution)/shard_map/finish/pallas_call | solution.py:327
Async XLA Ops:
  1.1 4.6 %collective-permute-start = (bf16[128,256]{1,0:T(8,128)(2,1)S(1)}, bf16[128,256]{1,0:T(8,128)(2,1)S(1)}, u32[]{:S(2)}, u32[]{:S(2)}) collective-permute-start(bf16[128,256]{1,0:T(8,128)(2,1)S(1)} %get-tuple-element.28), channel_id=1, source_target_pairs={{0,1},{1,2},{2,3},{3,0},{4,5},{5,6},{6,7},{7,4},{8,9},{9,10},{10,1... | collective-permute-start | bytes 196616 | tf_op jit(solution)/shard_map/ppermute | solution.py:345
  3.0 3.4 %collective-permute-start.1 = (bf16[128,256]{1,0:T(8,128)(2,1)S(1)}, bf16[128,256]{1,0:T(8,128)(2,1)S(1)}, u32[]{:S(2)}, u32[]{:S(2)}) collective-permute-start(bf16[128,256]{1,0:T(8,128)(2,1)S(1)} %get-tuple-element.30), channel_id=1, source_target_pairs={{0,2},{1,3},{2,0},{3,1},{4,6},{5,7},{6,4},{7,5},{8,10},{9,11},{10,... | collective-permute-start | bytes 196616 | tf_op jit(solution)/shard_map/ppermute | solution.py:345
  3.2 3.8 %collective-permute-start.2 = (bf16[128,256]{1,0:T(8,128)(2,1)S(1)}, bf16[128,256]{1,0:T(8,128)(2,1)S(1)}, u32[]{:S(2)}, u32[]{:S(2)}) collective-permute-start(bf16[128,256]{1,0:T(8,128)(2,1)S(1)} %get-tuple-element.31), channel_id=1, source_target_pairs={{0,3},{1,0},{2,1},{3,2},{4,7},{5,4},{6,5},{7,6},{8,11},{9,8},{10,9... | collective-permute-start | bytes 196616 | tf_op jit(solution)/shard_map/ppermute | solution.py:345
  7.5 14.5 %collective-permute-start.3 = (s16[1040,256]{1,0:T(8,128)(2,1)S(1)}, s16[1040,256]{1,0:T(8,128)(2,1)S(1)}, u32[]{:S(2)}, u32[]{:S(2)}) collective-permute-start(s16[1040,256]{1,0:T(8,128)(2,1)S(1)} %get-tuple-element.40), channel_id=1, source_target_pairs={{0,31},{1,2},{2,1},{3,4},{4,3},{5,6},{6,5},{7,8},{8,7},{9,10},{10,... | collective-permute-start | bytes 1597448 | tf_op jit(solution)/shard_map/ppermute | solution.py:352
  12.4 2.0 %collective-permute-start.4 = (s16[528,256]{1,0:T(8,128)(2,1)S(1)}, s16[528,256]{1,0:T(8,128)(2,1)S(1)}, u32[]{:S(2)}, u32[]{:S(2)}) collective-permute-start(s16[528,256]{1,0:T(8,128)(2,1)S(1)} %get-tuple-element.43), channel_id=1, source_target_pairs={{0,1},{1,0},{2,3},{3,2},{4,5},{5,4},{6,7},{7,6},{8,9},{9,8},{10,11... | collective-permute-start | bytes 811016 | tf_op jit(solution)/shard_map/ppermute | solution.py:353
  13.0 1.6 %collective-permute-start.5 = (s16[528,256]{1,0:T(8,128)(2,1)S(1)}, s16[528,256]{1,0:T(8,128)(2,1)S(1)}, u32[]{:S(2)}, u32[]{:S(2)}) collective-permute-start(s16[528,256]{1,0:T(8,128)(2,1)S(1)} %get-tuple-element.44), channel_id=1, source_target_pairs={{0,1},{1,0},{2,3},{3,2},{4,5},{5,4},{6,7},{7,6},{8,9},{9,8},{10,11... | collective-permute-start | bytes 811016 | tf_op jit(solution)/shard_map/ppermute | solution.py:353

commit v9 on v8

--- a/solution.py
+++ b/solution.py
@@ -110,39 +110,33 @@
     hit = target == wanted
     table = jnp.concatenate(
         [
-            jnp.concatenate(
-                [(hit & (place == k * capacity + j)).astype(jnp.float32) for j in range(capacity)], axis=1
-            )
+            (hit & (place == k * capacity + j)).astype(jnp.float32)
+            for j in range(capacity)
             for k in range(members)
         ],
         axis=0,
     ).astype(jnp.bfloat16)
-    left = (lax.broadcasted_iota(jnp.int32, (1, CHUNK), 1) < BLOCK).astype(jnp.float32)
-    low = left.astype(jnp.bfloat16)
-    high = (1.0 - left).astype(jnp.bfloat16)
+    side = members * count * EB
+    left = lax.broadcasted_iota(jnp.int32, (side, CHUNK), 1) < BLOCK
 
     def step(part, first, c, _):
         x = part[:, pl.ds(pl.multiple_of(c * CHUNK, CHUNK), CHUNK)]
         c = c + first
-        swapped = jnp.concatenate([x[:, BLOCK:], x[:, :BLOCK]], axis=1)
-        right = jnp.concatenate(
-            [
-                jnp.concatenate([x * low, swapped * low], axis=1),
-                jnp.concatenate([swapped * high, x * high], axis=1),
-            ],
-            axis=0,
+        sums = jnp.dot(table, x, preferred_element_type=jnp.float32)
+        one, two = sums[:side], sums[side:]
+        halves = (
+            jnp.where(left, one, pltpu.roll(two, BLOCK, 1)),
+            jnp.where(left, pltpu.roll(one, BLOCK, 1), two),
         )
-        sums = jnp.dot(table, right, preferred_element_type=jnp.float32)
-        coarse = sums.astype(jnp.bfloat16)
-        fine = (sums - coarse.astype(jnp.float32)).astype(jnp.bfloat16)
-        for k in range(members):
-            for n in range(count):
-                top = (k * count + n) * EB
-                for h in range(2):
-                    row = pl.ds(pl.multiple_of((2 * c + h) * EB, EB), EB)
-                    part = (slice(top, top + EB), slice(h * CHUNK, (h + 1) * CHUNK))
-                    for lanes, value in zip(lanes_of(k, members), (coarse, fine)):
-                        outs[n][row, lanes : lanes + CHUNK] = value[part]
+        for h, value in enumerate(halves):
+            coarse = value.astype(jnp.bfloat16)
+            fine = (value - coarse.astype(jnp.float32)).astype(jnp.bfloat16)
+            row = pl.ds(pl.multiple_of((2 * c + h) * EB, EB), EB)
+            for k in range(members):
+                for n in range(count):
+                    top = (k * count + n) * EB
+                    for lanes, part in zip(lanes_of(k, members), (coarse, fine)):
+                        outs[n][row, lanes : lanes + CHUNK] = part[top : top + EB]
         return 0
 
     each = half // CHUNK

time: 23.4 us -> 23.4 us (level)
  no operation moved by 1% of the time
where the time goes in v9:
time: 23.4 us; the launch traced here: 23.1 us
  Pallas kernels  11.6 us (50%)
  waiting for transfers between devices  7.37 us (31%)
  starting transfers between devices  4.04 us (17%)
    ppermute x1, waiting for transfers between devices, ring_swap(): lax.ppermute(shard, axes, [(i, (i + (1 if i % 2 else -1)) % count) for i...  6.17 us
    pallas_call x2, Pallas kernels, spread(): pl.pallas_call(functools.partial(spread_kernel, members, capacity, quarte...  5.25 us
    ppermute x3, starting transfers between devices, passed_along(): lax.ppermute(shard, axis, [(i, (i + by) % count) for i in range(count)])  2.3 us
    pallas_call x2, Pallas kernels, finish(): pl.pallas_call(functools.partial(finish_kernel, across, low, parts), out_...  2.2 us
    pallas_call x1, Pallas kernels, middle(): pl.pallas_call(middle_kernel, out_shape=[pltpu.VMEM((ROWS, COLS), jnp.flo...  1.26 us
    pallas_call x1, Pallas kernels, pick(): pl.pallas_call(functools.partial(pick_kernel, members, capacity), out_sha...  1.13 us
    ppermute x1, starting transfers between devices, ring_swap(): lax.ppermute(shard, axes, [(i, (i + (1 if i % 2 else -1)) % count) for i...  1.06 us
    ppermute x3, waiting for transfers between devices, passed_along(): lax.ppermute(shard, axis, [(i, (i + by) % count) for i in range(count)])  0.99 us
  transfers between devices with their start and end apart: 6, of which 4 were waited for; matrix products, arithmetic and copies ran while one was open for 0% of the time, Pallas kernels for 38%

profile of v9, /device:TPU:5, one launch (start us, length us, event | category | flops | bytes accessed | tf_op | source)
XLA Modules:
  0.0 23.1 jit_solution(11753893234226949677)
XLA Ops:
  0.0 1.1 %pick.1 = (bf16[128,256]{1,0:T(8,128)(2,1)S(1)}, bf16[128,256]{1,0:T(8,128)(2,1)S(1)}, bf16[128,256]{1,0:T(8,128)(2,1)S(1)}, bf16[128,256]{1,0:T(8,128)(2,1)S(1)...) custom-call(s32[1,8]{1,0:T(1,128)} %ids.1, s32[1,4]{1,0:T(1,128)} %counts.1, bf16[1024,256]{1,0:T(8,128)(2,1)} %source.1, ...), custom_call_target="tpu_custom_call" | custom-call | tf_op jit(solution)/shard_map/pick/pallas_call | solution.py:68
  1.1 1.8 %collective-permute-start = (bf16[128,256]{1,0:T(8,128)(2,1)S(1)}, bf16[128,256]{1,0:T(8,128)(2,1)S(1)}, u32[]{:S(2)}, u32[]{:S(2)}) collective-permute-start(bf16[128,256]{1,0:T(8,128)(2,1)S(1)} %get-tuple-element.28), channel_id=1, source_target_pairs={{0,1},{1,2},{2,3},{3,0},{4,5},{5,6},{6,7},{7,4},{8,9},{9,10},{10,1... | collective-permute-start | bytes 196616 | tf_op jit(solution)/shard_map/ppermute | solution.py:339
  3.0 0.3 %collective-permute-start.1 = (bf16[128,256]{1,0:T(8,128)(2,1)S(1)}, bf16[128,256]{1,0:T(8,128)(2,1)S(1)}, u32[]{:S(2)}, u32[]{:S(2)}) collective-permute-start(bf16[128,256]{1,0:T(8,128)(2,1)S(1)} %get-tuple-element.30), channel_id=1, source_target_pairs={{0,2},{1,3},{2,0},{3,1},{4,6},{5,7},{6,4},{7,5},{8,10},{9,11},{10,... | collective-permute-start | bytes 196616 | tf_op jit(solution)/shard_map/ppermute | solution.py:339
  3.2 0.2 collective-permute-start.2
  3.4 2.1 %spread.2.left = bf16[1024,1024]{1,0:T(8,128)(2,1)S(1)} custom-call(s32[1,128]{1,0:T(1,128)S(1)} %get-tuple-element.33.slots, s32[1,128]{1,0:T(1,128)S(1)} %get-tuple-element.34.targets, bf16[128,4096]{1,0:T(8,128)(2,1)} %weights.3), custom_call_target="tpu_custom_call" | custom-call | flops 268435456 | bytes 6291456 | tf_op jit(solution)/shard_map/spread/pallas_call | solution.py:151
  5.5 0.0 collective-permute-done.refs_1_
  5.5 0.4 %early.1 = (f32[1024,256]{1,0:T(8,128)S(1)}, bf16[512,256]{1,0:T(8,128)(2,1)S(1)}) custom-call(bf16[1024,1024]{1,0:T(8,128)(2,1)S(1)} %spread.2.left, bf16[128,256]{1,0:T(8,128)(2,1)S(1)} %get-tuple-element.27.refs_0_, bf16[128,256]{1,0:T(8,128)(2,1)S(1)} %collective-permute-done.refs_1_), custom_call_target="tpu_custom_call" | custom-call | flops 268435456 | bytes 2097152 | tf_op jit(solution)/shard_map/early/pallas_call | solution.py:182
  6.0 0.4 %collective-permute-done.1.refs_0_ = bf16[128,256]{1,0:T(8,128)(2,1)S(1)} collective-permute-done((bf16[128,256]{1,0:T(8,128)(2,1)S(1)}, bf16[128,256]{1,0:T(8,128)(2,1)S(1)}, u32[]{:S(2)}, u32[]{:S(2)}) %collective-permute-start.1) | collective-permute-done | bytes 65568 | tf_op jit(solution)/shard_map/ppermute | solution.py:339
  6.4 0.6 %collective-permute-done.2.refs_1_ = bf16[128,256]{1,0:T(8,128)(2,1)S(1)} collective-permute-done((bf16[128,256]{1,0:T(8,128)(2,1)S(1)}, bf16[128,256]{1,0:T(8,128)(2,1)S(1)}, u32[]{:S(2)}, u32[]{:S(2)}) %collective-permute-start.2) | collective-permute-done | bytes 65568 | tf_op jit(solution)/shard_map/ppermute | solution.py:339
  7.0 0.5 %across.1 = (s16[1040,256]{1,0:T(8,128)(2,1)S(1)}, bf16[512,256]{1,0:T(8,128)(2,1)S(1)}) custom-call(bf16[1024,1024]{1,0:T(8,128)(2,1)S(1)} %spread.2.left, f32[1024,256]{1,0:T(8,128)S(1)} %get-tuple-element.29.sums, bf16[128,256]{1,0:T(8,128)(2,1)S(1)} %collective-permute-done.1.refs_0_, bf16[128,256]{1,0:T(8,128)(2,1)S(1)} %collective-permute-done.2.refs_1_), custom_call_target="tpu_custom_call" | custom-call | flops 268435456 | bytes 2097152 | tf_op jit(solution)/shard_map/across/pallas_call | solution.py:238
  7.5 1.1 %collective-permute-start.3 = (s16[1040,256]{1,0:T(8,128)(2,1)S(1)}, s16[1040,256]{1,0:T(8,128)(2,1)S(1)}, u32[]{:S(2)}, u32[]{:S(2)}) collective-permute-start(s16[1040,256]{1,0:T(8,128)(2,1)S(1)} %get-tuple-element.40), channel_id=1, source_target_pairs={{0,31},{1,2},{2,1},{3,4},{4,3},{5,6},{6,5},{7,8},{8,7},{9,10},{10,... | collective-permute-start | bytes 1597448 | tf_op jit(solution)/shard_map/ppermute | solution.py:346
  8.5 3.2 %spread.3 = (bf16[1024,1024]{1,0:T(8,128)(2,1)S(1)}, bf16[1024,1024]{1,0:T(8,128)(2,1)S(1)}, bf16[1024,1024]{1,0:T(8,128)(2,1)S(1)}) custom-call(s32[1,128]{1,0:T(1,128)S(1)} %get-tuple-element.33.slots, s32[1,128]{1,0:T(1,128)S(1)} %get-tuple-element.34.targets, bf16[128,4096]{1,0:T(8,128)(2,1)} %weights.3), custom_call_target="tpu_custom_call" | custom-call | flops 805306368 | bytes 6291456 | tf_op jit(solution)/shard_map/spread/pallas_call | solution.py:151
  11.7 0.8 %chip.1 = (s16[528,256]{1,0:T(8,128)(2,1)S(1)}, s16[528,256]{1,0:T(8,128)(2,1)S(1)}) custom-call(bf16[1024,1024]{1,0:T(8,128)(2,1)S(1)} %get-tuple-element.42.left, bf16[512,256]{1,0:T(8,128)(2,1)S(1)} %get-tuple-element.37.first, bf16[512,256]{1,0:T(8,128)(2,1)S(1)} %get-tuple-element.38.later), custom_call_target="tpu_custom_call" | custom-call | flops 536870912 | bytes 2097152 | tf_op jit(solution)/shard_map/chip/pallas_call | solution.py:258
  12.5 0.6 %collective-permute-start.4 = (s16[528,256]{1,0:T(8,128)(2,1)S(1)}, s16[528,256]{1,0:T(8,128)(2,1)S(1)}, u32[]{:S(2)}, u32[]{:S(2)}) collective-permute-start(s16[528,256]{1,0:T(8,128)(2,1)S(1)} %get-tuple-element.43), channel_id=1, source_target_pairs={{0,1},{1,0},{2,3},{3,2},{4,5},{5,4},{6,7},{7,6},{8,9},{9,8},{10,11... | collective-permute-start | bytes 811016 | tf_op jit(solution)/shard_map/ppermute | solution.py:347
  13.1 0.1 collective-permute-start.5
  13.2 1.3 %middle.1 = (f32[1024,256]{1,0:T(8,128)S(1)}, f32[1024,256]{1,0:T(8,128)S(1)}) custom-call(bf16[1024,1024]{1,0:T(8,128)(2,1)S(1)} %get-tuple-element.35.left_0, bf16[1024,1024]{1,0:T(8,128)(2,1)S(1)} %get-tuple-element.36.left_1, bf16[512,256]{1,0:T(8,128)(2,1)S(1)} %get-tuple-element.37.first, bf16[512,256]{1,0:T(8,128)(2,1)S(1)} %get-tuple-element.38.later), custom_call_target="tpu_custom_call" | custom-call | flops 1073741824 | bytes 4194304 | tf_op jit(solution)/shard_map/middle/pallas_call | solution.py:278
  14.5 0.0 collective-permute-done.4.refs_0_
  14.5 0.2 collective-permute-done.5.refs_1_
  14.7 1.1 %finish.2.refs_1_ = f32[32,64,256]{2,1,0:T(8,128)} custom-call(f32[1024,256]{1,0:T(8,128)S(1)} %get-tuple-element.41.own, s16[528,256]{1,0:T(8,128)(2,1)S(1)} %collective-permute-done.4.refs_0_, s16[528,256]{1,0:T(8,128)(2,1)S(1)} %collective-permute-done.5.refs_1_), custom_call_target="tpu_custom_call" | custom-call | flops 786432 | bytes 2097152 | tf_op jit(solution)/shard_map/finish/pallas_call | solution.py:321
  15.8 6.2 %collective-permute-done.3.refs_0_ = s16[1040,256]{1,0:T(8,128)(2,1)S(1)} collective-permute-done((s16[1040,256]{1,0:T(8,128)(2,1)S(1)}, s16[1040,256]{1,0:T(8,128)(2,1)S(1)}, u32[]{:S(2)}, u32[]{:S(2)}) %collective-permute-start.3) | collective-permute-done | bytes 532512 | tf_op jit(solution)/shard_map/ppermute | solution.py:346
  22.0 1.1 %finish.3 = f32[32,64,256]{2,1,0:T(8,128)} custom-call(f32[1024,256]{1,0:T(8,128)S(1)} %get-tuple-element.39.own, s16[1040,256]{1,0:T(8,128)(2,1)S(1)} %collective-permute-done.3.refs_0_, f32[32,64,256]{2,1,0:T(8,128)} %finish.2.refs_1_), custom_call_target="tpu_custom_call", output_to_operand_aliasing={{}: (2, {})} | custom-call | flops 786432 | bytes 2097152 | tf_op jit(solution)/shard_map/finish/pallas_call | solution.py:321
Async XLA Ops:
  1.1 4.4 %collective-permute-start = (bf16[128,256]{1,0:T(8,128)(2,1)S(1)}, bf16[128,256]{1,0:T(8,128)(2,1)S(1)}, u32[]{:S(2)}, u32[]{:S(2)}) collective-permute-start(bf16[128,256]{1,0:T(8,128)(2,1)S(1)} %get-tuple-element.28), channel_id=1, source_target_pairs={{0,1},{1,2},{2,3},{3,0},{4,5},{5,6},{6,7},{7,4},{8,9},{9,10},{10,1... | collective-permute-start | bytes 196616 | tf_op jit(solution)/shard_map/ppermute | solution.py:339
  3.0 3.4 %collective-permute-start.1 = (bf16[128,256]{1,0:T(8,128)(2,1)S(1)}, bf16[128,256]{1,0:T(8,128)(2,1)S(1)}, u32[]{:S(2)}, u32[]{:S(2)}) collective-permute-start(bf16[128,256]{1,0:T(8,128)(2,1)S(1)} %get-tuple-element.30), channel_id=1, source_target_pairs={{0,2},{1,3},{2,0},{3,1},{4,6},{5,7},{6,4},{7,5},{8,10},{9,11},{10,... | collective-permute-start | bytes 196616 | tf_op jit(solution)/shard_map/ppermute | solution.py:339
  3.2 3.8 %collective-permute-start.2 = (bf16[128,256]{1,0:T(8,128)(2,1)S(1)}, bf16[128,256]{1,0:T(8,128)(2,1)S(1)}, u32[]{:S(2)}, u32[]{:S(2)}) collective-permute-start(bf16[128,256]{1,0:T(8,128)(2,1)S(1)} %get-tuple-element.31), channel_id=1, source_target_pairs={{0,3},{1,0},{2,1},{3,2},{4,7},{5,4},{6,5},{7,6},{8,11},{9,8},{10,9... | collective-permute-start | bytes 196616 | tf_op jit(solution)/shard_map/ppermute | solution.py:339
  7.5 14.5 %collective-permute-start.3 = (s16[1040,256]{1,0:T(8,128)(2,1)S(1)}, s16[1040,256]{1,0:T(8,128)(2,1)S(1)}, u32[]{:S(2)}, u32[]{:S(2)}) collective-permute-start(s16[1040,256]{1,0:T(8,128)(2,1)S(1)} %get-tuple-element.40), channel_id=1, source_target_pairs={{0,31},{1,2},{2,1},{3,4},{4,3},{5,6},{6,5},{7,8},{8,7},{9,10},{10,... | collective-permute-start | bytes 1597448 | tf_op jit(solution)/shard_map/ppermute | solution.py:346
  12.5 2.0 %collective-permute-start.4 = (s16[528,256]{1,0:T(8,128)(2,1)S(1)}, s16[528,256]{1,0:T(8,128)(2,1)S(1)}, u32[]{:S(2)}, u32[]{:S(2)}) collective-permute-start(s16[528,256]{1,0:T(8,128)(2,1)S(1)} %get-tuple-element.43), channel_id=1, source_target_pairs={{0,1},{1,0},{2,3},{3,2},{4,5},{5,4},{6,7},{7,6},{8,9},{9,8},{10,11... | collective-permute-start | bytes 811016 | tf_op jit(solution)/shard_map/ppermute | solution.py:347
  13.1 1.6 %collective-permute-start.5 = (s16[528,256]{1,0:T(8,128)(2,1)S(1)}, s16[528,256]{1,0:T(8,128)(2,1)S(1)}, u32[]{:S(2)}, u32[]{:S(2)}) collective-permute-start(s16[528,256]{1,0:T(8,128)(2,1)S(1)} %get-tuple-element.44), channel_id=1, source_target_pairs={{0,1},{1,0},{2,3},{3,2},{4,5},{5,4},{6,7},{7,6},{8,9},{9,8},{10,11... | collective-permute-start | bytes 811016 | tf_op jit(solution)/shard_map/ppermute | solution.py:347

commit v10 on v9

--- a/solution.py
+++ b/solution.py
@@ -34,20 +34,16 @@
     return lax.rem(lax.axis_index("grp") * lax.axis_size("blk") + lax.axis_index("blk"), 2)
 
 
-def pick_kernel(members, capacity, ids, counts, source, slots, targets, *refs):
-    picked, (slot_list, target_list, blocks, id_list, count_list, sems) = refs[:members], refs[members:]
+def pick_kernel(members, capacity, ids, counts, source, *refs):
+    picked, (blocks, id_list, count_list, sems) = refs[:members], refs[members:]
     own = lax.axis_index("blk")
-    pairs = (
-        (ids, id_list),
-        (counts, count_list),
-        (source, blocks),
-        (slots, slot_list),
-        (targets, target_list),
-    )
+    rows = blocks.shape[0] // 2
+    parts = [pl.ds(n * rows, rows) for n in range(2)]
+    pairs = [(ids, id_list), (counts, count_list)] + [(source.at[part], blocks.at[part]) for part in parts]
     copies = [pltpu.make_async_copy(here, there, sems.at[n]) for n, (here, there) in enumerate(pairs)]
+    for n, copy in enumerate(copies):
+        copy.start(priority=n % 2)
     for copy in copies:
-        copy.start()
-    for copy in copies[:3]:
         copy.wait()
     for k in range(members):
         reader = lax.rem(own + k, members)
@@ -55,32 +51,28 @@
             start = pl.multiple_of(id_list[0, reader * capacity + j] * BLOCK, BLOCK)
             live = (j < count_list[0, reader]).astype(jnp.float32).astype(jnp.bfloat16)
             picked[k][j * BLOCK : (j + 1) * BLOCK] = blocks[pl.ds(start, BLOCK)] * live
-    for copy in copies[3:]:
-        copy.wait()
 
 
 def in_hbm(*arrays):
     return [pltpu.with_memory_space_constraint(x, pltpu.HBM) for x in arrays]
 
 
-def pick(members, capacity, send_ids, send_counts, source, slots, targets):
+def pick(members, capacity, send_ids, send_counts, source):
     shape = (capacity * BLOCK, COLS)
-    results = pl.pallas_call(
+    return pl.pallas_call(
         functools.partial(pick_kernel, members, capacity),
-        out_shape=[pltpu.VMEM(shape, jnp.bfloat16)] * members
-        + [pltpu.VMEM(slots.shape, jnp.int32), pltpu.VMEM(targets.shape, jnp.int32)],
-        in_specs=[ANY] * 5,
-        out_specs=[VMEM] * (members + 2),
+        out_shape=[pltpu.VMEM(shape, jnp.bfloat16)] * members,
+        in_specs=[ANY] * 3,
+        out_specs=[VMEM] * members,
         scratch_shapes=[
             pltpu.VMEM(source.shape, source.dtype),
             pltpu.SMEM(send_ids.shape, jnp.int32),
             pltpu.SMEM(send_counts.shape, jnp.int32),
-            pltpu.SemaphoreType.DMA((5,)),
+            pltpu.SemaphoreType.DMA((4,)),
         ],
         compiler_params=params(),
         name="pick",
-    )(*in_hbm(send_ids, send_counts, source, slots, targets))
-    return results[:members], results[members:]
+    )(*in_hbm(send_ids, send_counts, source))
 
 
 def lanes_of(k, members):
@@ -89,13 +81,17 @@
     return (EARLY + k) * CHUNK, (members + k) * CHUNK
 
 
-def spread_kernel(members, capacity, quarters, slots, targets, weights, *refs):
-    outs, (held, sems) = refs[:-2], refs[-2:]
+def spread_kernel(members, capacity, quarters, slots_here, targets_here, weights, *refs):
+    outs, (slots, targets, held, sems) = refs[:-4], refs[-4:]
     half = weights.shape[1] // 2
     parts = [held.at[:, pl.ds(n * half, half)] for n in range(2)]
     copies = [pltpu.make_async_copy(weights.at[:, pl.ds(n * half, half)], parts[n], sems.at[n]) for n in range(2)]
-    for copy in copies:
+    lists = ((slots_here, slots), (targets_here, targets))
+    lists = [pltpu.make_async_copy(here, there, sems.at[2 + n]) for n, (here, there) in enumerate(lists)]
+    for copy in lists + copies:
         copy.start()
+    for copy in lists:
+        copy.wait()
     own = lax.axis_index("blk")
     tiles = weights.shape[0]
     count = len(quarters)
@@ -151,16 +147,18 @@
     return pl.pallas_call(
         functools.partial(spread_kernel, members, capacity, quarters),
         out_shape=[pltpu.VMEM(shape, jnp.bfloat16)] * len(quarters),
-        in_specs=[VMEM] * 2 + [ANY],
+        in_specs=[ANY] * 3,
         out_specs=[VMEM] * len(quarters),
         scratch_shapes=[
+            pltpu.VMEM(slots.shape, jnp.int32),
+            pltpu.VMEM(targets.shape, jnp.int32),
             pltpu.VMEM(weights.shape, weights.dtype),
-            pltpu.SemaphoreType.DMA((2,)),
+            pltpu.SemaphoreType.DMA((4,)),
         ],
         compiler_params=params(),
         cost_estimate=cost(2 * members * EB * len(quarters) * 2 * tiles * 8192, 6 * 2**20),
         name="spread",
-    )(slots, targets, *in_hbm(weights))
+    )(*in_hbm(slots, targets, weights))
 
 
 def stacked(blocks, both):
@@ -350,9 +348,8 @@
 def body(source, send_ids, send_counts, tile_slot, tile_target, tile_weights):
     members = lax.axis_size("blk")
     capacity = send_ids.shape[1] // members
-    picked, tiles = pick(
-        members, capacity, send_ids, send_counts, source, tile_slot, tile_target
-    )
+    picked = pick(members, capacity, send_ids, send_counts, source)
+    tiles = (tile_slot, tile_target)
     blocks = [picked[0]] + [passed_along(picked[k], "blk", k) for k in range(1, members)]
     (left_across,) = spread(members, capacity, ((0, 3),), *tiles, tile_weights)
     sums, first = early(left_across, blocks[:EARLY])

time: 23.4 us -> 23.4 us (level)
  transfers between devices with their start and end apart: 6 -> 6, of which waited for: 4 -> 4; matrix products, arithmetic and copies ran while one was open for 0% -> 0% of each run, Pallas kernels for 38% -> 39%
where the time goes in v10:
time: 23.4 us; the launch traced here: 23.1 us
  Pallas kernels  11.7 us (50%)
  waiting for transfers between devices  7.26 us (31%)
  starting transfers between devices  4.06 us (17%)
    ppermute x1, waiting for transfers between devices, ring_swap(): lax.ppermute(shard, axes, [(i, (i + (1 if i % 2 else -1)) % count) for i...  6.12 us
    pallas_call x2, Pallas kernels, spread(): pl.pallas_call(functools.partial(spread_kernel, members, capacity, quarte...  5.32 us
    ppermute x3, starting transfers between devices, passed_along(): lax.ppermute(shard, axis, [(i, (i + by) % count) for i in range(count)])  2.3 us
    pallas_call x2, Pallas kernels, finish(): pl.pallas_call(functools.partial(finish_kernel, across, low, parts), out_...  2.21 us
    pallas_call x1, Pallas kernels, middle(): pl.pallas_call(middle_kernel, out_shape=[pltpu.VMEM((ROWS, COLS), jnp.flo...  1.27 us
    pallas_call x1, Pallas kernels, pick(): pl.pallas_call(functools.partial(pick_kernel, members, capacity), out_sha...  1.1 us
    ppermute x1, starting transfers between devices, ring_swap(): lax.ppermute(shard, axes, [(i, (i + (1 if i % 2 else -1)) % count) for i...  1.06 us
    ppermute x3, waiting for transfers between devices, passed_along(): lax.ppermute(shard, axis, [(i, (i + by) % count) for i in range(count)])  0.95 us
  transfers between devices with their start and end apart: 6, of which 4 were waited for; matrix products, arithmetic and copies ran while one was open for 0% of the time, Pallas kernels for 39%

profile of v10, /device:TPU:5, one launch (start us, length us, event | category | flops | bytes accessed | tf_op | source)
XLA Modules:
  0.0 23.1 jit_solution(11128993621102363443)
XLA Ops:
  0.0 1.1 %pick.1 = (bf16[128,256]{1,0:T(8,128)(2,1)S(1)}, bf16[128,256]{1,0:T(8,128)(2,1)S(1)}, bf16[128,256]{1,0:T(8,128)(2,1)S(1)}, bf16[128,256]{1,0:T(8,128)(2,1)S(1)}) custom-call(s32[1,8]{1,0:T(1,128)} %ids.1, s32[1,4]{1,0:T(1,128)} %counts.1, bf16[1024,256]{1,0:T(8,128)(2,1)} %source.1), custom_call_target="tpu_custom_call" | custom-call | tf_op jit(solution)/shard_map/pick/pallas_call | solution.py:62
  1.1 1.8 %collective-permute-start = (bf16[128,256]{1,0:T(8,128)(2,1)S(1)}, bf16[128,256]{1,0:T(8,128)(2,1)S(1)}, u32[]{:S(2)}, u32[]{:S(2)}) collective-permute-start(bf16[128,256]{1,0:T(8,128)(2,1)S(1)} %get-tuple-element.24), channel_id=1, source_target_pairs={{0,1},{1,2},{2,3},{3,0},{4,5},{5,6},{6,7},{7,4},{8,9},{9,10},{10,1... | collective-permute-start | bytes 196616 | tf_op jit(solution)/shard_map/ppermute | solution.py:337
  2.9 0.3 %collective-permute-start.1 = (bf16[128,256]{1,0:T(8,128)(2,1)S(1)}, bf16[128,256]{1,0:T(8,128)(2,1)S(1)}, u32[]{:S(2)}, u32[]{:S(2)}) collective-permute-start(bf16[128,256]{1,0:T(8,128)(2,1)S(1)} %get-tuple-element.26), channel_id=1, source_target_pairs={{0,2},{1,3},{2,0},{3,1},{4,6},{5,7},{6,4},{7,5},{8,10},{9,11},{10,... | collective-permute-start | bytes 196616 | tf_op jit(solution)/shard_map/ppermute | solution.py:337
  3.2 0.2 collective-permute-start.2
  3.4 2.1 %spread.2.left = bf16[1024,1024]{1,0:T(8,128)(2,1)S(1)} custom-call(s32[1,128]{1,0:T(1,128)} %slots_here.2, s32[1,128]{1,0:T(1,128)} %targets_here.2, bf16[128,4096]{1,0:T(8,128)(2,1)} %weights.3), custom_call_target="tpu_custom_call" | custom-call | flops 268435456 | bytes 6291456 | tf_op jit(solution)/shard_map/spread/pallas_call | solution.py:147
  5.5 0.0 collective-permute-done.refs_1_
  5.6 0.4 %early.1 = (f32[1024,256]{1,0:T(8,128)S(1)}, bf16[512,256]{1,0:T(8,128)(2,1)S(1)}) custom-call(bf16[1024,1024]{1,0:T(8,128)(2,1)S(1)} %spread.2.left, bf16[128,256]{1,0:T(8,128)(2,1)S(1)} %get-tuple-element.23.refs_0_, bf16[128,256]{1,0:T(8,128)(2,1)S(1)} %collective-permute-done.refs_1_), custom_call_target="tpu_custom_call" | custom-call | flops 268435456 | bytes 2097152 | tf_op jit(solution)/shard_map/early/pallas_call | solution.py:180
  6.0 0.3 %collective-permute-done.1.refs_0_ = bf16[128,256]{1,0:T(8,128)(2,1)S(1)} collective-permute-done((bf16[128,256]{1,0:T(8,128)(2,1)S(1)}, bf16[128,256]{1,0:T(8,128)(2,1)S(1)}, u32[]{:S(2)}, u32[]{:S(2)}) %collective-permute-start.1) | collective-permute-done | bytes 65568 | tf_op jit(solution)/shard_map/ppermute | solution.py:337
  6.3 0.6 %collective-permute-done.2.refs_1_ = bf16[128,256]{1,0:T(8,128)(2,1)S(1)} collective-permute-done((bf16[128,256]{1,0:T(8,128)(2,1)S(1)}, bf16[128,256]{1,0:T(8,128)(2,1)S(1)}, u32[]{:S(2)}, u32[]{:S(2)}) %collective-permute-start.2) | collective-permute-done | bytes 65568 | tf_op jit(solution)/shard_map/ppermute | solution.py:337
  6.9 0.5 %across.1 = (s16[1040,256]{1,0:T(8,128)(2,1)S(1)}, bf16[512,256]{1,0:T(8,128)(2,1)S(1)}) custom-call(bf16[1024,1024]{1,0:T(8,128)(2,1)S(1)} %spread.2.left, f32[1024,256]{1,0:T(8,128)S(1)} %get-tuple-element.25.sums, bf16[128,256]{1,0:T(8,128)(2,1)S(1)} %collective-permute-done.1.refs_0_, bf16[128,256]{1,0:T(8,128)(2,1)S(1)} %collective-permute-done.2.refs_1_), custom_call_target="tpu_custom_call" | custom-call | flops 268435456 | bytes 2097152 | tf_op jit(solution)/shard_map/across/pallas_call | solution.py:236
  7.4 1.1 %collective-permute-start.3 = (s16[1040,256]{1,0:T(8,128)(2,1)S(1)}, s16[1040,256]{1,0:T(8,128)(2,1)S(1)}, u32[]{:S(2)}, u32[]{:S(2)}) collective-permute-start(s16[1040,256]{1,0:T(8,128)(2,1)S(1)} %get-tuple-element.36), channel_id=1, source_target_pairs={{0,31},{1,2},{2,1},{3,4},{4,3},{5,6},{6,5},{7,8},{8,7},{9,10},{10,... | collective-permute-start | bytes 1597448 | tf_op jit(solution)/shard_map/ppermute | solution.py:344
  8.5 3.2 %spread.3 = (bf16[1024,1024]{1,0:T(8,128)(2,1)S(1)}, bf16[1024,1024]{1,0:T(8,128)(2,1)S(1)}, bf16[1024,1024]{1,0:T(8,128)(2,1)S(1)}) custom-call(s32[1,128]{1,0:T(1,128)} %slots_here.2, s32[1,128]{1,0:T(1,128)} %targets_here.2, bf16[128,4096]{1,0:T(8,128)(2,1)} %weights.3), custom_call_target="tpu_custom_call" | custom-call | flops 805306368 | bytes 6291456 | tf_op jit(solution)/shard_map/spread/pallas_call | solution.py:147
  11.7 0.8 %chip.1 = (s16[528,256]{1,0:T(8,128)(2,1)S(1)}, s16[528,256]{1,0:T(8,128)(2,1)S(1)}) custom-call(bf16[1024,1024]{1,0:T(8,128)(2,1)S(1)} %get-tuple-element.38.left, bf16[512,256]{1,0:T(8,128)(2,1)S(1)} %get-tuple-element.33.first, bf16[512,256]{1,0:T(8,128)(2,1)S(1)} %get-tuple-element.34.later), custom_call_target="tpu_custom_call" | custom-call | flops 536870912 | bytes 2097152 | tf_op jit(solution)/shard_map/chip/pallas_call | solution.py:256
  12.5 0.6 %collective-permute-start.4 = (s16[528,256]{1,0:T(8,128)(2,1)S(1)}, s16[528,256]{1,0:T(8,128)(2,1)S(1)}, u32[]{:S(2)}, u32[]{:S(2)}) collective-permute-start(s16[528,256]{1,0:T(8,128)(2,1)S(1)} %get-tuple-element.39), channel_id=1, source_target_pairs={{0,1},{1,0},{2,3},{3,2},{4,5},{5,4},{6,7},{7,6},{8,9},{9,8},{10,11... | collective-permute-start | bytes 811016 | tf_op jit(solution)/shard_map/ppermute | solution.py:345
  13.2 0.1 collective-permute-start.5
  13.2 1.3 %middle.1 = (f32[1024,256]{1,0:T(8,128)S(1)}, f32[1024,256]{1,0:T(8,128)S(1)}) custom-call(bf16[1024,1024]{1,0:T(8,128)(2,1)S(1)} %get-tuple-element.31.left_0, bf16[1024,1024]{1,0:T(8,128)(2,1)S(1)} %get-tuple-element.32.left_1, bf16[512,256]{1,0:T(8,128)(2,1)S(1)} %get-tuple-element.33.first, bf16[512,256]{1,0:T(8,128)(2,1)S(1)} %get-tuple-element.34.later), custom_call_target="tpu_custom_call" | custom-call | flops 1073741824 | bytes 4194304 | tf_op jit(solution)/shard_map/middle/pallas_call | solution.py:276
  14.5 0.0 collective-permute-done.4.refs_0_
  14.5 0.2 collective-permute-done.5.refs_1_
  14.7 1.1 %finish.2.refs_1_ = f32[32,64,256]{2,1,0:T(8,128)} custom-call(f32[1024,256]{1,0:T(8,128)S(1)} %get-tuple-element.37.own, s16[528,256]{1,0:T(8,128)(2,1)S(1)} %collective-permute-done.4.refs_0_, s16[528,256]{1,0:T(8,128)(2,1)S(1)} %collective-permute-done.5.refs_1_), custom_call_target="tpu_custom_call" | custom-call | flops 786432 | bytes 2097152 | tf_op jit(solution)/shard_map/finish/pallas_call | solution.py:319
  15.8 6.1 %collective-permute-done.3.refs_0_ = s16[1040,256]{1,0:T(8,128)(2,1)S(1)} collective-permute-done((s16[1040,256]{1,0:T(8,128)(2,1)S(1)}, s16[1040,256]{1,0:T(8,128)(2,1)S(1)}, u32[]{:S(2)}, u32[]{:S(2)}) %collective-permute-start.3) | collective-permute-done | bytes 532512 | tf_op jit(solution)/shard_map/ppermute | solution.py:344
  21.9 1.1 %finish.3 = f32[32,64,256]{2,1,0:T(8,128)} custom-call(f32[1024,256]{1,0:T(8,128)S(1)} %get-tuple-element.35.own, s16[1040,256]{1,0:T(8,128)(2,1)S(1)} %collective-permute-done.3.refs_0_, f32[32,64,256]{2,1,0:T(8,128)} %finish.2.refs_1_), custom_call_target="tpu_custom_call", output_to_operand_aliasing={{}: (2, {})} | custom-call | flops 786432 | bytes 2097152 | tf_op jit(solution)/shard_map/finish/pallas_call | solution.py:319
Async XLA Ops:
  1.1 4.4 %collective-permute-start = (bf16[128,256]{1,0:T(8,128)(2,1)S(1)}, bf16[128,256]{1,0:T(8,128)(2,1)S(1)}, u32[]{:S(2)}, u32[]{:S(2)}) collective-permute-start(bf16[128,256]{1,0:T(8,128)(2,1)S(1)} %get-tuple-element.24), channel_id=1, source_target_pairs={{0,1},{1,2},{2,3},{3,0},{4,5},{5,6},{6,7},{7,4},{8,9},{9,10},{10,1... | collective-permute-start | bytes 196616 | tf_op jit(solution)/shard_map/ppermute | solution.py:337
  2.9 3.4 %collective-permute-start.1 = (bf16[128,256]{1,0:T(8,128)(2,1)S(1)}, bf16[128,256]{1,0:T(8,128)(2,1)S(1)}, u32[]{:S(2)}, u32[]{:S(2)}) collective-permute-start(bf16[128,256]{1,0:T(8,128)(2,1)S(1)} %get-tuple-element.26), channel_id=1, source_target_pairs={{0,2},{1,3},{2,0},{3,1},{4,6},{5,7},{6,4},{7,5},{8,10},{9,11},{10,... | collective-permute-start | bytes 196616 | tf_op jit(solution)/shard_map/ppermute | solution.py:337
  3.2 3.8 %collective-permute-start.2 = (bf16[128,256]{1,0:T(8,128)(2,1)S(1)}, bf16[128,256]{1,0:T(8,128)(2,1)S(1)}, u32[]{:S(2)}, u32[]{:S(2)}) collective-permute-start(bf16[128,256]{1,0:T(8,128)(2,1)S(1)} %get-tuple-element.27), channel_id=1, source_target_pairs={{0,3},{1,0},{2,1},{3,2},{4,7},{5,4},{6,5},{7,6},{8,11},{9,8},{10,9... | collective-permute-start | bytes 196616 | tf_op jit(solution)/shard_map/ppermute | solution.py:337
  7.4 14.5 %collective-permute-start.3 = (s16[1040,256]{1,0:T(8,128)(2,1)S(1)}, s16[1040,256]{1,0:T(8,128)(2,1)S(1)}, u32[]{:S(2)}, u32[]{:S(2)}) collective-permute-start(s16[1040,256]{1,0:T(8,128)(2,1)S(1)} %get-tuple-element.36), channel_id=1, source_target_pairs={{0,31},{1,2},{2,1},{3,4},{4,3},{5,6},{6,5},{7,8},{8,7},{9,10},{10,... | collective-permute-start | bytes 1597448 | tf_op jit(solution)/shard_map/ppermute | solution.py:344
  12.5 2.0 %collective-permute-start.4 = (s16[528,256]{1,0:T(8,128)(2,1)S(1)}, s16[528,256]{1,0:T(8,128)(2,1)S(1)}, u32[]{:S(2)}, u32[]{:S(2)}) collective-permute-start(s16[528,256]{1,0:T(8,128)(2,1)S(1)} %get-tuple-element.39), channel_id=1, source_target_pairs={{0,1},{1,0},{2,3},{3,2},{4,5},{5,4},{6,7},{7,6},{8,9},{9,8},{10,11... | collective-permute-start | bytes 811016 | tf_op jit(solution)/shard_map/ppermute | solution.py:345
  13.2 1.6 %collective-permute-start.5 = (s16[528,256]{1,0:T(8,128)(2,1)S(1)}, s16[528,256]{1,0:T(8,128)(2,1)S(1)}, u32[]{:S(2)}, u32[]{:S(2)}) collective-permute-start(s16[528,256]{1,0:T(8,128)(2,1)S(1)} %get-tuple-element.40), channel_id=1, source_target_pairs={{0,1},{1,0},{2,3},{3,2},{4,5},{5,4},{6,7},{7,6},{8,9},{9,8},{10,11... | collective-permute-start | bytes 811016 | tf_op jit(solution)/shard_map/ppermute | solution.py:345

commit v11 on v10

--- a/solution.py
+++ b/solution.py
@@ -357,8 +357,9 @@
     message_across = ring_swap(message_across, True)
     tiles, later = lax.optimization_barrier((tiles, later))
     left_chip, *own_left = spread(members, capacity, ((3, 0), (1, 2), (2, 1)), *tiles, tile_weights)
+    own_across, own_chip = middle(*own_left, first, later)
+    own_across, left_chip = lax.optimization_barrier((own_across, left_chip))
     messages_chip = [ring_swap(message, False) for message in chip_edge(PARTS, left_chip, first, later)]
-    own_across, own_chip = middle(*own_left, first, later)
     out = finish(False, 0, PARTS, own_chip, messages_chip)
     out = finish(True, 0, ACROSS, own_across, [message_across], out)
     return out.reshape(2 * ROWS, COLS)

time: 23.4 us -> 23.6 us (level)
  the two profiles are of different devices: /device:TPU:5 before, /device:TPU:0 now
where the time goes in v11:
time: 23.6 us; the launch traced here: 23.4 us
  Pallas kernels  11.7 us (50%)
  starting transfers between devices  10.2 us (43%)
  waiting for transfers between devices  1.43 us (6%)
    pallas_call x2, Pallas kernels, spread(): pl.pallas_call(functools.partial(spread_kernel, members, capacity, quarte...  5.35 us
    ppermute x1, starting transfers between devices, ring_swap(): lax.ppermute(shard, axes, [(i, (i + (1 if i % 2 else -1)) % count) for i...  5.19 us
    ppermute x3, starting transfers between devices, passed_along(): lax.ppermute(shard, axis, [(i, (i + by) % count) for i in range(count)])  4.46 us
    pallas_call x2, Pallas kernels, finish(): pl.pallas_call(functools.partial(finish_kernel, across, low, parts), out_...  2.2 us
    ppermute x2, waiting for transfers between devices, ring_swap(): return lax.ppermute(shard, axes, [(i, i ^ 1) for i in range(count)])  1.42 us
    pallas_call x1, Pallas kernels, middle(): pl.pallas_call(middle_kernel, out_shape=[pltpu.VMEM((ROWS, COLS), jnp.flo...  1.24 us
    pallas_call x1, Pallas kernels, pick(): pl.pallas_call(functools.partial(pick_kernel, members, capacity), out_sha...  1.1 us
    pallas_call x1, Pallas kernels, chip_edge(): pl.pallas_call(functools.partial(chip_kernel, parts), out_shape=[message_...  0.83 us
  transfers between devices with their start and end apart: 6, of which 2 were waited for; matrix products, arithmetic and copies ran while one was open for 0% of the time, Pallas kernels for 38%

profile of v11, /device:TPU:0, one launch (start us, length us, event | category | flops | bytes accessed | tf_op | source)
XLA Modules:
  0.0 23.4 jit_solution(12669387026077107165)
XLA Ops:
  0.0 1.1 %pick.1 = (bf16[128,256]{1,0:T(8,128)(2,1)S(1)}, bf16[128,256]{1,0:T(8,128)(2,1)S(1)}, bf16[128,256]{1,0:T(8,128)(2,1)S(1)}, bf16[128,256]{1,0:T(8,128)(2,1)S(1)}) custom-call(s32[1,8]{1,0:T(1,128)} %ids.1, s32[1,4]{1,0:T(1,128)} %counts.1, bf16[1024,256]{1,0:T(8,128)(2,1)} %source.1), custom_call_target="tpu_custom_call" | custom-call | tf_op jit(solution)/shard_map/pick/pallas_call | solution.py:62
  1.1 0.5 %collective-permute-start = (bf16[128,256]{1,0:T(8,128)(2,1)S(1)}, bf16[128,256]{1,0:T(8,128)(2,1)S(1)}, u32[]{:S(2)}, u32[]{:S(2)}) collective-permute-start(bf16[128,256]{1,0:T(8,128)(2,1)S(1)} %get-tuple-element.26), channel_id=1, source_target_pairs={{0,1},{1,2},{2,3},{3,0},{4,5},{5,6},{6,7},{7,4},{8,9},{9,10},{10,1... | collective-permute-start | bytes 196616 | tf_op jit(solution)/shard_map/ppermute | solution.py:337
  1.6 2.6 %collective-permute-start.1 = (bf16[128,256]{1,0:T(8,128)(2,1)S(1)}, bf16[128,256]{1,0:T(8,128)(2,1)S(1)}, u32[]{:S(2)}, u32[]{:S(2)}) collective-permute-start(bf16[128,256]{1,0:T(8,128)(2,1)S(1)} %get-tuple-element.28), channel_id=1, source_target_pairs={{0,2},{1,3},{2,0},{3,1},{4,6},{5,7},{6,4},{7,5},{8,10},{9,11},{10,... | collective-permute-start | bytes 196616 | tf_op jit(solution)/shard_map/ppermute | solution.py:337
  4.2 1.4 %collective-permute-start.2 = (bf16[128,256]{1,0:T(8,128)(2,1)S(1)}, bf16[128,256]{1,0:T(8,128)(2,1)S(1)}, u32[]{:S(2)}, u32[]{:S(2)}) collective-permute-start(bf16[128,256]{1,0:T(8,128)(2,1)S(1)} %get-tuple-element.29), channel_id=1, source_target_pairs={{0,3},{1,0},{2,1},{3,2},{4,7},{5,4},{6,5},{7,6},{8,11},{9,8},{10,9... | collective-permute-start | bytes 196616 | tf_op jit(solution)/shard_map/ppermute | solution.py:337
  5.6 2.1 %spread.2.left = bf16[1024,1024]{1,0:T(8,128)(2,1)S(1)} custom-call(s32[1,128]{1,0:T(1,128)} %slots_here.2, s32[1,128]{1,0:T(1,128)} %targets_here.2, bf16[128,4096]{1,0:T(8,128)(2,1)} %weights.3), custom_call_target="tpu_custom_call" | custom-call | flops 268435456 | bytes 6291456 | tf_op jit(solution)/shard_map/spread/pallas_call | solution.py:147
  7.7 0.0 collective-permute-done.refs_1_
  7.7 0.4 %early.1 = (f32[1024,256]{1,0:T(8,128)S(1)}, bf16[512,256]{1,0:T(8,128)(2,1)S(1)}) custom-call(bf16[1024,1024]{1,0:T(8,128)(2,1)S(1)} %spread.2.left, bf16[128,256]{1,0:T(8,128)(2,1)S(1)} %get-tuple-element.25.refs_0_, bf16[128,256]{1,0:T(8,128)(2,1)S(1)} %collective-permute-done.refs_1_), custom_call_target="tpu_custom_call" | custom-call | flops 268435456 | bytes 2097152 | tf_op jit(solution)/shard_map/early/pallas_call | solution.py:180
  8.2 0.0 collective-permute-done.1.refs_0_
  8.2 0.0 collective-permute-done.2.refs_1_
  8.2 0.5 %across.1 = (s16[1040,256]{1,0:T(8,128)(2,1)S(1)}, bf16[512,256]{1,0:T(8,128)(2,1)S(1)}) custom-call(bf16[1024,1024]{1,0:T(8,128)(2,1)S(1)} %spread.2.left, f32[1024,256]{1,0:T(8,128)S(1)} %get-tuple-element.27.sums, bf16[128,256]{1,0:T(8,128)(2,1)S(1)} %collective-permute-done.1.refs_0_, bf16[128,256]{1,0:T(8,128)(2,1)S(1)} %collective-permute-done.2.refs_1_), custom_call_target="tpu_custom_call" | custom-call | flops 268435456 | bytes 2097152 | tf_op jit(solution)/shard_map/across/pallas_call | solution.py:236
  8.7 5.2 %collective-permute-start.3 = (s16[1040,256]{1,0:T(8,128)(2,1)S(1)}, s16[1040,256]{1,0:T(8,128)(2,1)S(1)}, u32[]{:S(2)}, u32[]{:S(2)}) collective-permute-start(s16[1040,256]{1,0:T(8,128)(2,1)S(1)} %get-tuple-element.40), channel_id=1, source_target_pairs={{0,31},{1,2},{2,1},{3,4},{4,3},{5,6},{6,5},{7,8},{8,7},{9,10},{10,... | collective-permute-start | bytes 1597448 | tf_op jit(solution)/shard_map/ppermute | solution.py:344
  13.9 3.2 %spread.3 = (bf16[1024,1024]{1,0:T(8,128)(2,1)S(1)}, bf16[1024,1024]{1,0:T(8,128)(2,1)S(1)}, bf16[1024,1024]{1,0:T(8,128)(2,1)S(1)}) custom-call(s32[1,128]{1,0:T(1,128)} %slots_here.2, s32[1,128]{1,0:T(1,128)} %targets_here.2, bf16[128,4096]{1,0:T(8,128)(2,1)} %weights.3), custom_call_target="tpu_custom_call" | custom-call | flops 805306368 | bytes 6291456 | tf_op jit(solution)/shard_map/spread/pallas_call | solution.py:147
  17.1 1.2 %middle.1 = (f32[1024,256]{1,0:T(8,128)S(1)}, f32[1024,256]{1,0:T(8,128)S(1)}) custom-call(bf16[1024,1024]{1,0:T(8,128)(2,1)S(1)} %get-tuple-element.33.left_0, bf16[1024,1024]{1,0:T(8,128)(2,1)S(1)} %get-tuple-element.34.left_1, bf16[512,256]{1,0:T(8,128)(2,1)S(1)} %get-tuple-element.35.first, bf16[512,256]{1,0:T(8,128)(2,1)S(1)} %get-tuple-element.36.later), custom_call_target="tpu_custom_call" | custom-call | flops 1073741824 | bytes 4194304 | tf_op jit(solution)/shard_map/middle/pallas_call | solution.py:276
  18.3 0.8 %chip.1 = (s16[528,256]{1,0:T(8,128)(2,1)S(1)}, s16[528,256]{1,0:T(8,128)(2,1)S(1)}) custom-call(bf16[1024,1024]{1,0:T(8,128)(2,1)S(1)} %get-tuple-element.42.left, bf16[512,256]{1,0:T(8,128)(2,1)S(1)} %get-tuple-element.35.first, bf16[512,256]{1,0:T(8,128)(2,1)S(1)} %get-tuple-element.36.later), custom_call_target="tpu_custom_call" | custom-call | flops 536870912 | bytes 2097152 | tf_op jit(solution)/shard_map/chip/pallas_call | solution.py:256
  19.2 0.1 collective-permute-start.4
  19.3 0.5 %collective-permute-start.5 = (s16[528,256]{1,0:T(8,128)(2,1)S(1)}, s16[528,256]{1,0:T(8,128)(2,1)S(1)}, u32[]{:S(2)}, u32[]{:S(2)}) collective-permute-start(s16[528,256]{1,0:T(8,128)(2,1)S(1)} %get-tuple-element.44), channel_id=1, source_target_pairs={{0,1},{1,0},{2,3},{3,2},{4,5},{5,4},{6,7},{7,6},{8,9},{9,8},{10,11... | collective-permute-start | bytes 811016 | tf_op jit(solution)/shard_map/ppermute | solution.py:345
  19.8 1.0 %collective-permute-done.4.refs_0_ = s16[528,256]{1,0:T(8,128)(2,1)S(1)} collective-permute-done((s16[528,256]{1,0:T(8,128)(2,1)S(1)}, s16[528,256]{1,0:T(8,128)(2,1)S(1)}, u32[]{:S(2)}, u32[]{:S(2)}) %collective-permute-start.4) | collective-permute-done | bytes 270368 | tf_op jit(solution)/shard_map/ppermute | solution.py:345
  20.8 0.4 %collective-permute-done.5.refs_1_ = s16[528,256]{1,0:T(8,128)(2,1)S(1)} collective-permute-done((s16[528,256]{1,0:T(8,128)(2,1)S(1)}, s16[528,256]{1,0:T(8,128)(2,1)S(1)}, u32[]{:S(2)}, u32[]{:S(2)}) %collective-permute-start.5) | collective-permute-done | bytes 270368 | tf_op jit(solution)/shard_map/ppermute | solution.py:345
  21.2 1.1 %finish.2.refs_1_ = f32[32,64,256]{2,1,0:T(8,128)} custom-call(f32[1024,256]{1,0:T(8,128)S(1)} %get-tuple-element.41.own, s16[528,256]{1,0:T(8,128)(2,1)S(1)} %collective-permute-done.4.refs_0_, s16[528,256]{1,0:T(8,128)(2,1)S(1)} %collective-permute-done.5.refs_1_), custom_call_target="tpu_custom_call" | custom-call | flops 786432 | bytes 2097152 | tf_op jit(solution)/shard_map/finish/pallas_call | solution.py:319
  22.3 0.0 collective-permute-done.3.refs_0_
  22.3 1.1 %finish.3 = f32[32,64,256]{2,1,0:T(8,128)} custom-call(f32[1024,256]{1,0:T(8,128)S(1)} %get-tuple-element.39.own, s16[1040,256]{1,0:T(8,128)(2,1)S(1)} %collective-permute-done.3.refs_0_, f32[32,64,256]{2,1,0:T(8,128)} %finish.2.refs_1_), custom_call_target="tpu_custom_call", output_to_operand_aliasing={{}: (2, {})} | custom-call | flops 786432 | bytes 2097152 | tf_op jit(solution)/shard_map/finish/pallas_call | solution.py:319
Async XLA Ops:
  1.1 6.6 %collective-permute-start = (bf16[128,256]{1,0:T(8,128)(2,1)S(1)}, bf16[128,256]{1,0:T(8,128)(2,1)S(1)}, u32[]{:S(2)}, u32[]{:S(2)}) collective-permute-start(bf16[128,256]{1,0:T(8,128)(2,1)S(1)} %get-tuple-element.26), channel_id=1, source_target_pairs={{0,1},{1,2},{2,3},{3,0},{4,5},{5,6},{6,7},{7,4},{8,9},{9,10},{10,1... | collective-permute-start | bytes 196616 | tf_op jit(solution)/shard_map/ppermute | solution.py:337
  1.6 6.6 %collective-permute-start.1 = (bf16[128,256]{1,0:T(8,128)(2,1)S(1)}, bf16[128,256]{1,0:T(8,128)(2,1)S(1)}, u32[]{:S(2)}, u32[]{:S(2)}) collective-permute-start(bf16[128,256]{1,0:T(8,128)(2,1)S(1)} %get-tuple-element.28), channel_id=1, source_target_pairs={{0,2},{1,3},{2,0},{3,1},{4,6},{5,7},{6,4},{7,5},{8,10},{9,11},{10,... | collective-permute-start | bytes 196616 | tf_op jit(solution)/shard_map/ppermute | solution.py:337
  4.2 4.0 %collective-permute-start.2 = (bf16[128,256]{1,0:T(8,128)(2,1)S(1)}, bf16[128,256]{1,0:T(8,128)(2,1)S(1)}, u32[]{:S(2)}, u32[]{:S(2)}) collective-permute-start(bf16[128,256]{1,0:T(8,128)(2,1)S(1)} %get-tuple-element.29), channel_id=1, source_target_pairs={{0,3},{1,0},{2,1},{3,2},{4,7},{5,4},{6,5},{7,6},{8,11},{9,8},{10,9... | collective-permute-start | bytes 196616 | tf_op jit(solution)/shard_map/ppermute | solution.py:337
  8.7 13.6 %collective-permute-start.3 = (s16[1040,256]{1,0:T(8,128)(2,1)S(1)}, s16[1040,256]{1,0:T(8,128)(2,1)S(1)}, u32[]{:S(2)}, u32[]{:S(2)}) collective-permute-start(s16[1040,256]{1,0:T(8,128)(2,1)S(1)} %get-tuple-element.40), channel_id=1, source_target_pairs={{0,31},{1,2},{2,1},{3,4},{4,3},{5,6},{6,5},{7,8},{8,7},{9,10},{10,... | collective-permute-start | bytes 1597448 | tf_op jit(solution)/shard_map/ppermute | solution.py:344
  19.2 1.6 %collective-permute-start.4 = (s16[528,256]{1,0:T(8,128)(2,1)S(1)}, s16[528,256]{1,0:T(8,128)(2,1)S(1)}, u32[]{:S(2)}, u32[]{:S(2)}) collective-permute-start(s16[528,256]{1,0:T(8,128)(2,1)S(1)} %get-tuple-element.43), channel_id=1, source_target_pairs={{0,1},{1,0},{2,3},{3,2},{4,5},{5,4},{6,7},{7,6},{8,9},{9,8},{10,11... | collective-permute-start | bytes 811016 | tf_op jit(solution)/shard_map/ppermute | solution.py:345
  19.3 1.9 %collective-permute-start.5 = (s16[528,256]{1,0:T(8,128)(2,1)S(1)}, s16[528,256]{1,0:T(8,128)(2,1)S(1)}, u32[]{:S(2)}, u32[]{:S(2)}) collective-permute-start(s16[528,256]{1,0:T(8,128)(2,1)S(1)} %get-tuple-element.44), channel_id=1, source_target_pairs={{0,1},{1,0},{2,3},{3,2},{4,5},{5,4},{6,7},{7,6},{8,9},{9,8},{10,11... | collective-permute-start | bytes 811016 | tf_op jit(solution)/shard_map/ppermute | solution.py:345

commit v12 on v9

--- a/solution.py
+++ b/solution.py
@@ -12,7 +12,7 @@
 EB = 16
 CHUNK = 2 * BLOCK
 ROWS = EB * BLOCK
-GROUP = 64
+GROUP = 128
 EARLY = 2
 ACROSS = (ROWS,)
 PARTS = (ROWS // 2, ROWS // 2)

time: 23.4 us -> 23.5 us (level)
  no operation moved by 1% of the time
where the time goes in v12:
time: 23.5 us; the launch traced here: 23.1 us
  Pallas kernels  11.6 us (49%)
  waiting for transfers between devices  7.37 us (31%)
  starting transfers between devices  4.05 us (17%)
    ppermute x1, waiting for transfers between devices, ring_swap(): lax.ppermute(shard, axes, [(i, (i + (1 if i % 2 else -1)) % count) for i...  6.18 us
    pallas_call x2, Pallas kernels, spread(): pl.pallas_call(functools.partial(spread_kernel, members, capacity, quarte...  5.24 us
    ppermute x3, starting transfers between devices, passed_along(): lax.ppermute(shard, axis, [(i, (i + by) % count) for i in range(count)])  2.3 us
    pallas_call x2, Pallas kernels, finish(): pl.pallas_call(functools.partial(finish_kernel, across, low, parts), out_...  2.2 us
    pallas_call x1, Pallas kernels, middle(): pl.pallas_call(middle_kernel, out_shape=[pltpu.VMEM((ROWS, COLS), jnp.flo...  1.26 us
    pallas_call x1, Pallas kernels, pick(): pl.pallas_call(functools.partial(pick_kernel, members, capacity), out_sha...  1.13 us
    ppermute x1, starting transfers between devices, ring_swap(): lax.ppermute(shard, axes, [(i, (i + (1 if i % 2 else -1)) % count) for i...  1.05 us
    ppermute x3, waiting for transfers between devices, passed_along(): lax.ppermute(shard, axis, [(i, (i + by) % count) for i in range(count)])  0.99 us
  transfers between devices with their start and end apart: 6, of which 4 were waited for; matrix products, arithmetic and copies ran while one was open for 0% of the time, Pallas kernels for 38%

profile of v12, /device:TPU:5, one launch (start us, length us, event | category | flops | bytes accessed | tf_op | source)
XLA Modules:
  0.0 23.1 jit_solution(18149548246297008263)
XLA Ops:
  0.0 1.1 %pick.1 = (bf16[128,256]{1,0:T(8,128)(2,1)S(1)}, bf16[128,256]{1,0:T(8,128)(2,1)S(1)}, bf16[128,256]{1,0:T(8,128)(2,1)S(1)}, bf16[128,256]{1,0:T(8,128)(2,1)S(1)...) custom-call(s32[1,8]{1,0:T(1,128)} %ids.1, s32[1,4]{1,0:T(1,128)} %counts.1, bf16[1024,256]{1,0:T(8,128)(2,1)} %source.1, ...), custom_call_target="tpu_custom_call" | custom-call | tf_op jit(solution)/shard_map/pick/pallas_call | solution.py:68
  1.1 1.8 %collective-permute-start = (bf16[128,256]{1,0:T(8,128)(2,1)S(1)}, bf16[128,256]{1,0:T(8,128)(2,1)S(1)}, u32[]{:S(2)}, u32[]{:S(2)}) collective-permute-start(bf16[128,256]{1,0:T(8,128)(2,1)S(1)} %get-tuple-element.28), channel_id=1, source_target_pairs={{0,1},{1,2},{2,3},{3,0},{4,5},{5,6},{6,7},{7,4},{8,9},{9,10},{10,1... | collective-permute-start | bytes 196616 | tf_op jit(solution)/shard_map/ppermute | solution.py:339
  3.0 0.3 %collective-permute-start.1 = (bf16[128,256]{1,0:T(8,128)(2,1)S(1)}, bf16[128,256]{1,0:T(8,128)(2,1)S(1)}, u32[]{:S(2)}, u32[]{:S(2)}) collective-permute-start(bf16[128,256]{1,0:T(8,128)(2,1)S(1)} %get-tuple-element.30), channel_id=1, source_target_pairs={{0,2},{1,3},{2,0},{3,1},{4,6},{5,7},{6,4},{7,5},{8,10},{9,11},{10,... | collective-permute-start | bytes 196616 | tf_op jit(solution)/shard_map/ppermute | solution.py:339
  3.2 0.2 collective-permute-start.2
  3.4 2.1 %spread.2.left = bf16[1024,1024]{1,0:T(8,128)(2,1)S(1)} custom-call(s32[1,128]{1,0:T(1,128)S(1)} %get-tuple-element.33.slots, s32[1,128]{1,0:T(1,128)S(1)} %get-tuple-element.34.targets, bf16[128,4096]{1,0:T(8,128)(2,1)} %weights.3), custom_call_target="tpu_custom_call" | custom-call | flops 268435456 | bytes 6291456 | tf_op jit(solution)/shard_map/spread/pallas_call | solution.py:151
  5.5 0.0 collective-permute-done.refs_1_
  5.5 0.4 %early.1 = (f32[1024,256]{1,0:T(8,128)S(1)}, bf16[512,256]{1,0:T(8,128)(2,1)S(1)}) custom-call(bf16[1024,1024]{1,0:T(8,128)(2,1)S(1)} %spread.2.left, bf16[128,256]{1,0:T(8,128)(2,1)S(1)} %get-tuple-element.27.refs_0_, bf16[128,256]{1,0:T(8,128)(2,1)S(1)} %collective-permute-done.refs_1_), custom_call_target="tpu_custom_call" | custom-call | flops 268435456 | bytes 2097152 | tf_op jit(solution)/shard_map/early/pallas_call | solution.py:182
  6.0 0.4 %collective-permute-done.1.refs_0_ = bf16[128,256]{1,0:T(8,128)(2,1)S(1)} collective-permute-done((bf16[128,256]{1,0:T(8,128)(2,1)S(1)}, bf16[128,256]{1,0:T(8,128)(2,1)S(1)}, u32[]{:S(2)}, u32[]{:S(2)}) %collective-permute-start.1) | collective-permute-done | bytes 65568 | tf_op jit(solution)/shard_map/ppermute | solution.py:339
  6.4 0.6 %collective-permute-done.2.refs_1_ = bf16[128,256]{1,0:T(8,128)(2,1)S(1)} collective-permute-done((bf16[128,256]{1,0:T(8,128)(2,1)S(1)}, bf16[128,256]{1,0:T(8,128)(2,1)S(1)}, u32[]{:S(2)}, u32[]{:S(2)}) %collective-permute-start.2) | collective-permute-done | bytes 65568 | tf_op jit(solution)/shard_map/ppermute | solution.py:339
  7.0 0.5 %across.1 = (s16[1040,256]{1,0:T(8,128)(2,1)S(1)}, bf16[512,256]{1,0:T(8,128)(2,1)S(1)}) custom-call(bf16[1024,1024]{1,0:T(8,128)(2,1)S(1)} %spread.2.left, f32[1024,256]{1,0:T(8,128)S(1)} %get-tuple-element.29.sums, bf16[128,256]{1,0:T(8,128)(2,1)S(1)} %collective-permute-done.1.refs_0_, bf16[128,256]{1,0:T(8,128)(2,1)S(1)} %collective-permute-done.2.refs_1_), custom_call_target="tpu_custom_call" | custom-call | flops 268435456 | bytes 2097152 | tf_op jit(solution)/shard_map/across/pallas_call | solution.py:238
  7.5 1.1 %collective-permute-start.3 = (s16[1040,256]{1,0:T(8,128)(2,1)S(1)}, s16[1040,256]{1,0:T(8,128)(2,1)S(1)}, u32[]{:S(2)}, u32[]{:S(2)}) collective-permute-start(s16[1040,256]{1,0:T(8,128)(2,1)S(1)} %get-tuple-element.40), channel_id=1, source_target_pairs={{0,31},{1,2},{2,1},{3,4},{4,3},{5,6},{6,5},{7,8},{8,7},{9,10},{10,... | collective-permute-start | bytes 1597448 | tf_op jit(solution)/shard_map/ppermute | solution.py:346
  8.5 3.1 %spread.3 = (bf16[1024,1024]{1,0:T(8,128)(2,1)S(1)}, bf16[1024,1024]{1,0:T(8,128)(2,1)S(1)}, bf16[1024,1024]{1,0:T(8,128)(2,1)S(1)}) custom-call(s32[1,128]{1,0:T(1,128)S(1)} %get-tuple-element.33.slots, s32[1,128]{1,0:T(1,128)S(1)} %get-tuple-element.34.targets, bf16[128,4096]{1,0:T(8,128)(2,1)} %weights.3), custom_call_target="tpu_custom_call" | custom-call | flops 805306368 | bytes 6291456 | tf_op jit(solution)/shard_map/spread/pallas_call | solution.py:151
  11.7 0.8 %chip.1 = (s16[528,256]{1,0:T(8,128)(2,1)S(1)}, s16[528,256]{1,0:T(8,128)(2,1)S(1)}) custom-call(bf16[1024,1024]{1,0:T(8,128)(2,1)S(1)} %get-tuple-element.42.left, bf16[512,256]{1,0:T(8,128)(2,1)S(1)} %get-tuple-element.37.first, bf16[512,256]{1,0:T(8,128)(2,1)S(1)} %get-tuple-element.38.later), custom_call_target="tpu_custom_call" | custom-call | flops 536870912 | bytes 2097152 | tf_op jit(solution)/shard_map/chip/pallas_call | solution.py:258
  12.5 0.6 %collective-permute-start.4 = (s16[528,256]{1,0:T(8,128)(2,1)S(1)}, s16[528,256]{1,0:T(8,128)(2,1)S(1)}, u32[]{:S(2)}, u32[]{:S(2)}) collective-permute-start(s16[528,256]{1,0:T(8,128)(2,1)S(1)} %get-tuple-element.43), channel_id=1, source_target_pairs={{0,1},{1,0},{2,3},{3,2},{4,5},{5,4},{6,7},{7,6},{8,9},{9,8},{10,11... | collective-permute-start | bytes 811016 | tf_op jit(solution)/shard_map/ppermute | solution.py:347
  13.1 0.1 collective-permute-start.5
  13.2 1.3 %middle.1 = (f32[1024,256]{1,0:T(8,128)S(1)}, f32[1024,256]{1,0:T(8,128)S(1)}) custom-call(bf16[1024,1024]{1,0:T(8,128)(2,1)S(1)} %get-tuple-element.35.left_0, bf16[1024,1024]{1,0:T(8,128)(2,1)S(1)} %get-tuple-element.36.left_1, bf16[512,256]{1,0:T(8,128)(2,1)S(1)} %get-tuple-element.37.first, bf16[512,256]{1,0:T(8,128)(2,1)S(1)} %get-tuple-element.38.later), custom_call_target="tpu_custom_call" | custom-call | flops 1073741824 | bytes 4194304 | tf_op jit(solution)/shard_map/middle/pallas_call | solution.py:278
  14.5 0.0 collective-permute-done.4.refs_0_
  14.5 0.2 collective-permute-done.5.refs_1_
  14.7 1.1 %finish.2.refs_1_ = f32[32,64,256]{2,1,0:T(8,128)} custom-call(f32[1024,256]{1,0:T(8,128)S(1)} %get-tuple-element.41.own, s16[528,256]{1,0:T(8,128)(2,1)S(1)} %collective-permute-done.4.refs_0_, s16[528,256]{1,0:T(8,128)(2,1)S(1)} %collective-permute-done.5.refs_1_), custom_call_target="tpu_custom_call" | custom-call | flops 786432 | bytes 2097152 | tf_op jit(solution)/shard_map/finish/pallas_call | solution.py:321
  15.8 6.2 %collective-permute-done.3.refs_0_ = s16[1040,256]{1,0:T(8,128)(2,1)S(1)} collective-permute-done((s16[1040,256]{1,0:T(8,128)(2,1)S(1)}, s16[1040,256]{1,0:T(8,128)(2,1)S(1)}, u32[]{:S(2)}, u32[]{:S(2)}) %collective-permute-start.3) | collective-permute-done | bytes 532512 | tf_op jit(solution)/shard_map/ppermute | solution.py:346
  22.0 1.1 %finish.3 = f32[32,64,256]{2,1,0:T(8,128)} custom-call(f32[1024,256]{1,0:T(8,128)S(1)} %get-tuple-element.39.own, s16[1040,256]{1,0:T(8,128)(2,1)S(1)} %collective-permute-done.3.refs_0_, f32[32,64,256]{2,1,0:T(8,128)} %finish.2.refs_1_), custom_call_target="tpu_custom_call", output_to_operand_aliasing={{}: (2, {})} | custom-call | flops 786432 | bytes 2097152 | tf_op jit(solution)/shard_map/finish/pallas_call | solution.py:321
Async XLA Ops:
  1.1 4.4 %collective-permute-start = (bf16[128,256]{1,0:T(8,128)(2,1)S(1)}, bf16[128,256]{1,0:T(8,128)(2,1)S(1)}, u32[]{:S(2)}, u32[]{:S(2)}) collective-permute-start(bf16[128,256]{1,0:T(8,128)(2,1)S(1)} %get-tuple-element.28), channel_id=1, source_target_pairs={{0,1},{1,2},{2,3},{3,0},{4,5},{5,6},{6,7},{7,4},{8,9},{9,10},{10,1... | collective-permute-start | bytes 196616 | tf_op jit(solution)/shard_map/ppermute | solution.py:339
  3.0 3.4 %collective-permute-start.1 = (bf16[128,256]{1,0:T(8,128)(2,1)S(1)}, bf16[128,256]{1,0:T(8,128)(2,1)S(1)}, u32[]{:S(2)}, u32[]{:S(2)}) collective-permute-start(bf16[128,256]{1,0:T(8,128)(2,1)S(1)} %get-tuple-element.30), channel_id=1, source_target_pairs={{0,2},{1,3},{2,0},{3,1},{4,6},{5,7},{6,4},{7,5},{8,10},{9,11},{10,... | collective-permute-start | bytes 196616 | tf_op jit(solution)/shard_map/ppermute | solution.py:339
  3.2 3.8 %collective-permute-start.2 = (bf16[128,256]{1,0:T(8,128)(2,1)S(1)}, bf16[128,256]{1,0:T(8,128)(2,1)S(1)}, u32[]{:S(2)}, u32[]{:S(2)}) collective-permute-start(bf16[128,256]{1,0:T(8,128)(2,1)S(1)} %get-tuple-element.31), channel_id=1, source_target_pairs={{0,3},{1,0},{2,1},{3,2},{4,7},{5,4},{6,5},{7,6},{8,11},{9,8},{10,9... | collective-permute-start | bytes 196616 | tf_op jit(solution)/shard_map/ppermute | solution.py:339
  7.5 14.5 %collective-permute-start.3 = (s16[1040,256]{1,0:T(8,128)(2,1)S(1)}, s16[1040,256]{1,0:T(8,128)(2,1)S(1)}, u32[]{:S(2)}, u32[]{:S(2)}) collective-permute-start(s16[1040,256]{1,0:T(8,128)(2,1)S(1)} %get-tuple-element.40), channel_id=1, source_target_pairs={{0,31},{1,2},{2,1},{3,4},{4,3},{5,6},{6,5},{7,8},{8,7},{9,10},{10,... | collective-permute-start | bytes 1597448 | tf_op jit(solution)/shard_map/ppermute | solution.py:346
  12.5 2.0 %collective-permute-start.4 = (s16[528,256]{1,0:T(8,128)(2,1)S(1)}, s16[528,256]{1,0:T(8,128)(2,1)S(1)}, u32[]{:S(2)}, u32[]{:S(2)}) collective-permute-start(s16[528,256]{1,0:T(8,128)(2,1)S(1)} %get-tuple-element.43), channel_id=1, source_target_pairs={{0,1},{1,0},{2,3},{3,2},{4,5},{5,4},{6,7},{7,6},{8,9},{9,8},{10,11... | collective-permute-start | bytes 811016 | tf_op jit(solution)/shard_map/ppermute | solution.py:347
  13.1 1.6 %collective-permute-start.5 = (s16[528,256]{1,0:T(8,128)(2,1)S(1)}, s16[528,256]{1,0:T(8,128)(2,1)S(1)}, u32[]{:S(2)}, u32[]{:S(2)}) collective-permute-start(s16[528,256]{1,0:T(8,128)(2,1)S(1)} %get-tuple-element.44), channel_id=1, source_target_pairs={{0,1},{1,0},{2,3},{3,2},{4,5},{5,4},{6,7},{7,6},{8,9},{9,8},{10,11... | collective-permute-start | bytes 811016 | tf_op jit(solution)/shard_map/ppermute | solution.py:347
